TPU v7x, 32 devices: a whole 2x2x4 slice. The times are simulated.
32 devices in a mesh: energy: 8 (over z, x), momentum: 4 (over y, core).
Axes of the slice: x: 2, y: 2, z: 4, core: 2. Of those that a mesh axis runs over, the one named last changes fastest.
Arguments:
- green_tiles: bfloat16 [4, 16, 4, 2, 128, 128], P('momentum', 'energy'), may hold values from -6 to 6
- dham_blocks: bfloat16 [3, 4, 2, 128, 128], replicated, may hold values from -0.375 to 0.375
- phonon_weight: float32 [6, 3, 2], replicated, may hold values from 0.1 to 0.5
- phonon_modes: int32 [6, 2], replicated, may hold values from -1 to 2, as said below
- tile_pattern: int32 [4, 2], replicated, may hold values from 0 to 3, as said below
Outputs:
- self_energy: bfloat16 [4, 16, 4, 2, 128, 128], P('momentum', 'energy')
Inputs may be any that keep to these rules, and one draw needn't show every extreme that they name: `phonon_modes`: column 0 is a momentum offset and each of -1, 0, 1 is used by some mode; column 1 is an energy offset and each of 1 to 2 is used by some mode. `tile_pattern`: every block number appears in each column.
All inputs are finite; a program needn't handle non-finite values.
Results may differ from a plain program's by a relative error of at most 0.0062.
Values may be sent and summed in bfloat16 or wider, within the bound.
No kernel may reach another device: no remote copies, remote signals or barrier semaphores. Data moves between devices by JAX's collectives and lax.ppermute only.
A program may use at most 64 MiB of HBM per device.

v0:
```python
import jax
import jax.numpy as jnp
from jax import lax
from jax.sharding import PartitionSpec as P

OFFSETS = (-1, 0, 1)


def with_halo(block, sides, width):
    for axis, dim in sides:
        count = lax.axis_size(axis)
        forward = [(i, i + 1) for i in range(count - 1)]
        backward = [(target, source) for source, target in forward]
        low = lax.ppermute(
            lax.slice_in_dim(block, block.shape[dim] - width, None, axis=dim), axis, forward
        )
        high = lax.ppermute(lax.slice_in_dim(block, 0, width, axis=dim), axis, backward)
        block = jnp.concatenate([low, block, high], axis=dim)
    return block


def from_behind(block, axis, distance):
    devices = range(lax.axis_size(axis))
    route = [((i - distance) % len(devices), i) for i in devices]
    return lax.ppermute(block, axis, route)


def stack_blocks(left_sel, right_sel):
    left_real = left_sel[:, :, 0]
    left_imag = left_sel[:, :, 1]
    upper_row = jnp.stack([left_real, -left_imag], axis=3)
    lower_row = jnp.stack([left_imag, left_real], axis=3)
    left_big = jnp.stack([upper_row, lower_row], axis=2)
    right_real = jnp.swapaxes(right_sel[:, :, 0], -1, -2)
    right_imag = jnp.swapaxes(right_sel[:, :, 1], -1, -2)
    first_col = jnp.stack([right_real, -right_imag], axis=3)
    second_col = jnp.stack([right_imag, right_real], axis=3)
    right_big = jnp.stack([first_col, second_col], axis=2)
    return (left_big, right_big)


def coupling(phonon_modes, phonon_weight, offset, energy_count):
    span = jnp.arange(-energy_count, energy_count + 1, dtype=jnp.int32)
    chosen = (phonon_modes[:, 0] == offset).astype(jnp.float32)
    below = (span[None, :] == -phonon_modes[:, 1:2]).astype(jnp.float32)
    above = (span[None, :] == phonon_modes[:, 1:2]).astype(jnp.float32)
    terms = chosen[:, None, None] * (
        phonon_weight[:, :, 0:1] * below[:, None, :] + phonon_weight[:, :, 1:2] * above[:, None, :]
    )
    return jnp.sum(terms, axis=0).astype(jnp.bfloat16)


def band_matrix(kern, energy_count):
    relative = (
        jnp.arange(3 * energy_count, dtype=jnp.int32)[None, :]
        - energy_count
        - jnp.arange(energy_count, dtype=jnp.int32)[:, None]
    )
    span = jnp.arange(-energy_count, energy_count + 1, dtype=jnp.int32)
    onehot = (relative[:, :, None] == span[None, None, :]).astype(jnp.float32)
    table = jnp.einsum(
        "dx,ejx->dej", kern.astype(jnp.float32), onehot, precision=lax.Precision.HIGHEST
    )
    return table.astype(jnp.bfloat16).reshape(3 * energy_count, 3 * energy_count)


def contribution(window, table, left_big, right_big):
    energy_count = window.shape[0] // 3
    flat = window.reshape(window.shape[0], -1)
    mixed = jnp.dot(table, flat, preferred_element_type=jnp.float32).astype(jnp.bfloat16)
    mixed = mixed.reshape((3, energy_count) + window.shape[1:])
    product = jnp.einsum(
        "dtbicj,detcjk->detbik", left_big, mixed, preferred_element_type=jnp.float32
    ).astype(jnp.bfloat16)
    return jnp.einsum(
        "detcij,dtcjbk->etbik", product, right_big, preferred_element_type=jnp.float32
    )


def local(green_tiles, dham_blocks, phonon_weight, phonon_modes, tile_pattern):
    energy_count = green_tiles.shape[1]
    tile_count = green_tiles.shape[2]
    tile_size = green_tiles.shape[4]
    block_count = dham_blocks.shape[1]
    block_ids = jnp.arange(block_count, dtype=jnp.int32)[None, :]
    choose_left = (tile_pattern[:, 0:1] == block_ids).astype(jnp.bfloat16)
    choose_right = (tile_pattern[:, 1:2] == block_ids).astype(jnp.bfloat16)
    left_sel = jnp.einsum(
        "tb,dbcij->dtcij", choose_left, dham_blocks, preferred_element_type=jnp.float32
    ).astype(jnp.bfloat16)
    right_sel = jnp.einsum(
        "tb,dbcij->dtcij", choose_right, dham_blocks, preferred_element_type=jnp.float32
    ).astype(jnp.bfloat16)
    left_big, right_big = stack_blocks(left_sel, right_sel)
    tables = [
        band_matrix(coupling(phonon_modes, phonon_weight, offset, energy_count), energy_count)
        for offset in OFFSETS
    ]
    packed = green_tiles.reshape(1, energy_count * tile_count, 2, tile_size, tile_size)
    window_shape = (3 * energy_count, tile_count, 2, tile_size, tile_size)
    summed = jnp.zeros((energy_count, tile_count, 2, tile_size, tile_size), jnp.float32)
    window = with_halo(packed, (("energy", 0),), 1).reshape(window_shape)
    for position, offset in enumerate(OFFSETS):
        finished = contribution(window, tables[position], left_big, right_big)
        if offset != 0:
            finished = from_behind(finished, "momentum", offset)
        summed = summed + finished
    return summed.astype(jnp.bfloat16)[None]


def solution(mesh):
    placed = (P("momentum", "energy", None, None, None, None), P(), P(), P(), P())
    return jax.shard_map(
        local,
        mesh=mesh,
        in_specs=placed,
        out_specs=P("momentum", "energy", None, None, None, None),
        check_vma=False,
    )
```

profile of v0, /device:TPU:0, one launch (start us, length us, event | category | flops | bytes accessed | tf_op | source)
XLA Modules:
  0.0 69.0 jit_solution(13642242182011445817)
XLA Ops:
  0.0 1.4 %collective-permute-start.1 = (bf16[1,8,2,128,128]{4,3,2,1,0:T(8,128)(2,1)}, bf16[1,8,2,128,128]{4,3,2,1,0:T(8,128)(2,1)S(1)}, u32[]{:S(2)}, u32[]{:S(2)}) collective-permute-start(bf16[1,8,2,128,128]{4,3,2,1,0:T(8,128)(2,1)} %bitcast.212), channel_id=1, source_target_pairs={{4,0},{8,4},{12,8},{16,12},{20,16},{24,20},{28,24},{5,1},{9,5},{13... | collective-permute-start | bytes 1572872 | tf_op jit(solution)/shard_map/ppermute | solution.py:17
  1.4 5.5 %collective-permute-start = (bf16[1,8,2,128,128]{4,3,2,1,0:T(8,128)(2,1)}, bf16[1,8,2,128,128]{4,3,2,1,0:T(8,128)(2,1)S(1)}, u32[]{:S(2)}, u32[]{:S(2)}) collective-permute-start(bf16[1,8,2,128,128]{4,3,2,1,0:T(8,128)(2,1)} %bitcast.213), channel_id=1, source_target_pairs={{0,4},{4,8},{8,12},{12,16},{16,20},{20,24},{24,28},{1,5},{5,9},{9,... | collective-permute-start | bytes 1572872 | tf_op jit(solution)/shard_map/ppermute | solution.py:14
  7.0 0.7 negate_bitcast_fusion
  7.6 0.7 fusion.91
  8.3 0.8 %slice_bitcast_fusion.5 = (s32[4]{0:T(128)S(1)}, s32[4]{0:T(128)S(1)}) fusion(s32[4,2]{0,1:T(2,128)} %param.9), kind=kLoop, calls=%fused_computation.90 | loop fusion | bytes 64 | tf_op jit(solution)/shard_map/eq | solution.py:87
  9.1 0.8 %fusion.54 = bf16[3,4,2,128,128]{4,1,3,2,0:T(4,128)(2,1)S(1)} fusion(bf16[3,4,2,128,128]{4,3,2,1,0:T(8,128)(2,1)S(1)} %copy-done, s32[4]{0:T(128)S(1)} %get-tuple-element.18), kind=kOutput, calls=%fused_computation.29 | convolution fusion | flops 3538960 | bytes 1572880 | tf_op jit(solution)/shard_map/tb,dbcij->dtcij/dot_general | solution.py:91
  10.0 0.3 slice_bitcast_fusion.3
  10.3 0.2 copy-done.2
  10.8 0.2 convolution_convert_fusion.5
  11.2 0.2 convolution_convert_fusion.7
  11.4 0.8 %fusion.55 = bf16[3,4,2,128,128]{4,1,3,2,0:T(4,128)(2,1)S(1)} fusion(bf16[3,4,2,128,128]{4,3,2,1,0:T(8,128)(2,1)S(1)} %copy-done, s32[4]{0:T(128)S(1)} %get-tuple-element.19), kind=kOutput, calls=%fused_computation.30 | convolution fusion | flops 3538960 | bytes 1572880 | tf_op jit(solution)/shard_map/tb,dbcij->dtcij/dot_general | solution.py:88
  12.2 0.3 slice_bitcast_fusion
  12.5 0.8 %maximum_bitcast_fusion.2 = (bf16[3,4,1,128,2,128]{3,1,5,0,4,2:T(4,128)(2,1)S(1)}, bf16[3,4,1,128,2,128]{3,1,5,0,4,2:T(4,128)(2,1)S(1)}) fusion(bf16[3,4,128,1,128]{2,1,4,0,3:T(4,128)(2,1)S(1)} %fusion.72, bf16[3,4,128,1,128]{2,1,4,0,3:T(4,128)(2,1)S(1)} %get-tuple-element.9, bf16[3,4,128,1,128]{2,1,4,0,3:T(4,128)(2,1)S(1)} %get-tuple-element.8), kind=kLoop, calls=%fused_computation.41 | loop fusion | flops 786432 | bytes 2752512 | tf_op jit(solution)/shard_map/stack | solution.py:38
  13.3 2.3 %maximum_bitcast_fusion = bf16[3,4,2,128,2,128,1]{3,1,5,0,4,2,6:T(4,128)(2,1)} fusion(bf16[3,4,1,128,2,128]{3,1,5,0,4,2:T(4,128)(2,1)S(1)} %get-tuple-element.13, bf16[3,4,1,128,2,128]{3,1,5,0,4,2:T(4,128)(2,1)S(1)} %get-tuple-element.12), kind=kLoop, calls=%fused_computation.9 | loop fusion | flops 786432 | bytes 3145728 | tf_op jit(solution)/shard_map/stack | solution.py:38
  15.8 0.8 %maximum_bitcast_fusion.4 = (bf16[3,4,1,128,2,128]{5,1,3,0,4,2:T(4,128)(2,1)S(1)}, bf16[3,4,1,128,2,128]{5,1,3,0,4,2:T(4,128)(2,1)S(1)}) fusion(bf16[3,4,128,1,128]{4,1,2,0,3:T(4,128)(2,1)S(1)} %fusion.94, bf16[3,4,128,1,128]{4,1,2,0,3:T(4,128)(2,1)S(1)} %get-tuple-element.11, bf16[3,4,128,1,128]{4,1,2,0,3:T(4,128)(2,1)S(1)} %get-tuple-element.10), kind=kLoop, calls=%fused_computation.43 | loop fusion | flops 786432 | bytes 2752512 | tf_op jit(solution)/shard_map/stack | solution.py:33
  16.6 2.3 %maximum_bitcast_fusion.1 = bf16[3,4,2,128,2,128,1]{5,1,3,0,4,2,6:T(4,128)(2,1)} fusion(bf16[3,4,1,128,2,128]{5,1,3,0,4,2:T(4,128)(2,1)S(1)} %get-tuple-element.15, bf16[3,4,1,128,2,128]{5,1,3,0,4,2:T(4,128)(2,1)S(1)} %get-tuple-element.14), kind=kLoop, calls=%fused_computation.11 | loop fusion | flops 786432 | bytes 3145728 | tf_op jit(solution)/shard_map/stack | solution.py:33
  18.9 9.7 %collective-permute-done = bf16[1,8,2,128,128]{4,3,2,1,0:T(8,128)(2,1)S(1)} collective-permute-done((bf16[1,8,2,128,128]{4,3,2,1,0:T(8,128)(2,1)}, bf16[1,8,2,128,128]{4,3,2,1,0:T(8,128)(2,1)S(1)}, u32[]{:S(2)}, u32[]{:S(2)}) %collective-permute-start) | collective-permute-done | bytes 524320 | tf_op jit(solution)/shard_map/ppermute | solution.py:14
  28.6 1.3 %pad_maximum_fusion = bf16[3,8,2,128,128]{4,3,2,1,0:T(8,128)(2,1)} fusion(bf16[1,8,2,128,128]{4,3,2,1,0:T(8,128)(2,1)S(1)} %collective-permute-done.1, bf16[1,8,2,128,128]{4,3,2,1,0:T(8,128)(2,1)S(1)} %bitcast.214, bf16[1,8,2,128,128]{4,3,2,1,0:T(8,128)(2,1)S(1)} %collective-permute-done), kind=kLoop, calls=%fused_computation.10 | loop fusion | flops 1572864 | bytes 3145728 | tf_op jit(solution)/shard_map/concatenate | solution.py:18
  29.9 3.0 %reshape_reshape.2 = bf16[6,131072]{1,0:T(8,128)(2,1)S(1)} reshape(bf16[3,8,2,128,128]{4,3,2,1,0:T(8,128)(2,1)} %pad_maximum_fusion) | data formatting | bytes 3145728 | tf_op jit(solution)/shard_map/reshape;reshape | solution.py:69
  33.0 0.7 fusion.2
  33.7 1.4 %copy.128 = bf16[1,6,1024,128]{3,2,1,0:T(8,128)(2,1)} copy(bf16[1,6,1024,128]{3,1,2,0:T(8,128)(2,1)S(1)} %fusion.2) | data formatting | bytes 3145728
  35.0 4.5 %fusion.34 = f32[2,4,2,128,128]{3,4,0,2,1:T(8,128)} fusion(bf16[3,2,4,2,128,128,1]{5,4,3,2,1,0,6:T(8,128)(2,1)} %bitcast.210, bf16[3,4,2,128,2,128,1]{5,1,3,0,4,2,6:T(4,128)(2,1)} %maximum_bitcast_fusion.1, bf16[3,4,2,128,2,128,1]{3,1,5,0,4,2,6:T(4,128)(2,1)} %maximum_bitcast_fusion), kind=kOutput, calls=%fused_computation.25 | convolution fusion | flops 806092800 | bytes 5767168 | tf_op jit(solution)/shard_map/detcij,dtcjbk->etbik/dot_general | solution.py:75
  39.5 0.7 fusion
  40.2 1.4 %copy.126 = bf16[1,6,1024,128]{3,2,1,0:T(8,128)(2,1)} copy(bf16[1,6,1024,128]{3,1,2,0:T(8,128)(2,1)S(1)} %fusion) | data formatting | bytes 3145728
  41.6 4.5 %fusion.24 = f32[2,4,2,128,128]{3,4,0,2,1:T(8,128)} fusion(bf16[3,2,4,2,128,128,1]{5,4,3,2,1,0,6:T(8,128)(2,1)} %bitcast.211, bf16[3,4,2,128,2,128,1]{5,1,3,0,4,2,6:T(4,128)(2,1)} %maximum_bitcast_fusion.1, bf16[3,4,2,128,2,128,1]{3,1,5,0,4,2,6:T(4,128)(2,1)} %maximum_bitcast_fusion), kind=kOutput, calls=%fused_computation.23 | convolution fusion | flops 806092800 | bytes 5767168 | tf_op jit(solution)/shard_map/detcij,dtcjbk->etbik/dot_general | solution.py:75
  46.0 1.7 %collective-permute-start.2 = (f32[2,4,2,128,128]{3,4,0,2,1:T(8,128)}, f32[2,4,2,128,128]{3,4,0,2,1:T(8,128)}, u32[]{:S(2)}, u32[]{:S(2)}) collective-permute-start(f32[2,4,2,128,128]{3,4,0,2,1:T(8,128)} %fusion.24), channel_id=1, source_target_pairs={{1,0},{2,1},{3,2},{0,3},{5,4},{6,5},{7,6},{4,7},{9,8},{10,9},{11,1... | collective-permute-start | bytes 3145736 | tf_op jit(solution)/shard_map/ppermute | solution.py:25
  48.1 0.7 %fusion.1 = bf16[1,6,1024,128]{3,1,2,0:T(8,128)(2,1)S(1)} fusion(bf16[6,6]{1,0:T(8,128)(2,1)S(1)} %reshape.146, bf16[6,131072]{1,0:T(8,128)(2,1)S(1)} %reshape_reshape.2), kind=kOutput, calls=%fused_computation.7 | convolution fusion | flops 10223616 | bytes 3145800 | tf_op jit(solution)/shard_map/dot_general | solution.py:70
  48.8 0.2 copy.127
  49.0 7.9 %collective-permute-done.3 = f32[2,4,2,128,128]{3,4,0,2,1:T(8,128)} collective-permute-done((f32[2,4,2,128,128]{3,4,0,2,1:T(8,128)}, f32[2,4,2,128,128]{3,4,0,2,1:T(8,128)}, u32[]{:S(2)}, u32[]{:S(2)}) %collective-permute-start.3) | collective-permute-done | bytes 1048608 | tf_op jit(solution)/shard_map/ppermute | solution.py:25
  56.9 7.4 %collective-permute-done.2 = f32[2,4,2,128,128]{3,4,0,2,1:T(8,128)} collective-permute-done((f32[2,4,2,128,128]{3,4,0,2,1:T(8,128)}, f32[2,4,2,128,128]{3,4,0,2,1:T(8,128)}, u32[]{:S(2)}, u32[]{:S(2)}) %collective-permute-start.2) | collective-permute-done | bytes 1048608 | tf_op jit(solution)/shard_map/ppermute | solution.py:25
  64.3 3.6 %fusion.56 = bf16[1,2,4,2,128,128]{4,5,1,3,2,0:T(8,128)(2,1)S(1)} fusion(f32[2,4,2,128,128]{3,4,0,2,1:T(8,128)} %collective-permute-done.3, f32[2,4,2,128,128]{3,4,0,2,1:T(8,128)} %collective-permute-done.2, bf16[3,2,4,2,128,128,1]{5,4,3,2,1,0,6:T(8,128)(2,1)S(1)} %bitcast.209, bf16[3,4,2,128,2,128,1]{5,1,3,0,4,2,6:T(4,128)(2,1)} %maximum_bitcast_fusion.1, ...), kind=kOutput, calls=%fused_computation.31 | convolution fusion | flops 806879232 | bytes 7340032 | tf_op jit(solution)/shard_map/detcij,dtcjbk->etbik/dot_general | solution.py:75
  68.0 1.0 %copy.77 = bf16[1,2,4,2,128,128]{5,4,3,2,1,0:T(8,128)(2,1)} copy(bf16[1,2,4,2,128,128]{4,5,1,3,2,0:T(8,128)(2,1)S(1)} %fusion.56) | data formatting | bytes 1048576 | tf_op jit(solution)/shard_map/broadcast_in_dim | solution.py:108
  (26 shorter events, 1.2 us)
Async XLA Ops:
  0.0 9.1 %copy-start = (bf16[3,4,2,128,128]{4,3,2,1,0:T(8,128)(2,1)S(1)}, bf16[3,4,2,128,128]{4,3,2,1,0:T(8,128)(2,1)}, u32[]{:S(2)}) copy-start(bf16[3,4,2,128,128]{4,3,2,1,0:T(8,128)(2,1)} %param.6) | copy-start | bytes 2359300
  0.0 18.9 %collective-permute-start.1 = (bf16[1,8,2,128,128]{4,3,2,1,0:T(8,128)(2,1)}, bf16[1,8,2,128,128]{4,3,2,1,0:T(8,128)(2,1)S(1)}, u32[]{:S(2)}, u32[]{:S(2)}) collective-permute-start(bf16[1,8,2,128,128]{4,3,2,1,0:T(8,128)(2,1)} %bitcast.212), channel_id=1, source_target_pairs={{4,0},{8,4},{12,8},{16,12},{20,16},{24,20},{28,24},{5,1},{9,5},{13... | collective-permute-start | bytes 1572872 | tf_op jit(solution)/shard_map/ppermute | solution.py:17
  1.4 27.2 %collective-permute-start = (bf16[1,8,2,128,128]{4,3,2,1,0:T(8,128)(2,1)}, bf16[1,8,2,128,128]{4,3,2,1,0:T(8,128)(2,1)S(1)}, u32[]{:S(2)}, u32[]{:S(2)}) collective-permute-start(bf16[1,8,2,128,128]{4,3,2,1,0:T(8,128)(2,1)} %bitcast.213), channel_id=1, source_target_pairs={{0,4},{4,8},{8,12},{12,16},{16,20},{20,24},{24,28},{1,5},{5,9},{9,... | collective-permute-start | bytes 1572872 | tf_op jit(solution)/shard_map/ppermute | solution.py:14
  9.9 0.7 copy-start.2
  16.6 12.0 %copy-start.1 = (bf16[1,2,4,2,128,128]{5,4,3,2,1,0:T(8,128)(2,1)S(1)}, bf16[1,2,4,2,128,128]{5,4,3,2,1,0:T(8,128)(2,1)}, u32[]{:S(2)}) copy-start(bf16[1,2,4,2,128,128]{5,4,3,2,1,0:T(8,128)(2,1)} %param.5) | copy-start | bytes 1572868
  39.5 17.4 %collective-permute-start.3 = (f32[2,4,2,128,128]{3,4,0,2,1:T(8,128)}, f32[2,4,2,128,128]{3,4,0,2,1:T(8,128)}, u32[]{:S(2)}, u32[]{:S(2)}) collective-permute-start(f32[2,4,2,128,128]{3,4,0,2,1:T(8,128)} %fusion.34), channel_id=1, source_target_pairs={{3,0},{0,1},{1,2},{2,3},{7,4},{4,5},{5,6},{6,7},{11,8},{8,9},{9,10... | collective-permute-start | bytes 3145736 | tf_op jit(solution)/shard_map/ppermute | solution.py:25
  46.0 18.3 %collective-permute-start.2 = (f32[2,4,2,128,128]{3,4,0,2,1:T(8,128)}, f32[2,4,2,128,128]{3,4,0,2,1:T(8,128)}, u32[]{:S(2)}, u32[]{:S(2)}) collective-permute-start(f32[2,4,2,128,128]{3,4,0,2,1:T(8,128)} %fusion.24), channel_id=1, source_target_pairs={{1,0},{2,1},{3,2},{0,3},{5,4},{6,5},{7,6},{4,7},{9,8},{10,9},{11,1... | collective-permute-start | bytes 3145736 | tf_op jit(solution)/shard_map/ppermute | solution.py:25
where the time goes:
time: 69.6 us; the launch traced here: 69 us
  waiting for transfers between devices  25 us (36%)
  matrix products  16.8 us (24%)
  other arithmetic  9.45 us (14%)
  local copies, waits for them, and re-layouts  8.96 us (13%)
  starting transfers between devices  8.66 us (12%)
    ppermute x2, waiting for transfers between devices, from_behind(): return lax.ppermute(block, axis, route)  15.3 us
    dot_general x3, matrix products, contribution(): jnp.einsum('detcij,dtcjbk->etbik', product, right_big, preferred_element_...  12.6 us
    ppermute x1, waiting for transfers between devices, with_halo(): lax.ppermute(lax.slice_in_dim(block, block.shape[dim] - width, None, axis...  9.66 us
    ppermute x1, starting transfers between devices, with_halo(): lax.ppermute(lax.slice_in_dim(block, block.shape[dim] - width, None, axis...  5.51 us
    unnamed x13, local copies, waits for them, and re-layouts  3.48 us
    another operation x2, other arithmetic, stack_blocks(): left_big = jnp.stack([upper_row, lower_row], axis=2)  3.11 us
    another operation x2, other arithmetic, stack_blocks(): right_big = jnp.stack([first_col, second_col], axis=2)  3.11 us
    another operation x1, local copies, waits for them, and re-layouts, contribution(): flat = window.reshape(window.shape[0], -1)  3.05 us
  transfers between devices with their start and end apart: 4, of which 3 were waited for; matrix products, arithmetic and copies ran while one was open for 28% of the time, Pallas kernels for 0%

commit v1 on v0

v1 whole, which is shorter than its diff:
```python
import functools
import jax
import jax.numpy as jnp
from jax import lax
from jax.experimental import pallas as pl
from jax.experimental.pallas import tpu as pltpu
from jax.sharding import PartitionSpec as P

AXES = ("energy", "momentum")
SLOTS = 3
DIRS = 3
ROWS = 32
GRANT = 16 * 2**20


def in_vmem(array):
    return pltpu.with_memory_space_constraint(array, pltpu.VMEM)


def vmem_specs(count):
    return [pl.BlockSpec(memory_space=pltpu.VMEM)] * count


def routes(n_e, n_k):
    def pairs(step):
        out = []
        for e in range(n_e):
            for k in range(n_k):
                to_e, to_k = step(e, k)
                if 0 <= to_e < n_e:
                    out.append((e * n_k + k, to_e * n_k + to_k % n_k))
        return out

    return {
        "pair": pairs(lambda e, k: (e ^ 1, k)),
        "relay": pairs(lambda e, k: (e + 2 - 4 * (e % 2), k)),
        "back": pairs(lambda e, k: (e - 2 + 4 * (e % 2), k)),
        "core": pairs(lambda e, k: (e, k ^ 1)),
        "far": pairs(lambda e, k: (e, k - 1 + 2 * (k % 2))),
    }


def prepare_kernel(parity, modes, weight, pattern, dham, left, right, coef_in, coef_out, table):
    mode_count = modes.shape[0]
    tile_count = pattern.shape[0]
    for q in range(4):
        for d in range(DIRS):
            for s in range(9):
                table[q, d, s] = 0.0
    for m in range(mode_count):
        q = modes[m, 0] + 1
        step = modes[m, 1]
        for d in range(DIRS):
            table[q, d, 4 - step] = table[q, d, 4 - step] + weight[m, d, 0]
            table[q, d, 4 + step] = table[q, d, 4 + step] + weight[m, d, 1]
    e_dir = 1 - 2 * parity[0]
    k_dir = 1 - 2 * parity[1]
    e_dirs = (0, e_dir, -e_dir)
    k_dirs = (0, k_dir, -k_dir)

    def spread(value):
        return jnp.full((8, 128), value, jnp.float32).astype(jnp.bfloat16).astype(jnp.float32)

    for d in range(DIRS):
        for slot in range(SLOTS):
            for i in range(2):
                for block in range(SLOTS):
                    for j in range(2):
                        entry = ((d * SLOTS + slot) * 2 + i) * 6 + block * 2 + j
                        shift = j - i + 2 * e_dirs[block]
                        coef_in[entry] = spread(table[k_dirs[slot] + 1, d, shift + 4])
                        shift = j - i - 2 * e_dirs[slot]
                        coef_out[entry] = spread(table[1 - k_dirs[block], d, shift + 4])
    for t in range(tile_count):
        lo, hi = pattern[t, 0], pattern[t, 1]
        for d in range(DIRS):
            real, imag = dham[d, lo, 0], dham[d, lo, 1]
            left[t, d, :128, :128] = real
            left[t, d, :128, 128:] = -imag
            left[t, d, 128:, :128] = imag
            left[t, d, 128:, 128:] = real
            real, imag = dham[d, hi, 0].T, dham[d, hi, 1].T
            right[t, d, :128, :128] = real
            right[t, d, :128, 128:] = -imag
            right[t, d, 128:, :128] = imag
            right[t, d, 128:, 128:] = real


def prepare(parity, modes, weight, pattern, dham):
    tile_count = pattern.shape[0]
    entries = DIRS * SLOTS * 2 * 6
    big = pltpu.VMEM((tile_count, DIRS, 256, 256), jnp.bfloat16)
    coef = pltpu.VMEM((entries, 8, 128), jnp.float32)
    return pl.pallas_call(
        prepare_kernel,
        out_shape=(big, big, coef, coef),
        in_specs=[pl.BlockSpec(memory_space=pltpu.SMEM)] * 4 + vmem_specs(1),
        out_specs=tuple(vmem_specs(4)),
        scratch_shapes=[pltpu.SMEM((4, DIRS, 9), jnp.float32)],
        compiler_params=pltpu.CompilerParams(vmem_limit_bytes=GRANT),
        name="prepare",
    )(parity, modes, weight, pattern, dham)


def sandwich_kernel(first, own, near, far, left, right, coef, to_own, to_near, to_far, mixed, product):
    tiles = own.shape[1]
    outs = (to_own, to_near, to_far)
    sources = (own, near, far)
    for t in range(tiles):
        for part in range(2):
            for row in range(0, 128, ROWS):
                taken = [
                    sources[block][j, t, part, pl.ds(row, ROWS), :].astype(jnp.float32).reshape(ROWS // 8, 8, 128)
                    for block in range(SLOTS)
                    for j in range(2)
                ]
                for d in range(DIRS):
                    for item in range(2 * SLOTS):
                        base = (d * 2 * SLOTS + item) * 6
                        acc = taken[0] * coef[base]
                        for tap in range(1, 6):
                            acc = acc + taken[tap] * coef[base + tap]
                        mixed[t, d, pl.ds(part * 128 + row, ROWS), pl.ds(item * 128, 128)] = acc.reshape(ROWS, 128).astype(jnp.bfloat16)
        for d in range(DIRS):
            got = jnp.dot(left[first + t, d], mixed[t, d], preferred_element_type=jnp.float32).astype(jnp.bfloat16)
            for item in range(2 * SLOTS):
                for part in range(2):
                    product[t, pl.ds(item * 128, 128), pl.ds(d * 256 + part * 128, 128)] = got[
                        part * 128 : part * 128 + 128, item * 128 : item * 128 + 128
                    ]
        weights = right[first + t].reshape(DIRS * 256, 256)
        term = jnp.dot(product[t], weights, preferred_element_type=jnp.float32)
        for slot in range(SLOTS):
            for i in range(2):
                item = slot * 2 + i
                for part in range(2):
                    outs[slot][i, t, part] = term[item * 128 : item * 128 + 128, part * 128 : part * 128 + 128].astype(outs[slot].dtype)


def sandwich(first, own, near, far, left, right, coef, near_type):
    shape = own.shape
    tiles = shape[1]
    return pl.pallas_call(
        functools.partial(sandwich_kernel, first),
        out_shape=(
            pltpu.VMEM(shape, jnp.float32),
            pltpu.VMEM(shape, near_type),
            pltpu.VMEM(shape, jnp.bfloat16),
        ),
        in_specs=vmem_specs(6),
        out_specs=tuple(vmem_specs(3)),
        scratch_shapes=[
            pltpu.VMEM((tiles, DIRS, 256, 2 * SLOTS * 128), jnp.bfloat16),
            pltpu.VMEM((tiles, 2 * SLOTS * 128, DIRS * 256), jnp.bfloat16),
        ],
        compiler_params=pltpu.CompilerParams(vmem_limit_bytes=GRANT),
        name="sandwich",
    )(in_vmem(own), in_vmem(near), in_vmem(far), in_vmem(left), in_vmem(right), in_vmem(coef))


def add_kernel(a, b, out):
    out[...] = (a[...] + b[...].astype(jnp.float32)).astype(out.dtype)


def add(a, b):
    return pl.pallas_call(
        add_kernel,
        out_shape=pltpu.VMEM(a.shape, jnp.bfloat16),
        in_specs=vmem_specs(2),
        out_specs=vmem_specs(1)[0],
        compiler_params=pltpu.CompilerParams(vmem_limit_bytes=GRANT),
        name="add",
    )(in_vmem(a), in_vmem(b))


def finish_kernel(own_a, near_a, far_a, own_b, near_b, out):
    tiles = own_a.shape[1]
    f32 = jnp.float32
    out[0, :, :tiles] = (own_a[...] + near_a[...].astype(f32) + far_a[...].astype(f32)).astype(out.dtype)
    out[0, :, tiles:] = (own_b[...] + near_b[...].astype(f32)).astype(out.dtype)


def finish(own_a, near_a, far_a, own_b, near_b):
    e, ta = own_a.shape[:2]
    shape = (1, e, ta + own_b.shape[1]) + own_a.shape[2:]
    return pl.pallas_call(
        finish_kernel,
        out_shape=jax.ShapeDtypeStruct(shape, jnp.bfloat16),
        in_specs=vmem_specs(5),
        out_specs=vmem_specs(1)[0],
        compiler_params=pltpu.CompilerParams(vmem_limit_bytes=GRANT),
        name="finish",
    )(*map(in_vmem, (own_a, near_a, far_a, own_b, near_b)))


def local(green_tiles, dham_blocks, phonon_weight, phonon_modes, tile_pattern):
    n_e, n_k = (lax.axis_size(axis) for axis in AXES)
    route = routes(n_e, n_k)

    def send(block, name):
        return lax.ppermute(block, AXES, route[name])

    tiles = green_tiles[0]
    half = tiles.shape[1] // 2
    in_a, in_b = tiles[:, :half], tiles[:, half:]
    parity = jnp.stack([lax.axis_index(axis) % 2 for axis in AXES]).astype(jnp.int32)
    near_a = send(in_a, "pair")
    far_b = send(in_b, "far")
    near_b = send(in_b, "core")
    left, right, coef_in, coef_out = prepare(parity, phonon_modes, phonon_weight, tile_pattern, dham_blocks)
    far_a = send(near_a, "relay")
    own_b, pair_b, cross_b = sandwich(half, in_b, near_b, far_b, left, right, coef_out, jnp.float32)
    cross_b = send(cross_b, "back")
    own_a, core_a, next_a = sandwich(0, in_a, near_a, far_a, left, right, coef_in, jnp.bfloat16)
    next_a = send(next_a, "far")
    core_a = send(core_a, "core")
    pair_b = send(add(pair_b, cross_b), "pair")
    return finish(own_a, core_a, next_a, own_b, pair_b)


def solution(mesh):
    placed = (P("momentum", "energy", None, None, None, None), P(), P(), P(), P())
    return jax.shard_map(
        local,
        mesh=mesh,
        in_specs=placed,
        out_specs=P("momentum", "energy", None, None, None, None),
        check_vma=False,
    )
```

time: 69.6 us -> 39.5 us (0.57)
  the two profiles are of different devices: /device:TPU:0 before, /device:TPU:7 now
where the time goes in v1:
time: 39.5 us; the launch traced here: 39.2 us
  waiting for transfers between devices  19 us (48%)
  Pallas kernels  8.76 us (22%)
  starting transfers between devices  7.85 us (20%)
  local copies, waits for them, and re-layouts  3.46 us (9%)
    ppermute x8, waiting for transfers between devices, send(): return lax.ppermute(block, AXES, route[name])  19 us
    ppermute x8, starting transfers between devices, send(): return lax.ppermute(block, AXES, route[name])  7.85 us
    pallas_call x2, Pallas kernels, sandwich(): pl.pallas_call(functools.partial(sandwich_kernel, first), out_shape=(pltp...  6.19 us
    unnamed x5, local copies, waits for them, and re-layouts  2.32 us
    pallas_call x1, Pallas kernels, prepare(): pl.pallas_call(prepare_kernel, out_shape=(big, big, coef, coef), in_specs...  1.61 us
    slice x1, local copies, waits for them, and re-layouts, local(): in_a, in_b = (tiles[:, :half], tiles[:, half:])  1.14 us
    pallas_call x1, Pallas kernels, finish(): pl.pallas_call(finish_kernel, out_shape=jax.ShapeDtypeStruct(shape, jnp.b...  0.91 us
  transfers between devices with their start and end apart: 8, of which 5 were waited for; matrix products, arithmetic and copies ran while one was open for 6% of the time, Pallas kernels for 20%

profile of v1, /device:TPU:7, one launch (start us, length us, event | category | flops | bytes accessed | tf_op | source)
XLA Modules:
  0.0 39.2 jit_solution(8752603266327218674)
XLA Ops:
  0.0 0.0 copy-start
  0.0 1.1 %fusion = (bf16[2,2,2,128,128]{4,3,2,1,0:T(8,128)(2,1)S(1)}, bf16[2,2,2,128,128]{4,3,2,1,0:T(8,128)(2,1)S(1)}) fusion(bf16[2,4,2,128,128]{4,3,2,1,0:T(8,128)(2,1)} %bitcast.3), kind=kLoop, calls=%fused_computation.1 | loop fusion | bytes 1048576 | tf_op jit(solution)/shard_map/slice | solution.py:205
  1.1 0.7 %collective-permute-start.4 = (bf16[2,2,2,128,128]{4,3,2,1,0:T(8,128)(2,1)S(1)}, bf16[2,2,2,128,128]{4,3,2,1,0:T(8,128)(2,1)S(1)}, u32[]{:S(2)}, u32[]{:S(2)}) collective-permute-start(bf16[2,2,2,128,128]{4,3,2,1,0:T(8,128)(2,1)S(1)} %get-tuple-element.25.own), channel_id=1, source_target_pairs={{0,1},{1,0},{2,3},{3,2},{4,5},{5,4},{6,7},{7,6},{8,9},{9,8},{10,11... | collective-permute-start | bytes 786440 | tf_op jit(solution)/shard_map/ppermute | solution.py:201
  1.9 0.2 collective-permute-start.5
  2.1 0.1 collective-permute-start
  2.1 0.8 %copy.7.weight = f32[6,3,2]{2,1,0:T(4,128)S(1)} copy(f32[6,3,2]{0,2,1:T(2,128)} %param.7) | data formatting | bytes 288 | tf_op args[2]
  2.9 0.8 %copy.6.modes = s32[6,2]{1,0:T(8,128)S(1)} copy(s32[6,2]{0,1:T(2,128)} %param.8) | data formatting | bytes 96 | tf_op args[3]
  3.7 0.8 %copy.8.pattern = s32[4,2]{1,0:T(4,128)S(1)} copy(s32[4,2]{0,1:T(2,128)} %param.9) | data formatting | bytes 64 | tf_op args[4]
  4.5 0.1 pad_add_fusion.parity
  4.5 0.0 copy-done
  4.5 1.6 %prepare.1 = (bf16[4,3,256,256]{3,2,1,0:T(8,128)(2,1)S(1)}, bf16[4,3,256,256]{3,2,1,0:T(8,128)(2,1)S(1)}, f32[108,8,128]{2,1,0:T(8,128)S(1)}, f32[108,8,128]{2,1,0:T(8,128)S(1)}) custom-call(s32[2]{0:T(128)S(1)} %pad_add_fusion.parity, s32[6,2]{1,0:T(8,128)S(1)} %copy.6.modes, f32[6,3,2]{2,1,0:T(4,128)S(1)} %copy.7.weight, s32[4,2]{1,0:T(4,128)S(1)} %copy.8.pattern, ...), custom_call_target="tpu_custom_call" | custom-call | tf_op jit(solution)/shard_map/prepare/pallas_call | solution.py:94
  6.2 0.0 collective-permute-done.4.near
  6.2 4.0 %collective-permute-done.5.far = bf16[2,2,2,128,128]{4,3,2,1,0:T(8,128)(2,1)S(1)} collective-permute-done((bf16[2,2,2,128,128]{4,3,2,1,0:T(8,128)(2,1)S(1)}, bf16[2,2,2,128,128]{4,3,2,1,0:T(8,128)(2,1)S(1)}, u32[]{:S(2)}, u32[]{:S(2)}) %collective-permute-start.5) | collective-permute-done | bytes 262176 | tf_op jit(solution)/shard_map/ppermute | solution.py:201
  10.2 3.1 %sandwich.3 = (f32[2,2,2,128,128]{4,3,2,1,0:T(8,128)S(1)}, f32[2,2,2,128,128]{4,3,2,1,0:T(8,128)S(1)}, bf16[2,2,2,128,128]{4,3,2,1,0:T(8,128)(2,1)S(1)}) custom-call(bf16[2,2,2,128,128]{4,3,2,1,0:T(8,128)(2,1)S(1)} %get-tuple-element.25.own, bf16[2,2,2,128,128]{4,3,2,1,0:T(8,128)(2,1)S(1)} %collective-permute-done.4.near, ...), custom_call_target="tpu_custom_call" | custom-call | tf_op jit(solution)/shard_map/sandwich/pallas_call | solution.py:143
  13.3 3.2 %collective-permute-start.6 = (bf16[2,2,2,128,128]{4,3,2,1,0:T(8,128)(2,1)S(1)}, bf16[2,2,2,128,128]{4,3,2,1,0:T(8,128)(2,1)S(1)}, u32[]{:S(2)}, u32[]{:S(2)}) collective-permute-start(bf16[2,2,2,128,128]{4,3,2,1,0:T(8,128)(2,1)S(1)} %get-tuple-element.24), channel_id=1, source_target_pairs={{4,12},{5,13},{6,14},{7,15},{8,0},{9,1},{10,2},{11,3},{12,20},{13,... | collective-permute-start | bytes 786440 | tf_op jit(solution)/shard_map/ppermute | solution.py:201
  16.5 0.0 collective-permute-done.near
  16.5 1.3 %collective-permute-start.1 = (bf16[2,2,2,128,128]{4,3,2,1,0:T(8,128)(2,1)S(1)}, bf16[2,2,2,128,128]{4,3,2,1,0:T(8,128)(2,1)S(1)}, u32[]{:S(2)}, u32[]{:S(2)}) collective-permute-start(bf16[2,2,2,128,128]{4,3,2,1,0:T(8,128)(2,1)S(1)} %collective-permute-done.near), channel_id=1, source_target_pairs={{0,8},{1,9},{2,10},{3,11},{8,16},{9,17},{10,18},{11,19},{12,4},{13... | collective-permute-start | bytes 786440 | tf_op jit(solution)/shard_map/ppermute | solution.py:201
  17.8 4.5 %collective-permute-done.6.b = bf16[2,2,2,128,128]{4,3,2,1,0:T(8,128)(2,1)S(1)} collective-permute-done((bf16[2,2,2,128,128]{4,3,2,1,0:T(8,128)(2,1)S(1)}, bf16[2,2,2,128,128]{4,3,2,1,0:T(8,128)(2,1)S(1)}, u32[]{:S(2)}, u32[]{:S(2)}) %collective-permute-start.6) | collective-permute-done | bytes 262176 | tf_op jit(solution)/shard_map/ppermute | solution.py:201
  22.4 1.2 %collective-permute-start.7 = (bf16[2,2,2,128,128]{4,3,2,1,0:T(8,128)(2,1)S(1)}, bf16[2,2,2,128,128]{4,3,2,1,0:T(8,128)(2,1)S(1)}, u32[]{:S(2)}, u32[]{:S(2)}) collective-permute-start(bf16[2,2,2,128,128]{4,3,2,1,0:T(8,128)(2,1)S(1)} %add.12), channel_id=1, source_target_pairs={{0,4},{1,5},{2,6},{3,7},{4,0},{5,1},{6,2},{7,3},{8,12},{9,13},{10,... | collective-permute-start | bytes 786440 | tf_op jit(solution)/shard_map/ppermute | solution.py:201
  23.6 2.7 %collective-permute-done.1.far = bf16[2,2,2,128,128]{4,3,2,1,0:T(8,128)(2,1)S(1)} collective-permute-done((bf16[2,2,2,128,128]{4,3,2,1,0:T(8,128)(2,1)S(1)}, bf16[2,2,2,128,128]{4,3,2,1,0:T(8,128)(2,1)S(1)}, u32[]{:S(2)}, u32[]{:S(2)}) %collective-permute-start.1) | collective-permute-done | bytes 262176 | tf_op jit(solution)/shard_map/ppermute | solution.py:201
  26.3 3.1 %sandwich.2 = (f32[2,2,2,128,128]{4,3,2,1,0:T(8,128)S(1)}, bf16[2,2,2,128,128]{4,3,2,1,0:T(8,128)(2,1)S(1)}, bf16[2,2,2,128,128]{4,3,2,1,0:T(8,128)(2,1)S(1)}) custom-call(bf16[2,2,2,128,128]{4,3,2,1,0:T(8,128)(2,1)S(1)} %get-tuple-element.26.own, bf16[2,2,2,128,128]{4,3,2,1,0:T(8,128)(2,1)S(1)} %collective-permute-done.near, ...), custom_call_target="tpu_custom_call" | custom-call | tf_op jit(solution)/shard_map/sandwich/pallas_call | solution.py:143
  29.4 0.9 %collective-permute-start.2 = (bf16[2,2,2,128,128]{4,3,2,1,0:T(8,128)(2,1)S(1)}, bf16[2,2,2,128,128]{4,3,2,1,0:T(8,128)(2,1)S(1)}, u32[]{:S(2)}, u32[]{:S(2)}) collective-permute-start(bf16[2,2,2,128,128]{4,3,2,1,0:T(8,128)(2,1)S(1)} %get-tuple-element.19), channel_id=1, source_target_pairs={{0,1},{1,0},{2,3},{3,2},{4,5},{5,4},{6,7},{7,6},{8,9},{9,8},{10,11... | collective-permute-start | bytes 786440 | tf_op jit(solution)/shard_map/ppermute | solution.py:201
  30.3 0.2 collective-permute-start.3
  30.5 0.0 collective-permute-done.7.near_b
  30.5 1.0 %collective-permute-done.2.near_a = bf16[2,2,2,128,128]{4,3,2,1,0:T(8,128)(2,1)S(1)} collective-permute-done((bf16[2,2,2,128,128]{4,3,2,1,0:T(8,128)(2,1)S(1)}, bf16[2,2,2,128,128]{4,3,2,1,0:T(8,128)(2,1)S(1)}, u32[]{:S(2)}, u32[]{:S(2)}) %collective-permute-start.2) | collective-permute-done | bytes 262176 | tf_op jit(solution)/shard_map/ppermute | solution.py:201
  31.5 6.8 %collective-permute-done.3.far_a = bf16[2,2,2,128,128]{4,3,2,1,0:T(8,128)(2,1)S(1)} collective-permute-done((bf16[2,2,2,128,128]{4,3,2,1,0:T(8,128)(2,1)S(1)}, bf16[2,2,2,128,128]{4,3,2,1,0:T(8,128)(2,1)S(1)}, u32[]{:S(2)}, u32[]{:S(2)}) %collective-permute-start.3) | collective-permute-done | bytes 262176 | tf_op jit(solution)/shard_map/ppermute | solution.py:201
  38.3 0.9 %finish.1 = bf16[1,2,4,2,128,128]{5,4,3,2,1,0:T(8,128)(2,1)} custom-call(f32[2,2,2,128,128]{4,3,2,1,0:T(8,128)S(1)} %get-tuple-element.18.own_a, bf16[2,2,2,128,128]{4,3,2,1,0:T(8,128)(2,1)S(1)} %collective-permute-done.2.near_a, bf16[2,2,2,128,128]{4,3,2,1,0:T(8,128)(2,1)S(1)} %collective-permute-done.3.far_a, ...), custom_call_target="tpu_custom_call" | custom-call | tf_op jit(solution)/shard_map/finish/pallas_call | solution.py:186
  (1 shorter events, 0.0 us)
Async XLA Ops:
  0.0 4.5 %copy-start = (bf16[3,4,2,128,128]{4,3,2,1,0:T(8,128)(2,1)S(1)}, bf16[3,4,2,128,128]{4,3,2,1,0:T(8,128)(2,1)}, u32[]{:S(2)}) copy-start(bf16[3,4,2,128,128]{4,3,2,1,0:T(8,128)(2,1)} %dham.1) | copy-start | bytes 2359300
  1.1 5.0 %collective-permute-start.4 = (bf16[2,2,2,128,128]{4,3,2,1,0:T(8,128)(2,1)S(1)}, bf16[2,2,2,128,128]{4,3,2,1,0:T(8,128)(2,1)S(1)}, u32[]{:S(2)}, u32[]{:S(2)}) collective-permute-start(bf16[2,2,2,128,128]{4,3,2,1,0:T(8,128)(2,1)S(1)} %get-tuple-element.25.own), channel_id=1, source_target_pairs={{0,1},{1,0},{2,3},{3,2},{4,5},{5,4},{6,7},{7,6},{8,9},{9,8},{10,11... | collective-permute-start | bytes 786440 | tf_op jit(solution)/shard_map/ppermute | solution.py:201
  1.9 8.3 %collective-permute-start.5 = (bf16[2,2,2,128,128]{4,3,2,1,0:T(8,128)(2,1)S(1)}, bf16[2,2,2,128,128]{4,3,2,1,0:T(8,128)(2,1)S(1)}, u32[]{:S(2)}, u32[]{:S(2)}) collective-permute-start(bf16[2,2,2,128,128]{4,3,2,1,0:T(8,128)(2,1)S(1)} %get-tuple-element.25.own), channel_id=1, source_target_pairs={{0,3},{1,2},{2,1},{3,0},{4,7},{5,6},{6,5},{7,4},{8,11},{9,10},{10,... | collective-permute-start | bytes 786440 | tf_op jit(solution)/shard_map/ppermute | solution.py:201
  2.1 14.4 %collective-permute-start = (bf16[2,2,2,128,128]{4,3,2,1,0:T(8,128)(2,1)S(1)}, bf16[2,2,2,128,128]{4,3,2,1,0:T(8,128)(2,1)S(1)}, u32[]{:S(2)}, u32[]{:S(2)}) collective-permute-start(bf16[2,2,2,128,128]{4,3,2,1,0:T(8,128)(2,1)S(1)} %get-tuple-element.26.own), channel_id=1, source_target_pairs={{0,4},{1,5},{2,6},{3,7},{4,0},{5,1},{6,2},{7,3},{8,12},{9,13},{10,... | collective-permute-start | bytes 786440 | tf_op jit(solution)/shard_map/ppermute | solution.py:201
  13.3 9.0 %collective-permute-start.6 = (bf16[2,2,2,128,128]{4,3,2,1,0:T(8,128)(2,1)S(1)}, bf16[2,2,2,128,128]{4,3,2,1,0:T(8,128)(2,1)S(1)}, u32[]{:S(2)}, u32[]{:S(2)}) collective-permute-start(bf16[2,2,2,128,128]{4,3,2,1,0:T(8,128)(2,1)S(1)} %get-tuple-element.24), channel_id=1, source_target_pairs={{4,12},{5,13},{6,14},{7,15},{8,0},{9,1},{10,2},{11,3},{12,20},{13,... | collective-permute-start | bytes 786440 | tf_op jit(solution)/shard_map/ppermute | solution.py:201
  16.5 9.8 %collective-permute-start.1 = (bf16[2,2,2,128,128]{4,3,2,1,0:T(8,128)(2,1)S(1)}, bf16[2,2,2,128,128]{4,3,2,1,0:T(8,128)(2,1)S(1)}, u32[]{:S(2)}, u32[]{:S(2)}) collective-permute-start(bf16[2,2,2,128,128]{4,3,2,1,0:T(8,128)(2,1)S(1)} %collective-permute-done.near), channel_id=1, source_target_pairs={{0,8},{1,9},{2,10},{3,11},{8,16},{9,17},{10,18},{11,19},{12,4},{13... | collective-permute-start | bytes 786440 | tf_op jit(solution)/shard_map/ppermute | solution.py:201
  22.4 8.2 %collective-permute-start.7 = (bf16[2,2,2,128,128]{4,3,2,1,0:T(8,128)(2,1)S(1)}, bf16[2,2,2,128,128]{4,3,2,1,0:T(8,128)(2,1)S(1)}, u32[]{:S(2)}, u32[]{:S(2)}) collective-permute-start(bf16[2,2,2,128,128]{4,3,2,1,0:T(8,128)(2,1)S(1)} %add.12), channel_id=1, source_target_pairs={{0,4},{1,5},{2,6},{3,7},{4,0},{5,1},{6,2},{7,3},{8,12},{9,13},{10,... | collective-permute-start | bytes 786440 | tf_op jit(solution)/shard_map/ppermute | solution.py:201
  29.4 2.1 %collective-permute-start.2 = (bf16[2,2,2,128,128]{4,3,2,1,0:T(8,128)(2,1)S(1)}, bf16[2,2,2,128,128]{4,3,2,1,0:T(8,128)(2,1)S(1)}, u32[]{:S(2)}, u32[]{:S(2)}) collective-permute-start(bf16[2,2,2,128,128]{4,3,2,1,0:T(8,128)(2,1)S(1)} %get-tuple-element.19), channel_id=1, source_target_pairs={{0,1},{1,0},{2,3},{3,2},{4,5},{5,4},{6,7},{7,6},{8,9},{9,8},{10,11... | collective-permute-start | bytes 786440 | tf_op jit(solution)/shard_map/ppermute | solution.py:201
  30.3 8.0 %collective-permute-start.3 = (bf16[2,2,2,128,128]{4,3,2,1,0:T(8,128)(2,1)S(1)}, bf16[2,2,2,128,128]{4,3,2,1,0:T(8,128)(2,1)S(1)}, u32[]{:S(2)}, u32[]{:S(2)}) collective-permute-start(bf16[2,2,2,128,128]{4,3,2,1,0:T(8,128)(2,1)S(1)} %get-tuple-element.20), channel_id=1, source_target_pairs={{0,3},{1,2},{2,1},{3,0},{4,7},{5,6},{6,5},{7,4},{8,11},{9,10},{10,... | collective-permute-start | bytes 786440 | tf_op jit(solution)/shard_map/ppermute | solution.py:201

commit v2 on v1

v2 whole, which is shorter than its diff:
```python
import functools
import jax
import jax.numpy as jnp
from jax import lax
from jax.experimental import pallas as pl
from jax.experimental.pallas import tpu as pltpu
from jax.sharding import PartitionSpec as P

AXES = ("energy", "momentum")
DIRS = 3
REACH = 2
EVEN = 3 * DIRS * (2 * REACH + 1)
AT_REST = EVEN + 1
ENTRIES = EVEN + 2
ROWS = 32
GRANT = 16 * 2**20


def in_vmem(array):
    return pltpu.with_memory_space_constraint(array, pltpu.VMEM)


def in_hbm(array):
    return pltpu.with_memory_space_constraint(array, pltpu.HBM)


def vmem_specs(count):
    return [pl.BlockSpec(memory_space=pltpu.VMEM)] * count


def routes(n_e, n_k):
    def pairs(step):
        out = []
        for e in range(n_e):
            for k in range(n_k):
                to_e, to_k = step(e, k)
                if 0 <= to_e < n_e:
                    out.append((e * n_k + k, to_e * n_k + to_k % n_k))
        return out

    return {
        "pair": pairs(lambda e, k: (e ^ 1, k)),
        "relay": pairs(lambda e, k: (e + 2 - 4 * (e % 2), k)),
        "cross": pairs(lambda e, k: (e - 1 + 2 * (e % 2), k)),
        "core": pairs(lambda e, k: (e, k ^ 1)),
        "far": pairs(lambda e, k: (e, k - 1 + 2 * (k % 2))),
    }


def prepare_kernel(parity, modes, weight, pattern, dham, left, right, coef, table):
    mode_count = modes.shape[1]
    tile_count = pattern.shape[1]
    for q in range(4):
        for d in range(DIRS):
            for s in range(2 * REACH + 1):
                table[q, d, s] = 0.0
    for m in range(mode_count):
        q = modes[0, m] + 1
        step = modes[1, m]
        for d in range(DIRS):
            table[q, d, REACH - step] = table[q, d, REACH - step] + weight[d, 0, m]
            table[q, d, REACH + step] = table[q, d, REACH + step] + weight[d, 1, m]
    toward = 1 - 2 * parity[1]
    at_rest = 0.0
    for slot, q in enumerate((0, toward, -toward)):
        for d in range(DIRS):
            for s in range(2 * REACH + 1):
                value = table[q + 1, d, s]
                if s == REACH:
                    at_rest = at_rest + jnp.abs(value)
                value = jnp.full((8, 128), value, jnp.float32)
                coef[(slot * DIRS + d) * (2 * REACH + 1) + s] = value.astype(jnp.bfloat16).astype(jnp.float32)
    coef[EVEN] = jnp.full((8, 128), 1 - parity[0], jnp.int32).astype(jnp.float32)
    coef[AT_REST] = jnp.full((8, 128), at_rest, jnp.float32)
    for t in range(tile_count):
        lo, hi = pattern[0, t], pattern[1, t]
        for d in range(DIRS):
            real, imag = dham[d, lo, 0], dham[d, lo, 1]
            left[t, d, :128, :128] = real
            left[t, d, :128, 128:] = -imag
            left[t, d, 128:, :128] = imag
            left[t, d, 128:, 128:] = real
            real, imag = dham[d, hi, 0].T, dham[d, hi, 1].T
            right[t, d, :128, :128] = real
            right[t, d, :128, 128:] = -imag
            right[t, d, 128:, :128] = imag
            right[t, d, 128:, 128:] = real


def prepare(parity, modes, weight, pattern, dham):
    tile_count = pattern.shape[1]
    big = pltpu.VMEM((tile_count, DIRS, 256, 256), jnp.bfloat16)
    return pl.pallas_call(
        prepare_kernel,
        out_shape=(big, big, pltpu.VMEM((ENTRIES, 8, 128), jnp.float32)),
        in_specs=[pl.BlockSpec(memory_space=pltpu.SMEM)] * 4 + vmem_specs(1),
        out_specs=tuple(vmem_specs(3)),
        scratch_shapes=[pltpu.SMEM((4, DIRS, 2 * REACH + 1), jnp.float32)],
        compiler_params=pltpu.CompilerParams(vmem_limit_bytes=GRANT),
        name="prepare",
    )(parity, in_hbm(modes), in_hbm(weight), in_hbm(pattern), in_hbm(dham))


def mix(t, forward, steps, sources, coef, mixed):
    even = coef[EVEN] > 0.5
    own, near, far = sources

    def at(slot, d, s):
        return coef[(slot * DIRS + d) * (2 * REACH + 1) + s + REACH]

    for part in range(2):
        for row in range(0, 128, ROWS):

            def load(ref, j):
                return ref[j, t, part, pl.ds(row, ROWS), :].astype(jnp.float32).reshape(ROWS // 8, 8, 128)

            taken = [[load(ref, j) for j in range(2)] for ref in sources]
            if forward:
                below = [jnp.where(even, b, a) for a, b in zip(taken[1], taken[2])]
                above = [jnp.where(even, a, b) for a, b in zip(taken[1], taken[2])]
                line = below + taken[0] + above
            for d in range(DIRS):
                for item in range(6):
                    if forward:
                        slot, i = divmod(item, 2)
                        terms = [(line[2 + i + s], at(slot, d, s)) for s in steps]
                    else:
                        place = item - 2
                        terms = [(taken[m][j], at((0, 2, 1)[m], d, j - place)) for m in range(3) for j in range(2) if j - place in steps]
                    acc = terms[0][0] * terms[0][1]
                    for value, factor in terms[1:]:
                        acc = acc + value * factor
                    mixed[t, d, pl.ds(part * 128 + row, ROWS), pl.ds(item * 128, 128)] = acc.reshape(ROWS, 128).astype(jnp.bfloat16)


def multiply(t, first, forward, left, right, coef, outs, mixed, product):
    for d in range(DIRS):
        got = jnp.dot(left[first + t, d], mixed[t, d], preferred_element_type=jnp.float32).astype(jnp.bfloat16)
        for item in range(6):
            for part in range(2):
                product[t, pl.ds(item * 128, 128), pl.ds(d * 256 + part * 128, 128)] = got[
                    part * 128 : part * 128 + 128, item * 128 : item * 128 + 128
                ]
    term = jnp.dot(product[t], right[first + t].reshape(DIRS * 256, 256), preferred_element_type=jnp.float32)
    even = jnp.broadcast_to(coef[EVEN][:1] > 0.5, (128, 128))
    for i in range(2):
        for part in range(2):

            def result(item):
                return term[item * 128 : item * 128 + 128, part * 128 : part * 128 + 128]

            if forward:
                values = [result(slot * 2 + i) for slot in range(3)]
            else:
                below, own, above = (result(block * 2 + i) for block in range(3))
                values = [own, jnp.where(even, above, below), jnp.where(even, below, above)]
            for out, value in zip(outs, values):
                out[i, t, part] = value.astype(out.dtype)


def sandwich_kernel(first, forward, own, near, far, left, right, coef, to_own, to_near, to_far, mixed, product):
    tiles = own.shape[1]
    outs = (to_own, to_near, to_far)
    at_rest = jnp.max(coef[AT_REST])

    def run(t, steps):
        mix(t, forward, steps, (own, near, far), coef, mixed)
        multiply(t, first, forward, left, right, coef, outs, mixed, product)

    @pl.when(at_rest == 0.0)
    def _():
        for t in range(tiles):
            run(t, (-2, -1, 1, 2))

    @pl.when(at_rest != 0.0)
    def _():
        @pl.loop(0, tiles)
        def _(t):
            run(t, (-2, -1, 0, 1, 2))


def sandwich(first, forward, own, near, far, left, right, coef):
    shape = own.shape
    tiles = shape[1]
    return pl.pallas_call(
        functools.partial(sandwich_kernel, first, forward),
        out_shape=(
            pltpu.VMEM(shape, jnp.float32),
            pltpu.VMEM(shape, jnp.bfloat16),
            pltpu.VMEM(shape, jnp.bfloat16),
        ),
        in_specs=vmem_specs(6),
        out_specs=tuple(vmem_specs(3)),
        scratch_shapes=[
            pltpu.VMEM((tiles, DIRS, 256, 6 * 128), jnp.bfloat16),
            pltpu.VMEM((tiles, 6 * 128, DIRS * 256), jnp.bfloat16),
        ],
        compiler_params=pltpu.CompilerParams(vmem_limit_bytes=GRANT),
        cost_estimate=pl.CostEstimate(flops=1_200_000_000 * tiles, bytes_accessed=4_000_000 * tiles, transcendentals=0),
        name="sandwich",
    )(in_vmem(own), in_vmem(near), in_vmem(far), in_vmem(left), in_vmem(right), in_vmem(coef))


def gather_kernel(own, near, far, out):
    f32 = jnp.float32
    out[...] = (own[...] + near[...].astype(f32) + far[...].astype(f32)).astype(out.dtype)


def gather(own, near, far):
    return pl.pallas_call(
        gather_kernel,
        out_shape=pltpu.VMEM(own.shape, jnp.bfloat16),
        in_specs=vmem_specs(3),
        out_specs=vmem_specs(1)[0],
        compiler_params=pltpu.CompilerParams(vmem_limit_bytes=GRANT),
        cost_estimate=pl.CostEstimate(flops=4_000_000_000, bytes_accessed=16_000_000, transcendentals=0),
        name="gather",
    )(*map(in_vmem, (own, near, far)))


def finish_kernel(own_a, near_a, far_a, done_b, out, held, sems):
    tiles_a, tiles_b = own_a.shape[1], done_b.shape[1]
    f32 = jnp.float32
    copies = [pltpu.make_async_copy(done_b, out.at[0, :, pl.ds(tiles_a, tiles_b)], sems.at[tiles_a])]
    copies[0].start()
    for t in range(tiles_a):
        held[:, t] = (own_a[:, t] + near_a[:, t].astype(f32) + far_a[:, t].astype(f32)).astype(held.dtype)
        copies.append(pltpu.make_async_copy(held.at[:, t], out.at[0, :, t], sems.at[t]))
        copies[-1].start()
    for copy in copies:
        copy.wait()


def finish(own_a, near_a, far_a, done_b):
    e, tiles_a = own_a.shape[:2]
    rest = own_a.shape[2:]
    return pl.pallas_call(
        finish_kernel,
        out_shape=jax.ShapeDtypeStruct((1, e, tiles_a + done_b.shape[1]) + rest, jnp.bfloat16),
        in_specs=vmem_specs(4),
        out_specs=pl.BlockSpec(memory_space=pl.ANY),
        scratch_shapes=[pltpu.VMEM((e, tiles_a) + rest, jnp.bfloat16), pltpu.SemaphoreType.DMA((tiles_a + 1,))],
        compiler_params=pltpu.CompilerParams(vmem_limit_bytes=GRANT),
        name="finish",
    )(*map(in_vmem, (own_a, near_a, far_a, done_b)))


def local(green_tiles, dham_blocks, phonon_weight, phonon_modes, tile_pattern):
    n_e, n_k = (lax.axis_size(axis) for axis in AXES)
    route = routes(n_e, n_k)

    def send(block, name):
        return lax.ppermute(block, AXES, route[name])

    tiles = green_tiles[0]
    half = tiles.shape[1] // 2
    in_a, in_b = tiles[:, :half], tiles[:, half:]
    parity = jnp.stack([lax.axis_index(axis) % 2 for axis in AXES]).astype(jnp.int32)
    near_a = send(in_a, "pair")
    far_b = send(in_b, "far")
    near_b = send(in_b, "core")
    left, right, coef = prepare(parity, phonon_modes.T, phonon_weight.transpose(1, 2, 0), tile_pattern.T, dham_blocks)
    near_a, left = lax.optimization_barrier((near_a, left))
    far_a = send(near_a, "relay")
    far_b, near_a = lax.optimization_barrier((far_b, near_a))
    own_b, pair_b, cross_b = sandwich(half, False, in_b, near_b, far_b, left, right, coef)
    pair_b = send(pair_b, "pair")
    cross_b = send(cross_b, "cross")
    own_a, core_a, next_a = sandwich(0, True, in_a, near_a, far_a, left, right, coef)
    next_a = send(next_a, "far")
    core_a = send(core_a, "core")
    done_b = gather(own_b, pair_b, cross_b)
    return finish(own_a, core_a, next_a, done_b)


def solution(mesh):
    placed = (P("momentum", "energy", None, None, None, None), P(), P(), P(), P())
    return jax.shard_map(
        local,
        mesh=mesh,
        in_specs=placed,
        out_specs=P("momentum", "energy", None, None, None, None),
        check_vma=False,
    )
```

time: 39.5 us -> 31.7 us (0.80)
  the two profiles are of different devices: /device:TPU:7 before, /device:TPU:19 now
where the time goes in v2:
time: 31.7 us; the launch traced here: 31.5 us
  starting transfers between devices  12.5 us (39%)
  waiting for transfers between devices  9.91 us (31%)
  Pallas kernels  7.87 us (25%)
  local copies, waits for them, and re-layouts  1.06 us (3%)
    ppermute x8, starting transfers between devices, send(): return lax.ppermute(block, AXES, route[name])  12.5 us
    ppermute x8, waiting for transfers between devices, send(): return lax.ppermute(block, AXES, route[name])  9.91 us
    pallas_call x2, Pallas kernels, sandwich(): pl.pallas_call(functools.partial(sandwich_kernel, first, forward), out_sh...  5.32 us
    pallas_call x1, Pallas kernels, prepare(): pl.pallas_call(prepare_kernel, out_shape=(big, big, pltpu.VMEM((ENTRIES,...  1.63 us
    slice x1, local copies, waits for them, and re-layouts, local(): in_a, in_b = (tiles[:, :half], tiles[:, half:])  1.06 us
    pallas_call x1, Pallas kernels, finish(): pl.pallas_call(finish_kernel, out_shape=jax.ShapeDtypeStruct((1, e, tiles...  0.81 us
  transfers between devices with their start and end apart: 8, of which 3 were waited for; matrix products, arithmetic and copies ran while one was open for 0% of the time, Pallas kernels for 22%

profile of v2, /device:TPU:19, one launch (start us, length us, event | category | flops | bytes accessed | tf_op | source)
XLA Modules:
  0.0 31.5 jit_solution(17214927376010648152)
XLA Ops:
  0.0 1.1 %fusion = (bf16[2,2,2,128,128]{4,3,2,1,0:T(8,128)(2,1)S(1)}, bf16[2,2,2,128,128]{4,3,2,1,0:T(8,128)(2,1)S(1)}) fusion(bf16[2,4,2,128,128]{4,3,2,1,0:T(8,128)(2,1)} %bitcast.6), kind=kLoop, calls=%fused_computation.1 | loop fusion | bytes 1048576 | tf_op jit(solution)/shard_map/slice | solution.py:257
  1.1 0.3 %collective-permute-start.1 = (bf16[2,2,2,128,128]{4,3,2,1,0:T(8,128)(2,1)S(1)}, bf16[2,2,2,128,128]{4,3,2,1,0:T(8,128)(2,1)S(1)}, u32[]{:S(2)}, u32[]{:S(2)}) collective-permute-start(bf16[2,2,2,128,128]{4,3,2,1,0:T(8,128)(2,1)S(1)} %get-tuple-element.32.own), channel_id=1, source_target_pairs={{0,4},{1,5},{2,6},{3,7},{4,0},{5,1},{6,2},{7,3},{8,12},{9,13},{10,... | collective-permute-start | bytes 786440 | tf_op jit(solution)/shard_map/ppermute | solution.py:253
  1.4 2.1 %collective-permute-start = (bf16[2,2,2,128,128]{4,3,2,1,0:T(8,128)(2,1)S(1)}, bf16[2,2,2,128,128]{4,3,2,1,0:T(8,128)(2,1)S(1)}, u32[]{:S(2)}, u32[]{:S(2)}) collective-permute-start(bf16[2,2,2,128,128]{4,3,2,1,0:T(8,128)(2,1)S(1)} %get-tuple-element.31.own), channel_id=1, source_target_pairs={{0,3},{1,2},{2,1},{3,0},{4,7},{5,6},{6,5},{7,4},{8,11},{9,10},{10,... | collective-permute-start | bytes 786440 | tf_op jit(solution)/shard_map/ppermute | solution.py:253
  3.5 0.0 collective-permute-start.5
  3.5 0.1 pad_add_fusion.parity
  3.5 1.6 %prepare.1 = (bf16[4,3,256,256]{3,2,1,0:T(8,128)(2,1)S(1)}, bf16[4,3,256,256]{3,2,1,0:T(8,128)(2,1)S(1)}, f32[47,8,128]{2,1,0:T(8,128)S(1)}) custom-call(s32[2]{0:T(128)S(1)} %pad_add_fusion.parity, s32[2,6]{1,0:T(2,128)} %bitcast.8, f32[3,2,6]{2,1,0:T(2,128)} %bitcast.7, s32[2,4]{1,0:T(2,128)} %bitcast.9, bf16[3,4,2,128,128]{4,3,2,1,0:T(8,128)(2,1)} %dham.1), custom_call_target="tpu_custom_call" | custom-call | tf_op jit(solution)/shard_map/prepare/pallas_call | solution.py:93
  5.2 3.1 %collective-permute-done.1.near = bf16[2,2,2,128,128]{4,3,2,1,0:T(8,128)(2,1)S(1)} collective-permute-done((bf16[2,2,2,128,128]{4,3,2,1,0:T(8,128)(2,1)S(1)}, bf16[2,2,2,128,128]{4,3,2,1,0:T(8,128)(2,1)S(1)}, u32[]{:S(2)}, u32[]{:S(2)}) %collective-permute-start.1) | collective-permute-done | bytes 262176 | tf_op jit(solution)/shard_map/ppermute | solution.py:253
  8.3 2.1 %collective-permute-start.2 = (bf16[2,2,2,128,128]{4,3,2,1,0:T(8,128)(2,1)S(1)}, bf16[2,2,2,128,128]{4,3,2,1,0:T(8,128)(2,1)S(1)}, u32[]{:S(2)}, u32[]{:S(2)}) collective-permute-start(bf16[2,2,2,128,128]{4,3,2,1,0:T(8,128)(2,1)S(1)} %collective-permute-done.1.near), channel_id=1, source_target_pairs={{0,8},{1,9},{2,10},{3,11},{8,16},{9,17},{10,18},{11,19},{12,4},{13... | collective-permute-start | bytes 786440 | tf_op jit(solution)/shard_map/ppermute | solution.py:253
  10.4 0.1 collective-permute-done.far
  10.5 0.0 collective-permute-done.5.near
  10.5 2.7 %sandwich.3 = (f32[2,2,2,128,128]{4,3,2,1,0:T(8,128)S(1)}, bf16[2,2,2,128,128]{4,3,2,1,0:T(8,128)(2,1)S(1)}, bf16[2,2,2,128,128]{4,3,2,1,0:T(8,128)(2,1)S(1)}) custom-call(bf16[2,2,2,128,128]{4,3,2,1,0:T(8,128)(2,1)S(1)} %get-tuple-element.31.own, bf16[2,2,2,128,128]{4,3,2,1,0:T(8,128)(2,1)S(1)} %collective-permute-done.5.near, ...), custom_call_target="tpu_custom_call" | custom-call | flops 2400000000 | bytes 8000000 | tf_op jit(solution)/shard_map/sandwich/pallas_call | solution.py:185
  13.2 1.4 %collective-permute-start.6 = (bf16[2,2,2,128,128]{4,3,2,1,0:T(8,128)(2,1)S(1)}, bf16[2,2,2,128,128]{4,3,2,1,0:T(8,128)(2,1)S(1)}, u32[]{:S(2)}, u32[]{:S(2)}) collective-permute-start(bf16[2,2,2,128,128]{4,3,2,1,0:T(8,128)(2,1)S(1)} %get-tuple-element.29), channel_id=1, source_target_pairs={{0,4},{1,5},{2,6},{3,7},{4,0},{5,1},{6,2},{7,3},{8,12},{9,13},{10,... | collective-permute-start | bytes 786440 | tf_op jit(solution)/shard_map/ppermute | solution.py:253
  14.5 3.1 %collective-permute-start.7 = (bf16[2,2,2,128,128]{4,3,2,1,0:T(8,128)(2,1)S(1)}, bf16[2,2,2,128,128]{4,3,2,1,0:T(8,128)(2,1)S(1)}, u32[]{:S(2)}, u32[]{:S(2)}) collective-permute-start(bf16[2,2,2,128,128]{4,3,2,1,0:T(8,128)(2,1)S(1)} %get-tuple-element.30), channel_id=1, source_target_pairs={{4,8},{5,9},{6,10},{7,11},{8,4},{9,5},{10,6},{11,7},{12,16},{13,17... | collective-permute-start | bytes 786440 | tf_op jit(solution)/shard_map/ppermute | solution.py:253
  17.6 0.0 collective-permute-done.2.far
  17.6 2.7 %sandwich.2 = (f32[2,2,2,128,128]{4,3,2,1,0:T(8,128)S(1)}, bf16[2,2,2,128,128]{4,3,2,1,0:T(8,128)(2,1)S(1)}, bf16[2,2,2,128,128]{4,3,2,1,0:T(8,128)(2,1)S(1)}) custom-call(bf16[2,2,2,128,128]{4,3,2,1,0:T(8,128)(2,1)S(1)} %get-tuple-element.32.own, bf16[2,2,2,128,128]{4,3,2,1,0:T(8,128)(2,1)S(1)} %collective-permute-done.1.near, ...), custom_call_target="tpu_custom_call" | custom-call | flops 2400000000 | bytes 8000000 | tf_op jit(solution)/shard_map/sandwich/pallas_call | solution.py:185
  20.3 2.4 %collective-permute-start.3 = (bf16[2,2,2,128,128]{4,3,2,1,0:T(8,128)(2,1)S(1)}, bf16[2,2,2,128,128]{4,3,2,1,0:T(8,128)(2,1)S(1)}, u32[]{:S(2)}, u32[]{:S(2)}) collective-permute-start(bf16[2,2,2,128,128]{4,3,2,1,0:T(8,128)(2,1)S(1)} %get-tuple-element.25), channel_id=1, source_target_pairs={{0,1},{1,0},{2,3},{3,2},{4,5},{5,4},{6,7},{7,6},{8,9},{9,8},{10,11... | collective-permute-start | bytes 786440 | tf_op jit(solution)/shard_map/ppermute | solution.py:253
  22.7 1.2 %collective-permute-start.4 = (bf16[2,2,2,128,128]{4,3,2,1,0:T(8,128)(2,1)S(1)}, bf16[2,2,2,128,128]{4,3,2,1,0:T(8,128)(2,1)S(1)}, u32[]{:S(2)}, u32[]{:S(2)}) collective-permute-start(bf16[2,2,2,128,128]{4,3,2,1,0:T(8,128)(2,1)S(1)} %get-tuple-element.26), channel_id=1, source_target_pairs={{0,3},{1,2},{2,1},{3,0},{4,7},{5,6},{6,5},{7,4},{8,11},{9,10},{10,... | collective-permute-start | bytes 786440 | tf_op jit(solution)/shard_map/ppermute | solution.py:253
  23.9 0.0 collective-permute-done.6.near
  23.9 0.0 collective-permute-done.7.far
  23.9 0.1 gather.1.done_b
  24.0 0.0 collective-permute-done.3.near_a
  24.0 6.7 %collective-permute-done.4.far_a = bf16[2,2,2,128,128]{4,3,2,1,0:T(8,128)(2,1)S(1)} collective-permute-done((bf16[2,2,2,128,128]{4,3,2,1,0:T(8,128)(2,1)S(1)}, bf16[2,2,2,128,128]{4,3,2,1,0:T(8,128)(2,1)S(1)}, u32[]{:S(2)}, u32[]{:S(2)}) %collective-permute-start.4) | collective-permute-done | bytes 262176 | tf_op jit(solution)/shard_map/ppermute | solution.py:253
  30.7 0.8 %finish.1 = bf16[1,2,4,2,128,128]{5,4,3,2,1,0:T(8,128)(2,1)} custom-call(f32[2,2,2,128,128]{4,3,2,1,0:T(8,128)S(1)} %get-tuple-element.24.own_a, bf16[2,2,2,128,128]{4,3,2,1,0:T(8,128)(2,1)S(1)} %collective-permute-done.3.near_a, bf16[2,2,2,128,128]{4,3,2,1,0:T(8,128)(2,1)S(1)} %collective-permute-done.4.far_a, bf16[2,2,2,128,128]{4,3,2,1,0:T(8,128)(2,1)S(1)} %gather.1.done_b), custom_call_target="tpu_custom_call" | custom-call | tf_op jit(solution)/shard_map/finish/pallas_call | solution.py:237
Async XLA Ops:
  1.1 7.2 %collective-permute-start.1 = (bf16[2,2,2,128,128]{4,3,2,1,0:T(8,128)(2,1)S(1)}, bf16[2,2,2,128,128]{4,3,2,1,0:T(8,128)(2,1)S(1)}, u32[]{:S(2)}, u32[]{:S(2)}) collective-permute-start(bf16[2,2,2,128,128]{4,3,2,1,0:T(8,128)(2,1)S(1)} %get-tuple-element.32.own), channel_id=1, source_target_pairs={{0,4},{1,5},{2,6},{3,7},{4,0},{5,1},{6,2},{7,3},{8,12},{9,13},{10,... | collective-permute-start | bytes 786440 | tf_op jit(solution)/shard_map/ppermute | solution.py:253
  1.4 9.1 %collective-permute-start = (bf16[2,2,2,128,128]{4,3,2,1,0:T(8,128)(2,1)S(1)}, bf16[2,2,2,128,128]{4,3,2,1,0:T(8,128)(2,1)S(1)}, u32[]{:S(2)}, u32[]{:S(2)}) collective-permute-start(bf16[2,2,2,128,128]{4,3,2,1,0:T(8,128)(2,1)S(1)} %get-tuple-element.31.own), channel_id=1, source_target_pairs={{0,3},{1,2},{2,1},{3,0},{4,7},{5,6},{6,5},{7,4},{8,11},{9,10},{10,... | collective-permute-start | bytes 786440 | tf_op jit(solution)/shard_map/ppermute | solution.py:253
  3.5 7.0 %collective-permute-start.5 = (bf16[2,2,2,128,128]{4,3,2,1,0:T(8,128)(2,1)S(1)}, bf16[2,2,2,128,128]{4,3,2,1,0:T(8,128)(2,1)S(1)}, u32[]{:S(2)}, u32[]{:S(2)}) collective-permute-start(bf16[2,2,2,128,128]{4,3,2,1,0:T(8,128)(2,1)S(1)} %get-tuple-element.31.own), channel_id=1, source_target_pairs={{0,1},{1,0},{2,3},{3,2},{4,5},{5,4},{6,7},{7,6},{8,9},{9,8},{10,11... | collective-permute-start | bytes 786440 | tf_op jit(solution)/shard_map/ppermute | solution.py:253
  8.3 9.3 %collective-permute-start.2 = (bf16[2,2,2,128,128]{4,3,2,1,0:T(8,128)(2,1)S(1)}, bf16[2,2,2,128,128]{4,3,2,1,0:T(8,128)(2,1)S(1)}, u32[]{:S(2)}, u32[]{:S(2)}) collective-permute-start(bf16[2,2,2,128,128]{4,3,2,1,0:T(8,128)(2,1)S(1)} %collective-permute-done.1.near), channel_id=1, source_target_pairs={{0,8},{1,9},{2,10},{3,11},{8,16},{9,17},{10,18},{11,19},{12,4},{13... | collective-permute-start | bytes 786440 | tf_op jit(solution)/shard_map/ppermute | solution.py:253
  13.2 10.7 %collective-permute-start.6 = (bf16[2,2,2,128,128]{4,3,2,1,0:T(8,128)(2,1)S(1)}, bf16[2,2,2,128,128]{4,3,2,1,0:T(8,128)(2,1)S(1)}, u32[]{:S(2)}, u32[]{:S(2)}) collective-permute-start(bf16[2,2,2,128,128]{4,3,2,1,0:T(8,128)(2,1)S(1)} %get-tuple-element.29), channel_id=1, source_target_pairs={{0,4},{1,5},{2,6},{3,7},{4,0},{5,1},{6,2},{7,3},{8,12},{9,13},{10,... | collective-permute-start | bytes 786440 | tf_op jit(solution)/shard_map/ppermute | solution.py:253
  14.5 9.3 %collective-permute-start.7 = (bf16[2,2,2,128,128]{4,3,2,1,0:T(8,128)(2,1)S(1)}, bf16[2,2,2,128,128]{4,3,2,1,0:T(8,128)(2,1)S(1)}, u32[]{:S(2)}, u32[]{:S(2)}) collective-permute-start(bf16[2,2,2,128,128]{4,3,2,1,0:T(8,128)(2,1)S(1)} %get-tuple-element.30), channel_id=1, source_target_pairs={{4,8},{5,9},{6,10},{7,11},{8,4},{9,5},{10,6},{11,7},{12,16},{13,17... | collective-permute-start | bytes 786440 | tf_op jit(solution)/shard_map/ppermute | solution.py:253
  20.3 3.7 %collective-permute-start.3 = (bf16[2,2,2,128,128]{4,3,2,1,0:T(8,128)(2,1)S(1)}, bf16[2,2,2,128,128]{4,3,2,1,0:T(8,128)(2,1)S(1)}, u32[]{:S(2)}, u32[]{:S(2)}) collective-permute-start(bf16[2,2,2,128,128]{4,3,2,1,0:T(8,128)(2,1)S(1)} %get-tuple-element.25), channel_id=1, source_target_pairs={{0,1},{1,0},{2,3},{3,2},{4,5},{5,4},{6,7},{7,6},{8,9},{9,8},{10,11... | collective-permute-start | bytes 786440 | tf_op jit(solution)/shard_map/ppermute | solution.py:253
  22.7 8.0 %collective-permute-start.4 = (bf16[2,2,2,128,128]{4,3,2,1,0:T(8,128)(2,1)S(1)}, bf16[2,2,2,128,128]{4,3,2,1,0:T(8,128)(2,1)S(1)}, u32[]{:S(2)}, u32[]{:S(2)}) collective-permute-start(bf16[2,2,2,128,128]{4,3,2,1,0:T(8,128)(2,1)S(1)} %get-tuple-element.26), channel_id=1, source_target_pairs={{0,3},{1,2},{2,1},{3,0},{4,7},{5,6},{6,5},{7,4},{8,11},{9,10},{10,... | collective-permute-start | bytes 786440 | tf_op jit(solution)/shard_map/ppermute | solution.py:253

commit v3 on v2

v3 whole, which is shorter than its diff:
```python
import functools
import jax
import jax.numpy as jnp
from jax import lax
from jax.experimental import pallas as pl
from jax.experimental.pallas import tpu as pltpu
from jax.sharding import PartitionSpec as P

AXES = ("energy", "momentum")
DIRS = 3
REACH = 2
EVEN = 3 * DIRS * (2 * REACH + 1)
AT_REST = EVEN + 1
ENTRIES = EVEN + 2
ROWS = 32
GRANT = 16 * 2**20


def in_vmem(array):
    return pltpu.with_memory_space_constraint(array, pltpu.VMEM)


def in_hbm(array):
    return pltpu.with_memory_space_constraint(array, pltpu.HBM)


def vmem_specs(count):
    return [pl.BlockSpec(memory_space=pltpu.VMEM)] * count


def routes(n_e, n_k):
    def pairs(step):
        out = []
        for e in range(n_e):
            for k in range(n_k):
                to_e, to_k = step(e, k)
                if 0 <= to_e < n_e:
                    out.append((e * n_k + k, to_e * n_k + to_k % n_k))
        return out

    return {
        "pair": pairs(lambda e, k: (e ^ 1, k)),
        "relay": pairs(lambda e, k: (e + 2 - 4 * (e % 2), k)),
        "cross": pairs(lambda e, k: (e - 1 + 2 * (e % 2), k)),
        "core": pairs(lambda e, k: (e, k ^ 1)),
        "far": pairs(lambda e, k: (e, k - 1 + 2 * (k % 2))),
    }


def prepare_kernel(parity, modes, weight, pattern, dham, left, right, coef, table):
    mode_count = modes.shape[1]
    tile_count = pattern.shape[1]
    for q in range(4):
        for d in range(DIRS):
            for s in range(2 * REACH + 1):
                table[q, d, s] = 0.0
    for m in range(mode_count):
        q = modes[0, m] + 1
        step = modes[1, m]
        for d in range(DIRS):
            table[q, d, REACH - step] = table[q, d, REACH - step] + weight[d, 0, m]
            table[q, d, REACH + step] = table[q, d, REACH + step] + weight[d, 1, m]
    toward = 1 - 2 * parity[1]
    at_rest = 0.0
    for slot, q in enumerate((0, toward, -toward)):
        for d in range(DIRS):
            for s in range(2 * REACH + 1):
                value = table[q + 1, d, s]
                if s == REACH:
                    at_rest = at_rest + jnp.abs(value)
                value = jnp.full((8, 128), value, jnp.float32)
                coef[(slot * DIRS + d) * (2 * REACH + 1) + s] = value.astype(jnp.bfloat16).astype(jnp.float32)
    coef[EVEN] = jnp.full((8, 128), 1 - parity[0], jnp.int32).astype(jnp.float32)
    coef[AT_REST] = jnp.full((8, 128), at_rest, jnp.float32)
    for t in range(tile_count):
        lo, hi = pattern[0, t], pattern[1, t]
        for d in range(DIRS):
            real, imag = dham[d, lo, 0], dham[d, lo, 1]
            left[t, d, :128, :128] = real
            left[t, d, :128, 128:] = -imag
            left[t, d, 128:, :128] = imag
            left[t, d, 128:, 128:] = real
            real, imag = dham[d, hi, 0].T, dham[d, hi, 1].T
            right[t, d, :128, :128] = real
            right[t, d, :128, 128:] = -imag
            right[t, d, 128:, :128] = imag
            right[t, d, 128:, 128:] = real


def prepare(parity, modes, weight, pattern, dham):
    tile_count = pattern.shape[1]
    big = pltpu.VMEM((tile_count, DIRS, 256, 256), jnp.bfloat16)
    return pl.pallas_call(
        prepare_kernel,
        out_shape=(big, big, pltpu.VMEM((ENTRIES, 8, 128), jnp.float32)),
        in_specs=[pl.BlockSpec(memory_space=pltpu.SMEM)] * 4 + vmem_specs(1),
        out_specs=tuple(vmem_specs(3)),
        scratch_shapes=[pltpu.SMEM((4, DIRS, 2 * REACH + 1), jnp.float32)],
        compiler_params=pltpu.CompilerParams(vmem_limit_bytes=GRANT),
        name="prepare",
    )(parity, in_hbm(modes), in_hbm(weight), in_hbm(pattern), in_hbm(dham))


def mix(t, forward, steps, blocks, items, sources, coef, partial, out):
    even = coef[EVEN] > 0.5

    def at(slot, d, s):
        return coef[(slot * DIRS + d) * (2 * REACH + 1) + s + REACH]

    for part in range(2):
        for row in range(0, 128, ROWS):

            def load(ref, j):
                return ref[j, t, part, pl.ds(row, ROWS), :].astype(jnp.float32).reshape(ROWS // 8, 8, 128)

            taken = {block: [load(sources[block], j) for j in range(2)] for block in blocks}
            if forward:
                below = [jnp.where(even, b, a) for a, b in zip(taken[1], taken[2])]
                above = [jnp.where(even, a, b) for a, b in zip(taken[1], taken[2])]
                line = below + taken[0] + above
            for d in range(DIRS):
                for at_item, item in enumerate(items):
                    if forward:
                        slot, i = divmod(item, 2)
                        terms = [(line[2 + i + s], at(slot, d, s)) for s in steps]
                    else:
                        place = item - 2
                        terms = [(taken[m][j], at((0, 2, 1)[m], d, j - place)) for m in blocks for j in range(2) if j - place in steps]
                    here = (t, d, pl.ds(part * 128 + row, ROWS), pl.ds(at_item * 128, 128))
                    acc = terms[0][0] * terms[0][1]
                    if partial is not None:
                        acc = acc + partial[here].reshape(ROWS // 8, 8, 128)
                    for value, factor in terms[1:]:
                        acc = acc + value * factor
                    out[here] = acc.reshape(ROWS, 128).astype(out.dtype)


def multiply(t, first, count, left, right, mixed, product):
    for d in range(DIRS):
        got = jnp.dot(left[first + t, d], mixed[t, d], preferred_element_type=jnp.float32).astype(jnp.bfloat16)
        for item in range(count):
            for part in range(2):
                product[t, pl.ds(item * 128, 128), pl.ds(d * 256 + part * 128, 128)] = got[
                    part * 128 : part * 128 + 128, item * 128 : item * 128 + 128
                ]
    return jnp.dot(product[t], right[first + t].reshape(DIRS * 256, 256), preferred_element_type=jnp.float32)


def both_ways(coef, tiles, run):
    at_rest = jnp.max(coef[AT_REST])

    @pl.when(at_rest == 0.0)
    def _():
        for t in range(tiles):
            run(t, (-2, -1, 1, 2))

    @pl.when(at_rest != 0.0)
    def _():
        @pl.loop(0, tiles)
        def _(t):
            run(t, (-2, -1, 0, 1, 2))


def scratch(tiles, count):
    return [
        pltpu.VMEM((tiles, DIRS, 256, count * 128), jnp.bfloat16),
        pltpu.VMEM((tiles, count * 128, DIRS * 256), jnp.bfloat16),
    ]


SENT_IN, SENT_OUT, KEPT_IN, KEPT_OUT = (2, 3, 4, 5), (0, 1, 4, 5), (0, 1), (2, 3)


def premix_kernel(own, coef, partial):
    both_ways(coef, own.shape[1], lambda t, steps: mix(t, False, steps, (0,), SENT_OUT, (own,), coef, None, partial))


def premix(own, coef):
    tiles = own.shape[1]
    return pl.pallas_call(
        premix_kernel,
        out_shape=pltpu.VMEM((tiles, DIRS, 256, len(SENT_OUT) * 128), jnp.float32),
        in_specs=vmem_specs(2),
        out_specs=vmem_specs(1)[0],
        compiler_params=pltpu.CompilerParams(vmem_limit_bytes=GRANT),
        cost_estimate=pl.CostEstimate(flops=300_000_000 * tiles, bytes_accessed=1_000_000 * tiles, transcendentals=0),
        name="premix",
    )(in_vmem(own), in_vmem(coef))


def sent_kernel(first, forward, *refs):
    sources, (left, right, coef, to_near, to_far, mixed, product) = refs[:3], refs[3:]

    def run(t, steps):
        if forward:
            mix(t, True, steps, (0, 1, 2), SENT_IN, sources, coef, None, mixed)
        else:
            mix(t, False, steps, (1, 2), SENT_OUT, {1: sources[0], 2: sources[1]}, coef, sources[2], mixed)
        term = multiply(t, first, 4, left, right, mixed, product)
        even = jnp.broadcast_to(coef[EVEN][:1] > 0.5, (128, 128))
        for i in range(2):
            for part in range(2):
                one, two = (term[at * 128 : at * 128 + 128, part * 128 : part * 128 + 128] for at in (i, 2 + i))
                if not forward:
                    one, two = jnp.where(even, two, one), jnp.where(even, one, two)
                to_near[i, t, part] = one.astype(to_near.dtype)
                to_far[i, t, part] = two.astype(to_far.dtype)

    both_ways(coef, to_near.shape[1], run)


def sent(first, forward, sources, left, right, coef):
    shape = sources[0].shape
    tiles = shape[1]
    operands = (*sources, left, right, coef)
    return pl.pallas_call(
        functools.partial(sent_kernel, first, forward),
        out_shape=(pltpu.VMEM(shape, jnp.bfloat16), pltpu.VMEM(shape, jnp.bfloat16)),
        in_specs=vmem_specs(len(operands)),
        out_specs=tuple(vmem_specs(2)),
        scratch_shapes=scratch(tiles, 4),
        compiler_params=pltpu.CompilerParams(vmem_limit_bytes=GRANT),
        cost_estimate=pl.CostEstimate(flops=1_200_000_000 * tiles, bytes_accessed=4_000_000 * tiles, transcendentals=0),
        name="sent",
    )(*map(in_vmem, operands))


def kept_kernel(*refs):
    sources_a, sources_b, (left, right, coef, own_a, own_b, mixed_a, product_a, mixed_b, product_b) = refs[:3], refs[3:6], refs[6:]
    half = own_a.shape[1]

    def run(first, forward, items, sources, out, mixed, product, t, steps):
        mix(t, forward, steps, (0, 1, 2), items, sources, coef, None, mixed)
        term = multiply(t, first, 2, left, right, mixed, product)
        for i in range(2):
            for part in range(2):
                out[i, t, part] = term[i * 128 : i * 128 + 128, part * 128 : part * 128 + 128]

    both_ways(coef, half, functools.partial(run, 0, True, KEPT_IN, sources_a, own_a, mixed_a, product_a))
    both_ways(coef, own_b.shape[1], functools.partial(run, half, False, KEPT_OUT, sources_b, own_b, mixed_b, product_b))


def kept(sources_a, sources_b, left, right, coef):
    shape_a, shape_b = sources_a[0].shape, sources_b[0].shape
    operands = (*sources_a, *sources_b, left, right, coef)
    return pl.pallas_call(
        kept_kernel,
        out_shape=(pltpu.VMEM(shape_a, jnp.float32), pltpu.VMEM(shape_b, jnp.float32)),
        in_specs=vmem_specs(len(operands)),
        out_specs=tuple(vmem_specs(2)),
        scratch_shapes=scratch(shape_a[1], 2) + scratch(shape_b[1], 2),
        compiler_params=pltpu.CompilerParams(vmem_limit_bytes=GRANT),
        cost_estimate=pl.CostEstimate(flops=2_400_000_000, bytes_accessed=8_000_000, transcendentals=0),
        name="kept",
    )(*map(in_vmem, operands))


def gather_kernel(near, far, out):
    out[...] = near[...].astype(jnp.float32) + far[...].astype(jnp.float32)


def gather(near, far):
    return pl.pallas_call(
        gather_kernel,
        out_shape=pltpu.VMEM(near.shape, jnp.float32),
        in_specs=vmem_specs(2),
        out_specs=vmem_specs(1)[0],
        compiler_params=pltpu.CompilerParams(vmem_limit_bytes=GRANT),
        cost_estimate=pl.CostEstimate(flops=1000_000_000, bytes_accessed=1000_000, transcendentals=0),
        name="gather",
    )(in_vmem(near), in_vmem(far))


def finish_kernel(own_a, near_a, far_a, own_b, from_b, out, held, sems):
    tiles_a, tiles_b = own_a.shape[1], own_b.shape[1]
    f32 = jnp.float32
    copies = []
    for t in range(tiles_a + tiles_b):
        if t < tiles_a:
            value = own_a[:, t] + near_a[:, t].astype(f32) + far_a[:, t].astype(f32)
        else:
            value = own_b[:, t - tiles_a] + from_b[:, t - tiles_a]
        held[:, t] = value.astype(held.dtype)
        copies.append(pltpu.make_async_copy(held.at[:, t], out.at[0, :, t], sems.at[t]))
        copies[-1].start()
    for copy in copies:
        copy.wait()


def finish(own_a, near_a, far_a, own_b, from_b):
    e, tiles_a = own_a.shape[:2]
    tiles = tiles_a + own_b.shape[1]
    shape = (e, tiles) + own_a.shape[2:]
    return pl.pallas_call(
        finish_kernel,
        out_shape=jax.ShapeDtypeStruct((1,) + shape, jnp.bfloat16),
        in_specs=vmem_specs(5),
        out_specs=pl.BlockSpec(memory_space=pl.ANY),
        scratch_shapes=[pltpu.VMEM(shape, jnp.bfloat16), pltpu.SemaphoreType.DMA((tiles,))],
        compiler_params=pltpu.CompilerParams(vmem_limit_bytes=GRANT),
        name="finish",
    )(*map(in_vmem, (own_a, near_a, far_a, own_b, from_b)))


def local(green_tiles, dham_blocks, phonon_weight, phonon_modes, tile_pattern):
    n_e, n_k = (lax.axis_size(axis) for axis in AXES)
    route = routes(n_e, n_k)

    def send(block, name):
        return lax.ppermute(block, AXES, route[name])

    tiles = green_tiles[0]
    half = tiles.shape[1] // 2
    in_a, in_b = tiles[:, :half], tiles[:, half:]
    parity = jnp.stack([lax.axis_index(axis) % 2 for axis in AXES]).astype(jnp.int32)
    near_a = send(in_a, "pair")
    far_b = send(in_b, "far")
    near_b = send(in_b, "core")
    left, right, coef = prepare(parity, phonon_modes.T, phonon_weight.transpose(1, 2, 0), tile_pattern.T, dham_blocks)
    partial_b = premix(in_b, coef)
    near_a, partial_b = lax.optimization_barrier((near_a, partial_b))
    far_a = send(near_a, "relay")
    far_b, near_a = lax.optimization_barrier((far_b, near_a))
    pair_b, cross_b = sent(half, False, (near_b, far_b, partial_b), left, right, coef)
    pair_b = send(pair_b, "pair")
    cross_b = send(cross_b, "cross")
    core_a, next_a = sent(0, True, (in_a, near_a, far_a), left, right, coef)
    in_b, next_a = lax.optimization_barrier((in_b, next_a))
    core_a = send(core_a, "core")
    next_a = send(next_a, "far")
    own_a, own_b = kept((in_a, near_a, far_a), (in_b, near_b, far_b), left, right, coef)
    own_b, pair_b = lax.optimization_barrier((own_b, pair_b))
    return finish(own_a, core_a, next_a, own_b, gather(pair_b, cross_b))


def solution(mesh):
    placed = (P("momentum", "energy", None, None, None, None), P(), P(), P(), P())
    return jax.shard_map(
        local,
        mesh=mesh,
        in_specs=placed,
        out_specs=P("momentum", "energy", None, None, None, None),
        check_vma=False,
    )
```

time: 31.7 us -> 30.4 us (0.959)
  the two profiles are of different devices: /device:TPU:19 before, /device:TPU:0 now
where the time goes in v3:
time: 30.4 us; the launch traced here: 30.2 us
  starting transfers between devices  10.8 us (36%)
  Pallas kernels  9.08 us (30%)
  waiting for transfers between devices  9.06 us (30%)
  local copies, waits for them, and re-layouts  1.06 us (3%)
    ppermute x8, starting transfers between devices, send(): return lax.ppermute(block, AXES, route[name])  10.8 us
    ppermute x8, waiting for transfers between devices, send(): return lax.ppermute(block, AXES, route[name])  9.06 us
    pallas_call x2, Pallas kernels, sent(): pl.pallas_call(functools.partial(sent_kernel, first, forward), out_shape=...  3.82 us
    pallas_call x1, Pallas kernels, kept(): pl.pallas_call(kept_kernel, out_shape=(pltpu.VMEM(shape_a, jnp.float32),...  2.34 us
    pallas_call x1, Pallas kernels, prepare(): pl.pallas_call(prepare_kernel, out_shape=(big, big, pltpu.VMEM((ENTRIES,...  1.63 us
    slice x1, local copies, waits for them, and re-layouts, local(): in_a, in_b = (tiles[:, :half], tiles[:, half:])  1.06 us
    pallas_call x1, Pallas kernels, finish(): pl.pallas_call(finish_kernel, out_shape=jax.ShapeDtypeStruct((1,) + shape...  0.87 us
  transfers between devices with their start and end apart: 8, of which 4 were waited for; matrix products, arithmetic and copies ran while one was open for 0% of the time, Pallas kernels for 27%

profile of v3, /device:TPU:0, one launch (start us, length us, event | category | flops | bytes accessed | tf_op | source)
XLA Modules:
  0.0 30.2 jit_solution(14105891991537329549)
XLA Ops:
  0.0 1.1 %fusion = (bf16[2,2,2,128,128]{4,3,2,1,0:T(8,128)(2,1)S(1)}, bf16[2,2,2,128,128]{4,3,2,1,0:T(8,128)(2,1)S(1)}) fusion(bf16[2,4,2,128,128]{4,3,2,1,0:T(8,128)(2,1)} %bitcast.6), kind=kLoop, calls=%fused_computation.1 | loop fusion | bytes 1048576 | tf_op jit(solution)/shard_map/slice | solution.py:314
  1.1 3.0 %collective-permute-start.1 = (bf16[2,2,2,128,128]{4,3,2,1,0:T(8,128)(2,1)S(1)}, bf16[2,2,2,128,128]{4,3,2,1,0:T(8,128)(2,1)S(1)}, u32[]{:S(2)}, u32[]{:S(2)}) collective-permute-start(bf16[2,2,2,128,128]{4,3,2,1,0:T(8,128)(2,1)S(1)} %get-tuple-element.40.refs_0_), channel_id=1, source_target_pairs={{0,4},{1,5},{2,6},{3,7},{4,0},{5,1},{6,2},{7,3},{8,12},{9,13},{10,... | collective-permute-start | bytes 786440 | tf_op jit(solution)/shard_map/ppermute | solution.py:310
  4.1 0.7 %collective-permute-start = (bf16[2,2,2,128,128]{4,3,2,1,0:T(8,128)(2,1)S(1)}, bf16[2,2,2,128,128]{4,3,2,1,0:T(8,128)(2,1)S(1)}, u32[]{:S(2)}, u32[]{:S(2)}) collective-permute-start(bf16[2,2,2,128,128]{4,3,2,1,0:T(8,128)(2,1)S(1)} %get-tuple-element.28.own.refs_3_), channel_id=1, source_target_pairs={{0,3},{1,2},{2,1},{3,0},{4,7},{5,6},{6,5},{7,4},{8,11},{9,10},{10,... | collective-permute-start | bytes 786440 | tf_op jit(solution)/shard_map/ppermute | solution.py:310
  4.8 1.0 %collective-permute-start.3 = (bf16[2,2,2,128,128]{4,3,2,1,0:T(8,128)(2,1)S(1)}, bf16[2,2,2,128,128]{4,3,2,1,0:T(8,128)(2,1)S(1)}, u32[]{:S(2)}, u32[]{:S(2)}) collective-permute-start(bf16[2,2,2,128,128]{4,3,2,1,0:T(8,128)(2,1)S(1)} %get-tuple-element.28.own.refs_3_), channel_id=1, source_target_pairs={{0,1},{1,0},{2,3},{3,2},{4,5},{5,4},{6,7},{7,6},{8,9},{9,8},{10,11... | collective-permute-start | bytes 786440 | tf_op jit(solution)/shard_map/ppermute | solution.py:310
  5.7 0.1 pad_add_fusion.parity
  5.8 1.6 %prepare.1 = (bf16[4,3,256,256]{3,2,1,0:T(8,128)(2,1)S(1)}, bf16[4,3,256,256]{3,2,1,0:T(8,128)(2,1)S(1)}, f32[47,8,128]{2,1,0:T(8,128)S(1)}) custom-call(s32[2]{0:T(128)S(1)} %pad_add_fusion.parity, s32[2,6]{1,0:T(2,128)} %bitcast.8, f32[3,2,6]{2,1,0:T(2,128)} %bitcast.7, s32[2,4]{1,0:T(2,128)} %bitcast.9, bf16[3,4,2,128,128]{4,3,2,1,0:T(8,128)(2,1)} %dham.1), custom_call_target="tpu_custom_call" | custom-call | tf_op jit(solution)/shard_map/prepare/pallas_call | solution.py:93
  7.4 0.4 %premix.1.refs_2_ = f32[2,3,256,512]{3,2,1,0:T(8,128)S(1)} custom-call(bf16[2,2,2,128,128]{4,3,2,1,0:T(8,128)(2,1)S(1)} %get-tuple-element.28.own.refs_3_, f32[47,8,128]{2,1,0:T(8,128)S(1)} %get-tuple-element.22.coef.refs_5_.refs_8_), custom_call_target="tpu_custom_call" | custom-call | flops 600000000 | bytes 2000000 | tf_op jit(solution)/shard_map/premix/pallas_call | solution.py:180
  7.8 2.6 %collective-permute-done.1.refs_1_ = bf16[2,2,2,128,128]{4,3,2,1,0:T(8,128)(2,1)S(1)} collective-permute-done((bf16[2,2,2,128,128]{4,3,2,1,0:T(8,128)(2,1)S(1)}, bf16[2,2,2,128,128]{4,3,2,1,0:T(8,128)(2,1)S(1)}, u32[]{:S(2)}, u32[]{:S(2)}) %collective-permute-start.1) | collective-permute-done | bytes 262176 | tf_op jit(solution)/shard_map/ppermute | solution.py:310
  10.4 3.7 %collective-permute-start.2 = (bf16[2,2,2,128,128]{4,3,2,1,0:T(8,128)(2,1)S(1)}, bf16[2,2,2,128,128]{4,3,2,1,0:T(8,128)(2,1)S(1)}, u32[]{:S(2)}, u32[]{:S(2)}) collective-permute-start(bf16[2,2,2,128,128]{4,3,2,1,0:T(8,128)(2,1)S(1)} %collective-permute-done.1.refs_1_), channel_id=1, source_target_pairs={{0,8},{1,9},{2,10},{3,11},{8,16},{9,17},{10,18},{11,19},{12,4},{13... | collective-permute-start | bytes 786440 | tf_op jit(solution)/shard_map/ppermute | solution.py:310
  14.1 0.0 collective-permute-done.refs_5_.refs_1_
  14.1 0.0 collective-permute-done.3.refs_4_.refs_0_
  14.1 1.9 %sent.3 = (bf16[2,2,2,128,128]{4,3,2,1,0:T(8,128)(2,1)S(1)}, bf16[2,2,2,128,128]{4,3,2,1,0:T(8,128)(2,1)S(1)}) custom-call(bf16[2,2,2,128,128]{4,3,2,1,0:T(8,128)(2,1)S(1)} %collective-permute-done.3.refs_4_.refs_0_, bf16[2,2,2,128,128]{4,3,2,1,0:T(8,128)(2,1)S(1)} %collective-permute-done.refs_5_.refs_1_, f32[2,3,256,512]{3,2,1,0:T(8,128)S(1)} %premix.1.refs_2_, ...), custom_call_target="tpu_custom_call" | custom-call | flops 2400000000 | bytes 8000000 | tf_op jit(solution)/shard_map/sent/pallas_call | solution.py:216
  16.0 0.1 collective-permute-start.6
  16.1 0.7 %collective-permute-start.7 = (bf16[2,2,2,128,128]{4,3,2,1,0:T(8,128)(2,1)S(1)}, bf16[2,2,2,128,128]{4,3,2,1,0:T(8,128)(2,1)S(1)}, u32[]{:S(2)}, u32[]{:S(2)}) collective-permute-start(bf16[2,2,2,128,128]{4,3,2,1,0:T(8,128)(2,1)S(1)} %get-tuple-element.38), channel_id=1, source_target_pairs={{4,8},{5,9},{6,10},{7,11},{8,4},{9,5},{10,6},{11,7},{12,16},{13,17... | collective-permute-start | bytes 786440 | tf_op jit(solution)/shard_map/ppermute | solution.py:310
  16.8 2.0 %collective-permute-done.2.refs_2_ = bf16[2,2,2,128,128]{4,3,2,1,0:T(8,128)(2,1)S(1)} collective-permute-done((bf16[2,2,2,128,128]{4,3,2,1,0:T(8,128)(2,1)S(1)}, bf16[2,2,2,128,128]{4,3,2,1,0:T(8,128)(2,1)S(1)}, u32[]{:S(2)}, u32[]{:S(2)}) %collective-permute-start.2) | collective-permute-done | bytes 262176 | tf_op jit(solution)/shard_map/ppermute | solution.py:310
  18.8 1.9 %sent.2 = (bf16[2,2,2,128,128]{4,3,2,1,0:T(8,128)(2,1)S(1)}, bf16[2,2,2,128,128]{4,3,2,1,0:T(8,128)(2,1)S(1)}) custom-call(bf16[2,2,2,128,128]{4,3,2,1,0:T(8,128)(2,1)S(1)} %get-tuple-element.40.refs_0_, bf16[2,2,2,128,128]{4,3,2,1,0:T(8,128)(2,1)S(1)} %collective-permute-done.1.refs_1_, bf16[2,2,2,128,128]{4,3,2,1,0:T(8,128)(2,1)S(1)} %collective-permute-done.2.refs_2_, ...), custom_call_target="tpu_custom_call" | custom-call | flops 2400000000 | bytes 8000000 | tf_op jit(solution)/shard_map/sent/pallas_call | solution.py:216
  20.7 0.1 collective-permute-start.5
  20.8 1.6 %collective-permute-start.4 = (bf16[2,2,2,128,128]{4,3,2,1,0:T(8,128)(2,1)S(1)}, bf16[2,2,2,128,128]{4,3,2,1,0:T(8,128)(2,1)S(1)}, u32[]{:S(2)}, u32[]{:S(2)}) collective-permute-start(bf16[2,2,2,128,128]{4,3,2,1,0:T(8,128)(2,1)S(1)} %get-tuple-element.31), channel_id=1, source_target_pairs={{0,1},{1,0},{2,3},{3,2},{4,5},{5,4},{6,7},{7,6},{8,9},{9,8},{10,11... | collective-permute-start | bytes 786440 | tf_op jit(solution)/shard_map/ppermute | solution.py:310
  22.4 2.3 %kept.1 = (f32[2,2,2,128,128]{4,3,2,1,0:T(8,128)S(1)}, f32[2,2,2,128,128]{4,3,2,1,0:T(8,128)S(1)}) custom-call(bf16[2,2,2,128,128]{4,3,2,1,0:T(8,128)(2,1)S(1)} %get-tuple-element.40.refs_0_, bf16[2,2,2,128,128]{4,3,2,1,0:T(8,128)(2,1)S(1)} %collective-permute-done.1.refs_1_, bf16[2,2,2,128,128]{4,3,2,1,0:T(8,128)(2,1)S(1)} %collective-permute-done.2.refs_2_, ...), custom_call_target="tpu_custom_call" | custom-call | flops 2400000000 | bytes 8000000 | tf_op jit(solution)/shard_map/kept/pallas_call | solution.py:246
  24.8 1.7 %collective-permute-done.6.near = bf16[2,2,2,128,128]{4,3,2,1,0:T(8,128)(2,1)S(1)} collective-permute-done((bf16[2,2,2,128,128]{4,3,2,1,0:T(8,128)(2,1)S(1)}, bf16[2,2,2,128,128]{4,3,2,1,0:T(8,128)(2,1)S(1)}, u32[]{:S(2)}, u32[]{:S(2)}) %collective-permute-start.6) | collective-permute-done | bytes 262176 | tf_op jit(solution)/shard_map/ppermute | solution.py:310
  26.4 0.0 collective-permute-done.7.far
  26.4 0.1 gather.1.from_b
  26.5 2.8 %collective-permute-done.5.far_a = bf16[2,2,2,128,128]{4,3,2,1,0:T(8,128)(2,1)S(1)} collective-permute-done((bf16[2,2,2,128,128]{4,3,2,1,0:T(8,128)(2,1)S(1)}, bf16[2,2,2,128,128]{4,3,2,1,0:T(8,128)(2,1)S(1)}, u32[]{:S(2)}, u32[]{:S(2)}) %collective-permute-start.5) | collective-permute-done | bytes 262176 | tf_op jit(solution)/shard_map/ppermute | solution.py:310
  29.3 0.0 collective-permute-done.4.near_a
  29.3 0.9 %finish.1 = bf16[1,2,4,2,128,128]{5,4,3,2,1,0:T(8,128)(2,1)} custom-call(f32[2,2,2,128,128]{4,3,2,1,0:T(8,128)S(1)} %get-tuple-element.30.own_a, bf16[2,2,2,128,128]{4,3,2,1,0:T(8,128)(2,1)S(1)} %collective-permute-done.4.near_a, bf16[2,2,2,128,128]{4,3,2,1,0:T(8,128)(2,1)S(1)} %collective-permute-done.5.far_a, ...), custom_call_target="tpu_custom_call" | custom-call | tf_op jit(solution)/shard_map/finish/pallas_call | solution.py:294
Async XLA Ops:
  1.1 9.3 %collective-permute-start.1 = (bf16[2,2,2,128,128]{4,3,2,1,0:T(8,128)(2,1)S(1)}, bf16[2,2,2,128,128]{4,3,2,1,0:T(8,128)(2,1)S(1)}, u32[]{:S(2)}, u32[]{:S(2)}) collective-permute-start(bf16[2,2,2,128,128]{4,3,2,1,0:T(8,128)(2,1)S(1)} %get-tuple-element.40.refs_0_), channel_id=1, source_target_pairs={{0,4},{1,5},{2,6},{3,7},{4,0},{5,1},{6,2},{7,3},{8,12},{9,13},{10,... | collective-permute-start | bytes 786440 | tf_op jit(solution)/shard_map/ppermute | solution.py:310
  4.1 10.1 %collective-permute-start = (bf16[2,2,2,128,128]{4,3,2,1,0:T(8,128)(2,1)S(1)}, bf16[2,2,2,128,128]{4,3,2,1,0:T(8,128)(2,1)S(1)}, u32[]{:S(2)}, u32[]{:S(2)}) collective-permute-start(bf16[2,2,2,128,128]{4,3,2,1,0:T(8,128)(2,1)S(1)} %get-tuple-element.28.own.refs_3_), channel_id=1, source_target_pairs={{0,3},{1,2},{2,1},{3,0},{4,7},{5,6},{6,5},{7,4},{8,11},{9,10},{10,... | collective-permute-start | bytes 786440 | tf_op jit(solution)/shard_map/ppermute | solution.py:310
  4.8 9.4 %collective-permute-start.3 = (bf16[2,2,2,128,128]{4,3,2,1,0:T(8,128)(2,1)S(1)}, bf16[2,2,2,128,128]{4,3,2,1,0:T(8,128)(2,1)S(1)}, u32[]{:S(2)}, u32[]{:S(2)}) collective-permute-start(bf16[2,2,2,128,128]{4,3,2,1,0:T(8,128)(2,1)S(1)} %get-tuple-element.28.own.refs_3_), channel_id=1, source_target_pairs={{0,1},{1,0},{2,3},{3,2},{4,5},{5,4},{6,7},{7,6},{8,9},{9,8},{10,11... | collective-permute-start | bytes 786440 | tf_op jit(solution)/shard_map/ppermute | solution.py:310
  10.4 8.4 %collective-permute-start.2 = (bf16[2,2,2,128,128]{4,3,2,1,0:T(8,128)(2,1)S(1)}, bf16[2,2,2,128,128]{4,3,2,1,0:T(8,128)(2,1)S(1)}, u32[]{:S(2)}, u32[]{:S(2)}) collective-permute-start(bf16[2,2,2,128,128]{4,3,2,1,0:T(8,128)(2,1)S(1)} %collective-permute-done.1.refs_1_), channel_id=1, source_target_pairs={{0,8},{1,9},{2,10},{3,11},{8,16},{9,17},{10,18},{11,19},{12,4},{13... | collective-permute-start | bytes 786440 | tf_op jit(solution)/shard_map/ppermute | solution.py:310
  16.0 10.4 %collective-permute-start.6 = (bf16[2,2,2,128,128]{4,3,2,1,0:T(8,128)(2,1)S(1)}, bf16[2,2,2,128,128]{4,3,2,1,0:T(8,128)(2,1)S(1)}, u32[]{:S(2)}, u32[]{:S(2)}) collective-permute-start(bf16[2,2,2,128,128]{4,3,2,1,0:T(8,128)(2,1)S(1)} %get-tuple-element.35), channel_id=1, source_target_pairs={{0,4},{1,5},{2,6},{3,7},{4,0},{5,1},{6,2},{7,3},{8,12},{9,13},{10,... | collective-permute-start | bytes 786440 | tf_op jit(solution)/shard_map/ppermute | solution.py:310
  16.1 10.3 %collective-permute-start.7 = (bf16[2,2,2,128,128]{4,3,2,1,0:T(8,128)(2,1)S(1)}, bf16[2,2,2,128,128]{4,3,2,1,0:T(8,128)(2,1)S(1)}, u32[]{:S(2)}, u32[]{:S(2)}) collective-permute-start(bf16[2,2,2,128,128]{4,3,2,1,0:T(8,128)(2,1)S(1)} %get-tuple-element.38), channel_id=1, source_target_pairs={{4,8},{5,9},{6,10},{7,11},{8,4},{9,5},{10,6},{11,7},{12,16},{13,17... | collective-permute-start | bytes 786440 | tf_op jit(solution)/shard_map/ppermute | solution.py:310
  20.7 8.6 %collective-permute-start.5 = (bf16[2,2,2,128,128]{4,3,2,1,0:T(8,128)(2,1)S(1)}, bf16[2,2,2,128,128]{4,3,2,1,0:T(8,128)(2,1)S(1)}, u32[]{:S(2)}, u32[]{:S(2)}) collective-permute-start(bf16[2,2,2,128,128]{4,3,2,1,0:T(8,128)(2,1)S(1)} %get-tuple-element.32), channel_id=1, source_target_pairs={{0,3},{1,2},{2,1},{3,0},{4,7},{5,6},{6,5},{7,4},{8,11},{9,10},{10,... | collective-permute-start | bytes 786440 | tf_op jit(solution)/shard_map/ppermute | solution.py:310
  20.8 8.5 %collective-permute-start.4 = (bf16[2,2,2,128,128]{4,3,2,1,0:T(8,128)(2,1)S(1)}, bf16[2,2,2,128,128]{4,3,2,1,0:T(8,128)(2,1)S(1)}, u32[]{:S(2)}, u32[]{:S(2)}) collective-permute-start(bf16[2,2,2,128,128]{4,3,2,1,0:T(8,128)(2,1)S(1)} %get-tuple-element.31), channel_id=1, source_target_pairs={{0,1},{1,0},{2,3},{3,2},{4,5},{5,4},{6,7},{7,6},{8,9},{9,8},{10,11... | collective-permute-start | bytes 786440 | tf_op jit(solution)/shard_map/ppermute | solution.py:310

commit v4 on v3

--- a/solution.py
+++ b/solution.py
@@ -1,4 +1,5 @@
 import functools
+import itertools
 import jax
 import jax.numpy as jnp
 from jax import lax
@@ -11,7 +12,8 @@
 REACH = 2
 EVEN = 3 * DIRS * (2 * REACH + 1)
 AT_REST = EVEN + 1
-ENTRIES = EVEN + 2
+INNER = EVEN + 2
+ENTRIES = EVEN + 3
 ROWS = 32
 GRANT = 16 * 2**20
 
@@ -30,18 +32,15 @@
 
 def routes(n_e, n_k):
     def pairs(step):
-        out = []
-        for e in range(n_e):
-            for k in range(n_k):
-                to_e, to_k = step(e, k)
-                if 0 <= to_e < n_e:
-                    out.append((e * n_k + k, to_e * n_k + to_k % n_k))
-        return out
+        return [(e * n_k + k, to_e * n_k + to_k % n_k) for e in range(n_e) for k in range(n_k) for to_e, to_k in [step(e, k)]]
+
+    def inside(e, otherwise):
+        return e if 0 <= e < n_e else otherwise
 
     return {
         "pair": pairs(lambda e, k: (e ^ 1, k)),
-        "relay": pairs(lambda e, k: (e + 2 - 4 * (e % 2), k)),
-        "cross": pairs(lambda e, k: (e - 1 + 2 * (e % 2), k)),
+        "relay": pairs(lambda e, k: (inside(e + 2 - 4 * (e % 2), e ^ 1), k)),
+        "cross": pairs(lambda e, k: (inside(e - 1 + 2 * (e % 2), e), k ^ (0 <= e - 1 + 2 * (e % 2) < n_e) ^ 1)),
         "core": pairs(lambda e, k: (e, k ^ 1)),
         "far": pairs(lambda e, k: (e, k - 1 + 2 * (k % 2))),
     }
@@ -71,6 +70,7 @@
                 value = jnp.full((8, 128), value, jnp.float32)
                 coef[(slot * DIRS + d) * (2 * REACH + 1) + s] = value.astype(jnp.bfloat16).astype(jnp.float32)
     coef[EVEN] = jnp.full((8, 128), 1 - parity[0], jnp.int32).astype(jnp.float32)
+    coef[INNER] = jnp.full((8, 128), parity[2], jnp.int32).astype(jnp.float32)
     coef[AT_REST] = jnp.full((8, 128), at_rest, jnp.float32)
     for t in range(tile_count):
         lo, hi = pattern[0, t], pattern[1, t]
@@ -102,7 +102,7 @@
 
 
 def mix(t, forward, steps, blocks, items, sources, coef, partial, out):
-    even = coef[EVEN] > 0.5
+    even, inner = coef[EVEN] > 0.5, coef[INNER] > 0.5
 
     def at(slot, d, s):
         return coef[(slot * DIRS + d) * (2 * REACH + 1) + s + REACH]
@@ -115,6 +115,7 @@
 
             taken = {block: [load(sources[block], j) for j in range(2)] for block in blocks}
             if forward:
+                taken[2] = [jnp.where(inner, value, 0.0) for value in taken[2]]
                 below = [jnp.where(even, b, a) for a, b in zip(taken[1], taken[2])]
                 above = [jnp.where(even, a, b) for a, b in zip(taken[1], taken[2])]
                 line = below + taken[0] + above
@@ -255,23 +256,25 @@
     )(*map(in_vmem, operands))
 
 
-def gather_kernel(near, far, out):
-    out[...] = near[...].astype(jnp.float32) + far[...].astype(jnp.float32)
-
-
-def gather(near, far):
+def gather_kernel(own, far, coef, out):
+    inner = jnp.broadcast_to(coef[INNER][:1] > 0.5, out.shape[-2:])
+    for index in itertools.product(*map(range, out.shape[:-2])):
+        out[index] = own[index] + jnp.where(inner, far[index].astype(jnp.float32), 0.0)
+
+
+def gather(own, far, coef):
     return pl.pallas_call(
         gather_kernel,
-        out_shape=pltpu.VMEM(near.shape, jnp.float32),
-        in_specs=vmem_specs(2),
+        out_shape=pltpu.VMEM(own.shape, jnp.float32),
+        in_specs=vmem_specs(3),
         out_specs=vmem_specs(1)[0],
         compiler_params=pltpu.CompilerParams(vmem_limit_bytes=GRANT),
         cost_estimate=pl.CostEstimate(flops=1000_000_000, bytes_accessed=1000_000, transcendentals=0),
         name="gather",
-    )(in_vmem(near), in_vmem(far))
-
-
-def finish_kernel(own_a, near_a, far_a, own_b, from_b, out, held, sems):
+    )(in_vmem(own), in_vmem(far), in_vmem(coef))
+
+
+def finish_kernel(far_a, near_a, near_b, own_a, own_b, out, held, sems):
     tiles_a, tiles_b = own_a.shape[1], own_b.shape[1]
     f32 = jnp.float32
     copies = []
@@ -279,7 +282,7 @@
         if t < tiles_a:
             value = own_a[:, t] + near_a[:, t].astype(f32) + far_a[:, t].astype(f32)
         else:
-            value = own_b[:, t - tiles_a] + from_b[:, t - tiles_a]
+            value = own_b[:, t - tiles_a] + near_b[:, t - tiles_a].astype(f32)
         held[:, t] = value.astype(held.dtype)
         copies.append(pltpu.make_async_copy(held.at[:, t], out.at[0, :, t], sems.at[t]))
         copies[-1].start()
@@ -287,7 +290,7 @@
         copy.wait()
 
 
-def finish(own_a, near_a, far_a, own_b, from_b):
+def finish(far_a, near_a, near_b, own_a, own_b):
     e, tiles_a = own_a.shape[:2]
     tiles = tiles_a + own_b.shape[1]
     shape = (e, tiles) + own_a.shape[2:]
@@ -299,7 +302,7 @@
         scratch_shapes=[pltpu.VMEM(shape, jnp.bfloat16), pltpu.SemaphoreType.DMA((tiles,))],
         compiler_params=pltpu.CompilerParams(vmem_limit_bytes=GRANT),
         name="finish",
-    )(*map(in_vmem, (own_a, near_a, far_a, own_b, from_b)))
+    )(*map(in_vmem, (far_a, near_a, near_b, own_a, own_b)))
 
 
 def local(green_tiles, dham_blocks, phonon_weight, phonon_modes, tile_pattern):
@@ -312,7 +315,9 @@
     tiles = green_tiles[0]
     half = tiles.shape[1] // 2
     in_a, in_b = tiles[:, :half], tiles[:, half:]
-    parity = jnp.stack([lax.axis_index(axis) % 2 for axis in AXES]).astype(jnp.int32)
+    e, k = (lax.axis_index(axis) for axis in AXES)
+    inner = (e > 0) & (e < n_e - 1)
+    parity = jnp.stack([e % 2, k % 2, inner]).astype(jnp.int32)
     near_a = send(in_a, "pair")
     far_b = send(in_b, "far")
     near_b = send(in_b, "core")
@@ -322,15 +327,15 @@
     far_a = send(near_a, "relay")
     far_b, near_a = lax.optimization_barrier((far_b, near_a))
     pair_b, cross_b = sent(half, False, (near_b, far_b, partial_b), left, right, coef)
-    pair_b = send(pair_b, "pair")
     cross_b = send(cross_b, "cross")
     core_a, next_a = sent(0, True, (in_a, near_a, far_a), left, right, coef)
-    in_b, next_a = lax.optimization_barrier((in_b, next_a))
+    in_b, next_a, pair_b = lax.optimization_barrier((in_b, next_a, pair_b))
+    next_a = send(next_a, "far")
     core_a = send(core_a, "core")
-    next_a = send(next_a, "far")
+    pair_b = send(pair_b, "pair")
     own_a, own_b = kept((in_a, near_a, far_a), (in_b, near_b, far_b), left, right, coef)
-    own_b, pair_b = lax.optimization_barrier((own_b, pair_b))
-    return finish(own_a, core_a, next_a, own_b, gather(pair_b, cross_b))
+    own_b, cross_b = lax.optimization_barrier((own_b, cross_b))
+    return finish(next_a, core_a, pair_b, own_a, gather(own_b, cross_b, coef))
 
 
 def solution(mesh):

time: 30.4 us -> 29.7 us (0.977)
  starting transfers between devices: 10.8 us -> 9.48 us
  waiting for transfers between devices: 9.06 us -> 10 us
  Pallas kernels: 9.08 us -> 8.77 us
    ppermute x8, starting transfers between devices: 10.8 us -> 9.48 us  [send(): return lax.ppermute(block, AXES, route[name])]
    ppermute x8, waiting for transfers between devices: 9.06 us -> 10 us  [send(): return lax.ppermute(block, AXES, route[name])]
  transfers between devices with their start and end apart: 8 -> 8, of which waited for: 4 -> 5; matrix products, arithmetic and copies ran while one was open for 0% -> 0% of each run, Pallas kernels for 27% -> 27%
where the time goes in v4:
time: 29.7 us; the launch traced here: 29.5 us
  waiting for transfers between devices  10 us (34%)
  starting transfers between devices  9.48 us (32%)
  Pallas kernels  8.77 us (30%)
  local copies, waits for them, and re-layouts  1.06 us (4%)
    ppermute x8, waiting for transfers between devices, send(): return lax.ppermute(block, AXES, route[name])  10 us
    ppermute x8, starting transfers between devices, send(): return lax.ppermute(block, AXES, route[name])  9.48 us
    pallas_call x2, Pallas kernels, sent(): pl.pallas_call(functools.partial(sent_kernel, first, forward), out_shape=...  3.59 us
    pallas_call x1, Pallas kernels, kept(): pl.pallas_call(kept_kernel, out_shape=(pltpu.VMEM(shape_a, jnp.float32),...  2.26 us
    pallas_call x1, Pallas kernels, prepare(): pl.pallas_call(prepare_kernel, out_shape=(big, big, pltpu.VMEM((ENTRIES,...  1.63 us
    slice x1, local copies, waits for them, and re-layouts, local(): in_a, in_b = (tiles[:, :half], tiles[:, half:])  1.06 us
    pallas_call x1, Pallas kernels, finish(): pl.pallas_call(finish_kernel, out_shape=jax.ShapeDtypeStruct((1,) + shape...  0.86 us
  transfers between devices with their start and end apart: 8, of which 5 were waited for; matrix products, arithmetic and copies ran while one was open for 0% of the time, Pallas kernels for 27%

profile of v4, /device:TPU:0, one launch (start us, length us, event | category | flops | bytes accessed | tf_op | source)
XLA Modules:
  0.0 29.5 jit_solution(3702813629307312401)
XLA Ops:
  0.0 1.1 %fusion = (bf16[2,2,2,128,128]{4,3,2,1,0:T(8,128)(2,1)S(1)}, bf16[2,2,2,128,128]{4,3,2,1,0:T(8,128)(2,1)S(1)}) fusion(bf16[2,4,2,128,128]{4,3,2,1,0:T(8,128)(2,1)} %bitcast.7), kind=kLoop, calls=%fused_computation.1 | loop fusion | bytes 1048576 | tf_op jit(solution)/shard_map/slice | solution.py:317
  1.1 3.0 %collective-permute-start.1 = (bf16[2,2,2,128,128]{4,3,2,1,0:T(8,128)(2,1)S(1)}, bf16[2,2,2,128,128]{4,3,2,1,0:T(8,128)(2,1)S(1)}, u32[]{:S(2)}, u32[]{:S(2)}) collective-permute-start(bf16[2,2,2,128,128]{4,3,2,1,0:T(8,128)(2,1)S(1)} %get-tuple-element.41.refs_0_), channel_id=1, source_target_pairs={{0,4},{1,5},{2,6},{3,7},{4,0},{5,1},{6,2},{7,3},{8,12},{9,13},{10,... | collective-permute-start | bytes 786440 | tf_op jit(solution)/shard_map/ppermute | solution.py:313
  4.1 0.7 %collective-permute-start = (bf16[2,2,2,128,128]{4,3,2,1,0:T(8,128)(2,1)S(1)}, bf16[2,2,2,128,128]{4,3,2,1,0:T(8,128)(2,1)S(1)}, u32[]{:S(2)}, u32[]{:S(2)}) collective-permute-start(bf16[2,2,2,128,128]{4,3,2,1,0:T(8,128)(2,1)S(1)} %get-tuple-element.35.own.refs_3_), channel_id=1, source_target_pairs={{0,3},{1,2},{2,1},{3,0},{4,7},{5,6},{6,5},{7,4},{8,11},{9,10},{10,... | collective-permute-start | bytes 786440 | tf_op jit(solution)/shard_map/ppermute | solution.py:313
  4.8 1.0 %collective-permute-start.3 = (bf16[2,2,2,128,128]{4,3,2,1,0:T(8,128)(2,1)S(1)}, bf16[2,2,2,128,128]{4,3,2,1,0:T(8,128)(2,1)S(1)}, u32[]{:S(2)}, u32[]{:S(2)}) collective-permute-start(bf16[2,2,2,128,128]{4,3,2,1,0:T(8,128)(2,1)S(1)} %get-tuple-element.35.own.refs_3_), channel_id=1, source_target_pairs={{0,1},{1,0},{2,3},{3,2},{4,5},{5,4},{6,7},{7,6},{8,9},{9,8},{10,11... | collective-permute-start | bytes 786440 | tf_op jit(solution)/shard_map/ppermute | solution.py:313
  5.7 0.1 pad_add_fusion.parity
  5.8 1.6 %prepare.1 = (bf16[4,3,256,256]{3,2,1,0:T(8,128)(2,1)S(1)}, bf16[4,3,256,256]{3,2,1,0:T(8,128)(2,1)S(1)}, f32[48,8,128]{2,1,0:T(8,128)S(1)}) custom-call(s32[3]{0:T(128)S(1)} %pad_add_fusion.parity, s32[2,6]{1,0:T(2,128)} %bitcast.9, f32[3,2,6]{2,1,0:T(2,128)} %bitcast.8, s32[2,4]{1,0:T(2,128)} %bitcast.10, bf16[3,4,2,128,128]{4,3,2,1,0:T(8,128)(2,1)} %dham.1), custom_call_target="tpu_custom_call" | custom-call | tf_op jit(solution)/shard_map/prepare/pallas_call | solution.py:93
  7.4 0.4 %premix.1.refs_2_ = f32[2,3,256,512]{3,2,1,0:T(8,128)S(1)} custom-call(bf16[2,2,2,128,128]{4,3,2,1,0:T(8,128)(2,1)S(1)} %get-tuple-element.35.own.refs_3_, f32[48,8,128]{2,1,0:T(8,128)S(1)} %get-tuple-element.23.coef.refs_5_.refs_8_), custom_call_target="tpu_custom_call" | custom-call | flops 600000000 | bytes 2000000 | tf_op jit(solution)/shard_map/premix/pallas_call | solution.py:181
  7.8 2.6 %collective-permute-done.1.refs_1_ = bf16[2,2,2,128,128]{4,3,2,1,0:T(8,128)(2,1)S(1)} collective-permute-done((bf16[2,2,2,128,128]{4,3,2,1,0:T(8,128)(2,1)S(1)}, bf16[2,2,2,128,128]{4,3,2,1,0:T(8,128)(2,1)S(1)}, u32[]{:S(2)}, u32[]{:S(2)}) %collective-permute-start.1) | collective-permute-done | bytes 262176 | tf_op jit(solution)/shard_map/ppermute | solution.py:313
  10.4 1.8 %collective-permute-start.2 = (bf16[2,2,2,128,128]{4,3,2,1,0:T(8,128)(2,1)S(1)}, bf16[2,2,2,128,128]{4,3,2,1,0:T(8,128)(2,1)S(1)}, u32[]{:S(2)}, u32[]{:S(2)}) collective-permute-start(bf16[2,2,2,128,128]{4,3,2,1,0:T(8,128)(2,1)S(1)} %collective-permute-done.1.refs_1_), channel_id=1, source_target_pairs={{0,8},{1,9},{2,10},{3,11},{4,0},{5,1},{6,2},{7,3},{8,16},{9,17},{1... | collective-permute-start | bytes 786440 | tf_op jit(solution)/shard_map/ppermute | solution.py:313
  12.2 0.4 %collective-permute-done.refs_1_.refs_5_ = bf16[2,2,2,128,128]{4,3,2,1,0:T(8,128)(2,1)S(1)} collective-permute-done((bf16[2,2,2,128,128]{4,3,2,1,0:T(8,128)(2,1)S(1)}, bf16[2,2,2,128,128]{4,3,2,1,0:T(8,128)(2,1)S(1)}, u32[]{:S(2)}, u32[]{:S(2)}) %collective-permute-start) | collective-permute-done | bytes 262176 | tf_op jit(solution)/shard_map/ppermute | solution.py:313
  12.6 0.0 collective-permute-done.3.refs_0_.refs_4_
  12.6 1.7 %sent.3 = (bf16[2,2,2,128,128]{4,3,2,1,0:T(8,128)(2,1)S(1)}, bf16[2,2,2,128,128]{4,3,2,1,0:T(8,128)(2,1)S(1)}) custom-call(bf16[2,2,2,128,128]{4,3,2,1,0:T(8,128)(2,1)S(1)} %collective-permute-done.3.refs_0_.refs_4_, bf16[2,2,2,128,128]{4,3,2,1,0:T(8,128)(2,1)S(1)} %collective-permute-done.refs_1_.refs_5_, f32[2,3,256,512]{3,2,1,0:T(8,128)S(1)} %premix.1.refs_2_, ...), custom_call_target="tpu_custom_call" | custom-call | flops 2400000000 | bytes 8000000 | tf_op jit(solution)/shard_map/sent/pallas_call | solution.py:217
  14.3 0.2 collective-permute-start.7
  14.5 3.4 %collective-permute-done.2.refs_2_ = bf16[2,2,2,128,128]{4,3,2,1,0:T(8,128)(2,1)S(1)} collective-permute-done((bf16[2,2,2,128,128]{4,3,2,1,0:T(8,128)(2,1)S(1)}, bf16[2,2,2,128,128]{4,3,2,1,0:T(8,128)(2,1)S(1)}, u32[]{:S(2)}, u32[]{:S(2)}) %collective-permute-start.2) | collective-permute-done | bytes 262176 | tf_op jit(solution)/shard_map/ppermute | solution.py:313
  17.9 1.9 %sent.2 = (bf16[2,2,2,128,128]{4,3,2,1,0:T(8,128)(2,1)S(1)}, bf16[2,2,2,128,128]{4,3,2,1,0:T(8,128)(2,1)S(1)}) custom-call(bf16[2,2,2,128,128]{4,3,2,1,0:T(8,128)(2,1)S(1)} %get-tuple-element.41.refs_0_, bf16[2,2,2,128,128]{4,3,2,1,0:T(8,128)(2,1)S(1)} %collective-permute-done.1.refs_1_, bf16[2,2,2,128,128]{4,3,2,1,0:T(8,128)(2,1)S(1)} %collective-permute-done.2.refs_2_, ...), custom_call_target="tpu_custom_call" | custom-call | flops 2400000000 | bytes 8000000 | tf_op jit(solution)/shard_map/sent/pallas_call | solution.py:217
  19.8 0.1 collective-permute-start.4
  19.8 1.5 %collective-permute-start.6 = (bf16[2,2,2,128,128]{4,3,2,1,0:T(8,128)(2,1)S(1)}, bf16[2,2,2,128,128]{4,3,2,1,0:T(8,128)(2,1)S(1)}, u32[]{:S(2)}, u32[]{:S(2)}) collective-permute-start(bf16[2,2,2,128,128]{4,3,2,1,0:T(8,128)(2,1)S(1)} %get-tuple-element.34), channel_id=1, source_target_pairs={{0,4},{1,5},{2,6},{3,7},{4,0},{5,1},{6,2},{7,3},{8,12},{9,13},{10,... | collective-permute-start | bytes 786440 | tf_op jit(solution)/shard_map/ppermute | solution.py:313
  21.3 1.3 %collective-permute-start.5 = (bf16[2,2,2,128,128]{4,3,2,1,0:T(8,128)(2,1)S(1)}, bf16[2,2,2,128,128]{4,3,2,1,0:T(8,128)(2,1)S(1)}, u32[]{:S(2)}, u32[]{:S(2)}) collective-permute-start(bf16[2,2,2,128,128]{4,3,2,1,0:T(8,128)(2,1)S(1)} %get-tuple-element.33), channel_id=1, source_target_pairs={{0,1},{1,0},{2,3},{3,2},{4,5},{5,4},{6,7},{7,6},{8,9},{9,8},{10,11... | collective-permute-start | bytes 786440 | tf_op jit(solution)/shard_map/ppermute | solution.py:313
  22.6 2.3 %kept.1 = (f32[2,2,2,128,128]{4,3,2,1,0:T(8,128)S(1)}, f32[2,2,2,128,128]{4,3,2,1,0:T(8,128)S(1)}) custom-call(bf16[2,2,2,128,128]{4,3,2,1,0:T(8,128)(2,1)S(1)} %get-tuple-element.41.refs_0_, bf16[2,2,2,128,128]{4,3,2,1,0:T(8,128)(2,1)S(1)} %collective-permute-done.1.refs_1_, bf16[2,2,2,128,128]{4,3,2,1,0:T(8,128)(2,1)S(1)} %collective-permute-done.2.refs_2_, ...), custom_call_target="tpu_custom_call" | custom-call | flops 2400000000 | bytes 8000000 | tf_op jit(solution)/shard_map/kept/pallas_call | solution.py:247
  24.9 0.0 collective-permute-done.7.far
  24.9 0.1 gather.1.own_b
  24.9 3.5 %collective-permute-done.4.far_a = bf16[2,2,2,128,128]{4,3,2,1,0:T(8,128)(2,1)S(1)} collective-permute-done((bf16[2,2,2,128,128]{4,3,2,1,0:T(8,128)(2,1)S(1)}, bf16[2,2,2,128,128]{4,3,2,1,0:T(8,128)(2,1)S(1)}, u32[]{:S(2)}, u32[]{:S(2)}) %collective-permute-start.4) | collective-permute-done | bytes 262176 | tf_op jit(solution)/shard_map/ppermute | solution.py:313
  28.4 0.2 collective-permute-done.6.near_b
  28.6 0.0 collective-permute-done.5.near_a
  28.6 0.9 %finish.1 = bf16[1,2,4,2,128,128]{5,4,3,2,1,0:T(8,128)(2,1)} custom-call(bf16[2,2,2,128,128]{4,3,2,1,0:T(8,128)(2,1)S(1)} %collective-permute-done.4.far_a, bf16[2,2,2,128,128]{4,3,2,1,0:T(8,128)(2,1)S(1)} %collective-permute-done.5.near_a, bf16[2,2,2,128,128]{4,3,2,1,0:T(8,128)(2,1)S(1)} %collective-permute-done.6.near_b, ...), custom_call_target="tpu_custom_call" | custom-call | tf_op jit(solution)/shard_map/finish/pallas_call | solution.py:297
Async XLA Ops:
  1.1 9.3 %collective-permute-start.1 = (bf16[2,2,2,128,128]{4,3,2,1,0:T(8,128)(2,1)S(1)}, bf16[2,2,2,128,128]{4,3,2,1,0:T(8,128)(2,1)S(1)}, u32[]{:S(2)}, u32[]{:S(2)}) collective-permute-start(bf16[2,2,2,128,128]{4,3,2,1,0:T(8,128)(2,1)S(1)} %get-tuple-element.41.refs_0_), channel_id=1, source_target_pairs={{0,4},{1,5},{2,6},{3,7},{4,0},{5,1},{6,2},{7,3},{8,12},{9,13},{10,... | collective-permute-start | bytes 786440 | tf_op jit(solution)/shard_map/ppermute | solution.py:313
  4.1 8.5 %collective-permute-start = (bf16[2,2,2,128,128]{4,3,2,1,0:T(8,128)(2,1)S(1)}, bf16[2,2,2,128,128]{4,3,2,1,0:T(8,128)(2,1)S(1)}, u32[]{:S(2)}, u32[]{:S(2)}) collective-permute-start(bf16[2,2,2,128,128]{4,3,2,1,0:T(8,128)(2,1)S(1)} %get-tuple-element.35.own.refs_3_), channel_id=1, source_target_pairs={{0,3},{1,2},{2,1},{3,0},{4,7},{5,6},{6,5},{7,4},{8,11},{9,10},{10,... | collective-permute-start | bytes 786440 | tf_op jit(solution)/shard_map/ppermute | solution.py:313
  4.8 7.9 %collective-permute-start.3 = (bf16[2,2,2,128,128]{4,3,2,1,0:T(8,128)(2,1)S(1)}, bf16[2,2,2,128,128]{4,3,2,1,0:T(8,128)(2,1)S(1)}, u32[]{:S(2)}, u32[]{:S(2)}) collective-permute-start(bf16[2,2,2,128,128]{4,3,2,1,0:T(8,128)(2,1)S(1)} %get-tuple-element.35.own.refs_3_), channel_id=1, source_target_pairs={{0,1},{1,0},{2,3},{3,2},{4,5},{5,4},{6,7},{7,6},{8,9},{9,8},{10,11... | collective-permute-start | bytes 786440 | tf_op jit(solution)/shard_map/ppermute | solution.py:313
  10.4 7.5 %collective-permute-start.2 = (bf16[2,2,2,128,128]{4,3,2,1,0:T(8,128)(2,1)S(1)}, bf16[2,2,2,128,128]{4,3,2,1,0:T(8,128)(2,1)S(1)}, u32[]{:S(2)}, u32[]{:S(2)}) collective-permute-start(bf16[2,2,2,128,128]{4,3,2,1,0:T(8,128)(2,1)S(1)} %collective-permute-done.1.refs_1_), channel_id=1, source_target_pairs={{0,8},{1,9},{2,10},{3,11},{4,0},{5,1},{6,2},{7,3},{8,16},{9,17},{1... | collective-permute-start | bytes 786440 | tf_op jit(solution)/shard_map/ppermute | solution.py:313
  14.3 10.5 %collective-permute-start.7 = (bf16[2,2,2,128,128]{4,3,2,1,0:T(8,128)(2,1)S(1)}, bf16[2,2,2,128,128]{4,3,2,1,0:T(8,128)(2,1)S(1)}, u32[]{:S(2)}, u32[]{:S(2)}) collective-permute-start(bf16[2,2,2,128,128]{4,3,2,1,0:T(8,128)(2,1)S(1)} %get-tuple-element.38), channel_id=1, source_target_pairs={{0,1},{1,0},{2,3},{3,2},{4,8},{5,9},{6,10},{7,11},{8,4},{9,5},{10,... | collective-permute-start | bytes 786440 | tf_op jit(solution)/shard_map/ppermute | solution.py:313
  19.8 8.7 %collective-permute-start.4 = (bf16[2,2,2,128,128]{4,3,2,1,0:T(8,128)(2,1)S(1)}, bf16[2,2,2,128,128]{4,3,2,1,0:T(8,128)(2,1)S(1)}, u32[]{:S(2)}, u32[]{:S(2)}) collective-permute-start(bf16[2,2,2,128,128]{4,3,2,1,0:T(8,128)(2,1)S(1)} %get-tuple-element.32), channel_id=1, source_target_pairs={{0,3},{1,2},{2,1},{3,0},{4,7},{5,6},{6,5},{7,4},{8,11},{9,10},{10,... | collective-permute-start | bytes 786440 | tf_op jit(solution)/shard_map/ppermute | solution.py:313
  19.8 8.8 %collective-permute-start.6 = (bf16[2,2,2,128,128]{4,3,2,1,0:T(8,128)(2,1)S(1)}, bf16[2,2,2,128,128]{4,3,2,1,0:T(8,128)(2,1)S(1)}, u32[]{:S(2)}, u32[]{:S(2)}) collective-permute-start(bf16[2,2,2,128,128]{4,3,2,1,0:T(8,128)(2,1)S(1)} %get-tuple-element.34), channel_id=1, source_target_pairs={{0,4},{1,5},{2,6},{3,7},{4,0},{5,1},{6,2},{7,3},{8,12},{9,13},{10,... | collective-permute-start | bytes 786440 | tf_op jit(solution)/shard_map/ppermute | solution.py:313
  21.3 7.3 %collective-permute-start.5 = (bf16[2,2,2,128,128]{4,3,2,1,0:T(8,128)(2,1)S(1)}, bf16[2,2,2,128,128]{4,3,2,1,0:T(8,128)(2,1)S(1)}, u32[]{:S(2)}, u32[]{:S(2)}) collective-permute-start(bf16[2,2,2,128,128]{4,3,2,1,0:T(8,128)(2,1)S(1)} %get-tuple-element.33), channel_id=1, source_target_pairs={{0,1},{1,0},{2,3},{3,2},{4,5},{5,4},{6,7},{7,6},{8,9},{9,8},{10,11... | collective-permute-start | bytes 786440 | tf_op jit(solution)/shard_map/ppermute | solution.py:313

commit v5 on v4

--- a/solution.py
+++ b/solution.py
@@ -110,8 +110,9 @@
     for part in range(2):
         for row in range(0, 128, ROWS):
 
-            def load(ref, j):
-                return ref[j, t, part, pl.ds(row, ROWS), :].astype(jnp.float32).reshape(ROWS // 8, 8, 128)
+            def load(source, j):
+                ref, tile = (source[t], 0) if isinstance(source, list) else (source, t)
+                return ref[j, tile, part, pl.ds(row, ROWS), :].astype(jnp.float32).reshape(ROWS // 8, 8, 128)
 
             taken = {block: [load(sources[block], j) for j in range(2)] for block in blocks}
             if forward:
@@ -157,9 +158,13 @@
 
     @pl.when(at_rest != 0.0)
     def _():
-        @pl.loop(0, tiles)
-        def _(t):
+        for t in range(tiles):
             run(t, (-2, -1, 0, 1, 2))
+
+
+def flat(*sources):
+    arrays, places = jax.tree.flatten(sources)
+    return arrays, functools.partial(jax.tree.unflatten, places), len(arrays)
 
 
 def scratch(tiles, count):
@@ -172,25 +177,26 @@
 SENT_IN, SENT_OUT, KEPT_IN, KEPT_OUT = (2, 3, 4, 5), (0, 1, 4, 5), (0, 1), (2, 3)
 
 
-def premix_kernel(own, coef, partial):
-    both_ways(coef, own.shape[1], lambda t, steps: mix(t, False, steps, (0,), SENT_OUT, (own,), coef, None, partial))
-
-
-def premix(own, coef):
-    tiles = own.shape[1]
-    return pl.pallas_call(
-        premix_kernel,
+def premix_kernel(places, count, *refs):
+    (own,), (coef, partial) = places(refs[:count]), refs[count:]
+    both_ways(coef, partial.shape[0], lambda t, steps: mix(t, False, steps, (0,), SENT_OUT, (own,), coef, None, partial))
+
+
+def premix(tiles, own, coef):
+    arrays, places, count = flat(own)
+    return pl.pallas_call(
+        functools.partial(premix_kernel, places, count),
         out_shape=pltpu.VMEM((tiles, DIRS, 256, len(SENT_OUT) * 128), jnp.float32),
-        in_specs=vmem_specs(2),
+        in_specs=vmem_specs(count + 1),
         out_specs=vmem_specs(1)[0],
         compiler_params=pltpu.CompilerParams(vmem_limit_bytes=GRANT),
         cost_estimate=pl.CostEstimate(flops=300_000_000 * tiles, bytes_accessed=1_000_000 * tiles, transcendentals=0),
         name="premix",
-    )(in_vmem(own), in_vmem(coef))
-
-
-def sent_kernel(first, forward, *refs):
-    sources, (left, right, coef, to_near, to_far, mixed, product) = refs[:3], refs[3:]
+    )(*map(in_vmem, (*arrays, coef)))
+
+
+def sent_kernel(first, forward, places, count, *refs):
+    sources, (left, right, coef, to_near, to_far, mixed, product) = places(refs[:count]), refs[count:]
 
     def run(t, steps):
         if forward:
@@ -210,24 +216,24 @@
     both_ways(coef, to_near.shape[1], run)
 
 
-def sent(first, forward, sources, left, right, coef):
-    shape = sources[0].shape
+def sent(first, forward, shape, sources, left, right, coef):
     tiles = shape[1]
-    operands = (*sources, left, right, coef)
-    return pl.pallas_call(
-        functools.partial(sent_kernel, first, forward),
+    arrays, places, count = flat(*sources)
+    return pl.pallas_call(
+        functools.partial(sent_kernel, first, forward, places, count),
         out_shape=(pltpu.VMEM(shape, jnp.bfloat16), pltpu.VMEM(shape, jnp.bfloat16)),
-        in_specs=vmem_specs(len(operands)),
+        in_specs=vmem_specs(count + 3),
         out_specs=tuple(vmem_specs(2)),
         scratch_shapes=scratch(tiles, 4),
         compiler_params=pltpu.CompilerParams(vmem_limit_bytes=GRANT),
         cost_estimate=pl.CostEstimate(flops=1_200_000_000 * tiles, bytes_accessed=4_000_000 * tiles, transcendentals=0),
         name="sent",
-    )(*map(in_vmem, operands))
-
-
-def kept_kernel(*refs):
-    sources_a, sources_b, (left, right, coef, own_a, own_b, mixed_a, product_a, mixed_b, product_b) = refs[:3], refs[3:6], refs[6:]
+    )(*map(in_vmem, (*arrays, left, right, coef)))
+
+
+def kept_kernel(places, count, *refs):
+    (sources_a, sources_b), rest = places(refs[:count]), refs[count:]
+    left, right, coef, own_a, own_b, mixed_a, product_a, mixed_b, product_b = rest
     half = own_a.shape[1]
 
     def run(first, forward, items, sources, out, mixed, product, t, steps):
@@ -241,40 +247,39 @@
     both_ways(coef, own_b.shape[1], functools.partial(run, half, False, KEPT_OUT, sources_b, own_b, mixed_b, product_b))
 
 
-def kept(sources_a, sources_b, left, right, coef):
-    shape_a, shape_b = sources_a[0].shape, sources_b[0].shape
-    operands = (*sources_a, *sources_b, left, right, coef)
-    return pl.pallas_call(
-        kept_kernel,
+def kept(shape_a, shape_b, sources_a, sources_b, left, right, coef):
+    arrays, places, count = flat(sources_a, sources_b)
+    return pl.pallas_call(
+        functools.partial(kept_kernel, places, count),
         out_shape=(pltpu.VMEM(shape_a, jnp.float32), pltpu.VMEM(shape_b, jnp.float32)),
-        in_specs=vmem_specs(len(operands)),
+        in_specs=vmem_specs(count + 3),
         out_specs=tuple(vmem_specs(2)),
         scratch_shapes=scratch(shape_a[1], 2) + scratch(shape_b[1], 2),
         compiler_params=pltpu.CompilerParams(vmem_limit_bytes=GRANT),
         cost_estimate=pl.CostEstimate(flops=2_400_000_000, bytes_accessed=8_000_000, transcendentals=0),
         name="kept",
-    )(*map(in_vmem, operands))
-
-
-def gather_kernel(own, far, coef, out):
+    )(*map(in_vmem, (*arrays, left, right, coef)))
+
+
+def gather_kernel(far, near, coef, out):
     inner = jnp.broadcast_to(coef[INNER][:1] > 0.5, out.shape[-2:])
     for index in itertools.product(*map(range, out.shape[:-2])):
-        out[index] = own[index] + jnp.where(inner, far[index].astype(jnp.float32), 0.0)
-
-
-def gather(own, far, coef):
+        out[index] = near[index].astype(jnp.float32) + jnp.where(inner, far[index].astype(jnp.float32), 0.0)
+
+
+def gather(near, far, coef):
     return pl.pallas_call(
         gather_kernel,
-        out_shape=pltpu.VMEM(own.shape, jnp.float32),
+        out_shape=pltpu.VMEM(near.shape, jnp.float32),
         in_specs=vmem_specs(3),
         out_specs=vmem_specs(1)[0],
         compiler_params=pltpu.CompilerParams(vmem_limit_bytes=GRANT),
         cost_estimate=pl.CostEstimate(flops=1000_000_000, bytes_accessed=1000_000, transcendentals=0),
         name="gather",
-    )(in_vmem(own), in_vmem(far), in_vmem(coef))
-
-
-def finish_kernel(far_a, near_a, near_b, own_a, own_b, out, held, sems):
+    )(in_vmem(far), in_vmem(near), in_vmem(coef))
+
+
+def finish_kernel(own_a, near_a, far_a, own_b, from_b, out, held, sems):
     tiles_a, tiles_b = own_a.shape[1], own_b.shape[1]
     f32 = jnp.float32
     copies = []
@@ -282,7 +287,7 @@
         if t < tiles_a:
             value = own_a[:, t] + near_a[:, t].astype(f32) + far_a[:, t].astype(f32)
         else:
-            value = own_b[:, t - tiles_a] + near_b[:, t - tiles_a].astype(f32)
+            value = own_b[:, t - tiles_a] + from_b[:, t - tiles_a]
         held[:, t] = value.astype(held.dtype)
         copies.append(pltpu.make_async_copy(held.at[:, t], out.at[0, :, t], sems.at[t]))
         copies[-1].start()
@@ -290,7 +295,7 @@
         copy.wait()
 
 
-def finish(far_a, near_a, near_b, own_a, own_b):
+def finish(own_a, near_a, far_a, own_b, from_b):
     e, tiles_a = own_a.shape[:2]
     tiles = tiles_a + own_b.shape[1]
     shape = (e, tiles) + own_a.shape[2:]
@@ -302,7 +307,31 @@
         scratch_shapes=[pltpu.VMEM(shape, jnp.bfloat16), pltpu.SemaphoreType.DMA((tiles,))],
         compiler_params=pltpu.CompilerParams(vmem_limit_bytes=GRANT),
         name="finish",
-    )(*map(in_vmem, (far_a, near_a, near_b, own_a, own_b)))
+    )(*map(in_vmem, (own_a, near_a, far_a, own_b, from_b)))
+
+
+def split_kernel(source, *refs):
+    outs, sems = refs[:-1], refs[-1]
+    copies, tile = [], 0
+    for at, out in enumerate(outs):
+        copies.append(pltpu.make_async_copy(source.at[0, :, pl.ds(tile, out.shape[1])], out, sems.at[at]))
+        copies[-1].start()
+        tile += out.shape[1]
+    for copy in copies:
+        copy.wait()
+
+
+def split(tiles, counts):
+    _, e, _, *rest = tiles.shape
+    return pl.pallas_call(
+        split_kernel,
+        out_shape=tuple(pltpu.VMEM((e, count, *rest), tiles.dtype) for count in counts),
+        in_specs=[pl.BlockSpec(memory_space=pltpu.HBM)],
+        out_specs=tuple(vmem_specs(len(counts))),
+        scratch_shapes=[pltpu.SemaphoreType.DMA((len(counts),))],
+        compiler_params=pltpu.CompilerParams(vmem_limit_bytes=GRANT),
+        name="split",
+    )(in_hbm(tiles))
 
 
 def local(green_tiles, dham_blocks, phonon_weight, phonon_modes, tile_pattern):
@@ -314,28 +343,30 @@
 
     tiles = green_tiles[0]
     half = tiles.shape[1] // 2
-    in_a, in_b = tiles[:, :half], tiles[:, half:]
+    e_count, tile_count, *rest = tiles.shape
+    shape_a, shape_b = (e_count, half, *rest), (e_count, tile_count - half, *rest)
+    *in_a, in_b = split(green_tiles, [1] * half + [tile_count - half])
     e, k = (lax.axis_index(axis) for axis in AXES)
     inner = (e > 0) & (e < n_e - 1)
     parity = jnp.stack([e % 2, k % 2, inner]).astype(jnp.int32)
-    near_a = send(in_a, "pair")
+    near_a = [send(block, "pair") for block in in_a]
     far_b = send(in_b, "far")
     near_b = send(in_b, "core")
     left, right, coef = prepare(parity, phonon_modes.T, phonon_weight.transpose(1, 2, 0), tile_pattern.T, dham_blocks)
-    partial_b = premix(in_b, coef)
-    near_a, partial_b = lax.optimization_barrier((near_a, partial_b))
-    far_a = send(near_a, "relay")
+    partial_b = premix(shape_b[1], in_b, coef)
+    near_a[0], partial_b = lax.optimization_barrier((near_a[0], partial_b))
+    far_a = [send(block, "relay") for block in near_a]
     far_b, near_a = lax.optimization_barrier((far_b, near_a))
-    pair_b, cross_b = sent(half, False, (near_b, far_b, partial_b), left, right, coef)
+    pair_b, cross_b = sent(half, False, shape_b, (near_b, far_b, partial_b), left, right, coef)
     cross_b = send(cross_b, "cross")
-    core_a, next_a = sent(0, True, (in_a, near_a, far_a), left, right, coef)
-    in_b, next_a, pair_b = lax.optimization_barrier((in_b, next_a, pair_b))
+    pair_b = send(pair_b, "pair")
+    core_a, next_a = sent(0, True, shape_a, (in_a, near_a, far_a), left, right, coef)
+    in_b, next_a = lax.optimization_barrier((in_b, next_a))
+    core_a = send(core_a, "core")
     next_a = send(next_a, "far")
-    core_a = send(core_a, "core")
-    pair_b = send(pair_b, "pair")
-    own_a, own_b = kept((in_a, near_a, far_a), (in_b, near_b, far_b), left, right, coef)
-    own_b, cross_b = lax.optimization_barrier((own_b, cross_b))
-    return finish(next_a, core_a, pair_b, own_a, gather(own_b, cross_b, coef))
+    own_a, own_b = kept(shape_a, shape_b, (in_a, near_a, far_a), (in_b, near_b, far_b), left, right, coef)
+    own_b, pair_b = lax.optimization_barrier((own_b, pair_b))
+    return finish(own_a, core_a, next_a, own_b, gather(pair_b, cross_b, coef))
 
 
 def solution(mesh):

time: 29.7 us -> 29.5 us (level)
  Pallas kernels: 8.77 us -> 9.89 us
  local copies, waits for them, and re-layouts: 1.06 us -> 0 us
  starting transfers between devices: 9.48 us -> 8.99 us
  waiting for transfers between devices: 10 us -> 10.3 us
    pallas_call x5 -> x6, Pallas kernels: 6.28 us -> 7.4 us  [the longest x2 3.59 us: sent(): pl.pallas_call(functools.partial(sent_kernel, first, forward, places, cou...]
    slice x1 -> x0, local copies, waits for them, and re-layouts: 1.06 us -> none  [local(): in_a, in_b = (tiles[:, :half], tiles[:, half:])]
    ppermute x8 -> x10, starting transfers between devices: 9.48 us -> 8.99 us  [send(): return lax.ppermute(block, AXES, route[name])]
    ppermute x8 -> x10, waiting for transfers between devices: 10 us -> 10.3 us  [send(): return lax.ppermute(block, AXES, route[name])]
  transfers between devices with their start and end apart: 8 -> 10, of which waited for: 5 -> 5; matrix products, arithmetic and copies ran while one was open for 0% -> 0% of each run, Pallas kernels for 27% -> 27%
where the time goes in v5:
time: 29.5 us; the launch traced here: 29.4 us
  waiting for transfers between devices  10.3 us (35%)
  Pallas kernels  9.89 us (34%)
  starting transfers between devices  8.99 us (30%)
    ppermute x10, waiting for transfers between devices, send(): return lax.ppermute(block, AXES, route[name])  10.3 us
    ppermute x10, starting transfers between devices, send(): return lax.ppermute(block, AXES, route[name])  8.99 us
    pallas_call x2, Pallas kernels, sent(): pl.pallas_call(functools.partial(sent_kernel, first, forward, places, cou...  3.59 us
    pallas_call x1, Pallas kernels, kept(): pl.pallas_call(functools.partial(kept_kernel, places, count), out_shape=(...  2.26 us
    pallas_call x1, Pallas kernels, prepare(): pl.pallas_call(prepare_kernel, out_shape=(big, big, pltpu.VMEM((ENTRIES,...  1.63 us
    pallas_call x1, Pallas kernels, split(): pl.pallas_call(split_kernel, out_shape=tuple((pltpu.VMEM((e, count, *rest...  1.11 us
    pallas_call x1, Pallas kernels, finish(): pl.pallas_call(finish_kernel, out_shape=jax.ShapeDtypeStruct((1,) + shape...  0.86 us
  transfers between devices with their start and end apart: 10, of which 5 were waited for; matrix products, arithmetic and copies ran while one was open for 0% of the time, Pallas kernels for 27%

profile of v5, /device:TPU:0, one launch (start us, length us, event | category | flops | bytes accessed | tf_op | source)
XLA Modules:
  0.0 29.4 jit_solution(6186973554256733241)
XLA Ops:
  0.0 1.1 %split.1 = (bf16[2,1,2,128,128]{4,3,2,1,0:T(8,128)(2,1)S(1)}, bf16[2,1,2,128,128]{4,3,2,1,0:T(8,128)(2,1)S(1)}, bf16[2,2,2,128,128]{4,3,2,1,0:T(8,128)(2,1)S(1)}) custom-call(bf16[1,2,4,2,128,128]{5,4,3,2,1,0:T(8,128)(2,1)} %source.1), custom_call_target="tpu_custom_call" | custom-call | tf_op jit(solution)/shard_map/split/pallas_call | solution.py:326
  1.1 2.5 %collective-permute-start = (bf16[2,2,2,128,128]{4,3,2,1,0:T(8,128)(2,1)S(1)}, bf16[2,2,2,128,128]{4,3,2,1,0:T(8,128)(2,1)S(1)}, u32[]{:S(2)}, u32[]{:S(2)}) collective-permute-start(bf16[2,2,2,128,128]{4,3,2,1,0:T(8,128)(2,1)S(1)} %get-tuple-element.36.refs_0_.refs_6_), channel_id=1, source_target_pairs={{0,3},{1,2},{2,1},{3,0},{4,7},{5,6},{6,5},{7,4},{8,11},{9,10},{10,... | collective-permute-start | bytes 786440 | tf_op jit(solution)/shard_map/ppermute | solution.py:342
  3.6 0.7 %collective-permute-start.5 = (bf16[2,2,2,128,128]{4,3,2,1,0:T(8,128)(2,1)S(1)}, bf16[2,2,2,128,128]{4,3,2,1,0:T(8,128)(2,1)S(1)}, u32[]{:S(2)}, u32[]{:S(2)}) collective-permute-start(bf16[2,2,2,128,128]{4,3,2,1,0:T(8,128)(2,1)S(1)} %get-tuple-element.36.refs_0_.refs_6_), channel_id=1, source_target_pairs={{0,1},{1,0},{2,3},{3,2},{4,5},{5,4},{6,7},{7,6},{8,9},{9,8},{10,11... | collective-permute-start | bytes 786440 | tf_op jit(solution)/shard_map/ppermute | solution.py:342
  4.3 1.5 %collective-permute-start.1 = (bf16[2,1,2,128,128]{4,3,2,1,0:T(8,128)(2,1)S(1)}, bf16[2,1,2,128,128]{4,3,2,1,0:T(8,128)(2,1)S(1)}, u32[]{:S(2)}, u32[]{:S(2)}) collective-permute-start(bf16[2,1,2,128,128]{4,3,2,1,0:T(8,128)(2,1)S(1)} %get-tuple-element.26.refs_0_), channel_id=1, source_target_pairs={{0,4},{1,5},{2,6},{3,7},{4,0},{5,1},{6,2},{7,3},{8,12},{9,13},{10,... | collective-permute-start | bytes 393224 | tf_op jit(solution)/shard_map/ppermute | solution.py:342
  5.8 0.5 %collective-permute-start.2 = (bf16[2,1,2,128,128]{4,3,2,1,0:T(8,128)(2,1)S(1)}, bf16[2,1,2,128,128]{4,3,2,1,0:T(8,128)(2,1)S(1)}, u32[]{:S(2)}, u32[]{:S(2)}) collective-permute-start(bf16[2,1,2,128,128]{4,3,2,1,0:T(8,128)(2,1)S(1)} %get-tuple-element.27.refs_1_), channel_id=1, source_target_pairs={{0,4},{1,5},{2,6},{3,7},{4,0},{5,1},{6,2},{7,3},{8,12},{9,13},{10,... | collective-permute-start | bytes 393224 | tf_op jit(solution)/shard_map/ppermute | solution.py:342
  6.3 0.1 pad_add_fusion.parity
  6.4 1.6 %prepare.1 = (bf16[4,3,256,256]{3,2,1,0:T(8,128)(2,1)S(1)}, bf16[4,3,256,256]{3,2,1,0:T(8,128)(2,1)S(1)}, f32[48,8,128]{2,1,0:T(8,128)S(1)}) custom-call(s32[3]{0:T(128)S(1)} %pad_add_fusion.parity, s32[2,6]{1,0:T(2,128)} %bitcast.7, f32[3,2,6]{2,1,0:T(2,128)} %bitcast.6, s32[2,4]{1,0:T(2,128)} %bitcast.8, bf16[3,4,2,128,128]{4,3,2,1,0:T(8,128)(2,1)} %dham.1), custom_call_target="tpu_custom_call" | custom-call | tf_op jit(solution)/shard_map/prepare/pallas_call | solution.py:93
  8.0 0.4 %premix.1.refs_2_ = f32[2,3,256,512]{3,2,1,0:T(8,128)S(1)} custom-call(bf16[2,2,2,128,128]{4,3,2,1,0:T(8,128)(2,1)S(1)} %get-tuple-element.36.refs_0_.refs_6_, f32[48,8,128]{2,1,0:T(8,128)S(1)} %get-tuple-element.29.refs_1_.refs_8_.refs_11_.refs_5_.coef), custom_call_target="tpu_custom_call" | custom-call | flops 600000000 | bytes 2000000 | tf_op jit(solution)/shard_map/premix/pallas_call | solution.py:187
  8.4 2.2 %collective-permute-done.1.refs_2_ = bf16[2,1,2,128,128]{4,3,2,1,0:T(8,128)(2,1)S(1)} collective-permute-done((bf16[2,1,2,128,128]{4,3,2,1,0:T(8,128)(2,1)S(1)}, bf16[2,1,2,128,128]{4,3,2,1,0:T(8,128)(2,1)S(1)}, u32[]{:S(2)}, u32[]{:S(2)}) %collective-permute-start.1) | collective-permute-done | bytes 131104 | tf_op jit(solution)/shard_map/ppermute | solution.py:342
  10.6 1.6 %collective-permute-start.3 = (bf16[2,1,2,128,128]{4,3,2,1,0:T(8,128)(2,1)S(1)}, bf16[2,1,2,128,128]{4,3,2,1,0:T(8,128)(2,1)S(1)}, u32[]{:S(2)}, u32[]{:S(2)}) collective-permute-start(bf16[2,1,2,128,128]{4,3,2,1,0:T(8,128)(2,1)S(1)} %collective-permute-done.1.refs_2_), channel_id=1, source_target_pairs={{0,8},{1,9},{2,10},{3,11},{4,0},{5,1},{6,2},{7,3},{8,16},{9,17},{1... | collective-permute-start | bytes 393224 | tf_op jit(solution)/shard_map/ppermute | solution.py:342
  12.2 1.2 %collective-permute-done.2.refs_3_ = bf16[2,1,2,128,128]{4,3,2,1,0:T(8,128)(2,1)S(1)} collective-permute-done((bf16[2,1,2,128,128]{4,3,2,1,0:T(8,128)(2,1)S(1)}, bf16[2,1,2,128,128]{4,3,2,1,0:T(8,128)(2,1)S(1)}, u32[]{:S(2)}, u32[]{:S(2)}) %collective-permute-start.2) | collective-permute-done | bytes 131104 | tf_op jit(solution)/shard_map/ppermute | solution.py:342
  13.4 0.6 %collective-permute-start.4 = (bf16[2,1,2,128,128]{4,3,2,1,0:T(8,128)(2,1)S(1)}, bf16[2,1,2,128,128]{4,3,2,1,0:T(8,128)(2,1)S(1)}, u32[]{:S(2)}, u32[]{:S(2)}) collective-permute-start(bf16[2,1,2,128,128]{4,3,2,1,0:T(8,128)(2,1)S(1)} %collective-permute-done.2.refs_3_), channel_id=1, source_target_pairs={{0,8},{1,9},{2,10},{3,11},{4,0},{5,1},{6,2},{7,3},{8,16},{9,17},{1... | collective-permute-start | bytes 393224 | tf_op jit(solution)/shard_map/ppermute | solution.py:342
  14.1 0.0 collective-permute-done.refs_8_.refs_1_
  14.1 0.0 collective-permute-done.5.refs_7_.refs_0_
  14.1 1.7 %sent.3 = (bf16[2,2,2,128,128]{4,3,2,1,0:T(8,128)(2,1)S(1)}, bf16[2,2,2,128,128]{4,3,2,1,0:T(8,128)(2,1)S(1)}) custom-call(bf16[2,2,2,128,128]{4,3,2,1,0:T(8,128)(2,1)S(1)} %collective-permute-done.5.refs_7_.refs_0_, bf16[2,2,2,128,128]{4,3,2,1,0:T(8,128)(2,1)S(1)} %collective-permute-done.refs_8_.refs_1_, f32[2,3,256,512]{3,2,1,0:T(8,128)S(1)} %premix.1.refs_2_, ...), custom_call_target="tpu_custom_call" | custom-call | flops 2400000000 | bytes 8000000 | tf_op jit(solution)/shard_map/sent/pallas_call | solution.py:222
  15.8 1.5 %collective-permute-start.8 = (bf16[2,2,2,128,128]{4,3,2,1,0:T(8,128)(2,1)S(1)}, bf16[2,2,2,128,128]{4,3,2,1,0:T(8,128)(2,1)S(1)}, u32[]{:S(2)}, u32[]{:S(2)}) collective-permute-start(bf16[2,2,2,128,128]{4,3,2,1,0:T(8,128)(2,1)S(1)} %get-tuple-element.43), channel_id=1, source_target_pairs={{0,4},{1,5},{2,6},{3,7},{4,0},{5,1},{6,2},{7,3},{8,12},{9,13},{10,... | collective-permute-start | bytes 786440 | tf_op jit(solution)/shard_map/ppermute | solution.py:342
  17.3 0.0 collective-permute-start.9
  17.3 0.0 collective-permute-done.3.refs_4_
  17.3 2.2 %collective-permute-done.4.refs_5_ = bf16[2,1,2,128,128]{4,3,2,1,0:T(8,128)(2,1)S(1)} collective-permute-done((bf16[2,1,2,128,128]{4,3,2,1,0:T(8,128)(2,1)S(1)}, bf16[2,1,2,128,128]{4,3,2,1,0:T(8,128)(2,1)S(1)}, u32[]{:S(2)}, u32[]{:S(2)}) %collective-permute-start.4) | collective-permute-done | bytes 131104 | tf_op jit(solution)/shard_map/ppermute | solution.py:342
  19.5 1.9 %sent.2 = (bf16[2,2,2,128,128]{4,3,2,1,0:T(8,128)(2,1)S(1)}, bf16[2,2,2,128,128]{4,3,2,1,0:T(8,128)(2,1)S(1)}) custom-call(bf16[2,1,2,128,128]{4,3,2,1,0:T(8,128)(2,1)S(1)} %get-tuple-element.26.refs_0_, bf16[2,1,2,128,128]{4,3,2,1,0:T(8,128)(2,1)S(1)} %get-tuple-element.27.refs_1_, bf16[2,1,2,128,128]{4,3,2,1,0:T(8,128)(2,1)S(1)} %collective-permute-done.1.refs_2_, ...), custom_call_target="tpu_custom_call" | custom-call | flops 2400000000 | bytes 8000000 | tf_op jit(solution)/shard_map/sent/pallas_call | solution.py:222
  21.4 0.1 collective-permute-start.7
  21.5 0.1 collective-permute-start.6
  21.5 2.3 %kept.1 = (f32[2,2,2,128,128]{4,3,2,1,0:T(8,128)S(1)}, f32[2,2,2,128,128]{4,3,2,1,0:T(8,128)S(1)}) custom-call(bf16[2,1,2,128,128]{4,3,2,1,0:T(8,128)(2,1)S(1)} %get-tuple-element.26.refs_0_, bf16[2,1,2,128,128]{4,3,2,1,0:T(8,128)(2,1)S(1)} %get-tuple-element.27.refs_1_, bf16[2,1,2,128,128]{4,3,2,1,0:T(8,128)(2,1)S(1)} %collective-permute-done.1.refs_2_, ...), custom_call_target="tpu_custom_call" | custom-call | flops 2400000000 | bytes 8000000 | tf_op jit(solution)/shard_map/kept/pallas_call | solution.py:252
  23.8 2.7 %collective-permute-done.8.near = bf16[2,2,2,128,128]{4,3,2,1,0:T(8,128)(2,1)S(1)} collective-permute-done((bf16[2,2,2,128,128]{4,3,2,1,0:T(8,128)(2,1)S(1)}, bf16[2,2,2,128,128]{4,3,2,1,0:T(8,128)(2,1)S(1)}, u32[]{:S(2)}, u32[]{:S(2)}) %collective-permute-start.8) | collective-permute-done | bytes 262176 | tf_op jit(solution)/shard_map/ppermute | solution.py:342
  26.5 0.0 collective-permute-done.9.far
  26.5 0.1 gather.1.from_b
  26.6 1.9 %collective-permute-done.7.far_a = bf16[2,2,2,128,128]{4,3,2,1,0:T(8,128)(2,1)S(1)} collective-permute-done((bf16[2,2,2,128,128]{4,3,2,1,0:T(8,128)(2,1)S(1)}, bf16[2,2,2,128,128]{4,3,2,1,0:T(8,128)(2,1)S(1)}, u32[]{:S(2)}, u32[]{:S(2)}) %collective-permute-start.7) | collective-permute-done | bytes 262176 | tf_op jit(solution)/shard_map/ppermute | solution.py:342
  28.5 0.0 collective-permute-done.6.near_a
  28.5 0.9 %finish.1 = bf16[1,2,4,2,128,128]{5,4,3,2,1,0:T(8,128)(2,1)} custom-call(f32[2,2,2,128,128]{4,3,2,1,0:T(8,128)S(1)} %get-tuple-element.38.own_a, bf16[2,2,2,128,128]{4,3,2,1,0:T(8,128)(2,1)S(1)} %collective-permute-done.6.near_a, bf16[2,2,2,128,128]{4,3,2,1,0:T(8,128)(2,1)S(1)} %collective-permute-done.7.far_a, ...), custom_call_target="tpu_custom_call" | custom-call | tf_op jit(solution)/shard_map/finish/pallas_call | solution.py:302
Async XLA Ops:
  1.1 12.9 %collective-permute-start = (bf16[2,2,2,128,128]{4,3,2,1,0:T(8,128)(2,1)S(1)}, bf16[2,2,2,128,128]{4,3,2,1,0:T(8,128)(2,1)S(1)}, u32[]{:S(2)}, u32[]{:S(2)}) collective-permute-start(bf16[2,2,2,128,128]{4,3,2,1,0:T(8,128)(2,1)S(1)} %get-tuple-element.36.refs_0_.refs_6_), channel_id=1, source_target_pairs={{0,3},{1,2},{2,1},{3,0},{4,7},{5,6},{6,5},{7,4},{8,11},{9,10},{10,... | collective-permute-start | bytes 786440 | tf_op jit(solution)/shard_map/ppermute | solution.py:342
  3.6 10.5 %collective-permute-start.5 = (bf16[2,2,2,128,128]{4,3,2,1,0:T(8,128)(2,1)S(1)}, bf16[2,2,2,128,128]{4,3,2,1,0:T(8,128)(2,1)S(1)}, u32[]{:S(2)}, u32[]{:S(2)}) collective-permute-start(bf16[2,2,2,128,128]{4,3,2,1,0:T(8,128)(2,1)S(1)} %get-tuple-element.36.refs_0_.refs_6_), channel_id=1, source_target_pairs={{0,1},{1,0},{2,3},{3,2},{4,5},{5,4},{6,7},{7,6},{8,9},{9,8},{10,11... | collective-permute-start | bytes 786440 | tf_op jit(solution)/shard_map/ppermute | solution.py:342
  4.3 6.4 %collective-permute-start.1 = (bf16[2,1,2,128,128]{4,3,2,1,0:T(8,128)(2,1)S(1)}, bf16[2,1,2,128,128]{4,3,2,1,0:T(8,128)(2,1)S(1)}, u32[]{:S(2)}, u32[]{:S(2)}) collective-permute-start(bf16[2,1,2,128,128]{4,3,2,1,0:T(8,128)(2,1)S(1)} %get-tuple-element.26.refs_0_), channel_id=1, source_target_pairs={{0,4},{1,5},{2,6},{3,7},{4,0},{5,1},{6,2},{7,3},{8,12},{9,13},{10,... | collective-permute-start | bytes 393224 | tf_op jit(solution)/shard_map/ppermute | solution.py:342
  5.8 7.7 %collective-permute-start.2 = (bf16[2,1,2,128,128]{4,3,2,1,0:T(8,128)(2,1)S(1)}, bf16[2,1,2,128,128]{4,3,2,1,0:T(8,128)(2,1)S(1)}, u32[]{:S(2)}, u32[]{:S(2)}) collective-permute-start(bf16[2,1,2,128,128]{4,3,2,1,0:T(8,128)(2,1)S(1)} %get-tuple-element.27.refs_1_), channel_id=1, source_target_pairs={{0,4},{1,5},{2,6},{3,7},{4,0},{5,1},{6,2},{7,3},{8,12},{9,13},{10,... | collective-permute-start | bytes 393224 | tf_op jit(solution)/shard_map/ppermute | solution.py:342
  10.6 6.6 %collective-permute-start.3 = (bf16[2,1,2,128,128]{4,3,2,1,0:T(8,128)(2,1)S(1)}, bf16[2,1,2,128,128]{4,3,2,1,0:T(8,128)(2,1)S(1)}, u32[]{:S(2)}, u32[]{:S(2)}) collective-permute-start(bf16[2,1,2,128,128]{4,3,2,1,0:T(8,128)(2,1)S(1)} %collective-permute-done.1.refs_2_), channel_id=1, source_target_pairs={{0,8},{1,9},{2,10},{3,11},{4,0},{5,1},{6,2},{7,3},{8,16},{9,17},{1... | collective-permute-start | bytes 393224 | tf_op jit(solution)/shard_map/ppermute | solution.py:342
  13.4 6.1 %collective-permute-start.4 = (bf16[2,1,2,128,128]{4,3,2,1,0:T(8,128)(2,1)S(1)}, bf16[2,1,2,128,128]{4,3,2,1,0:T(8,128)(2,1)S(1)}, u32[]{:S(2)}, u32[]{:S(2)}) collective-permute-start(bf16[2,1,2,128,128]{4,3,2,1,0:T(8,128)(2,1)S(1)} %collective-permute-done.2.refs_3_), channel_id=1, source_target_pairs={{0,8},{1,9},{2,10},{3,11},{4,0},{5,1},{6,2},{7,3},{8,16},{9,17},{1... | collective-permute-start | bytes 393224 | tf_op jit(solution)/shard_map/ppermute | solution.py:342
  15.8 10.7 %collective-permute-start.8 = (bf16[2,2,2,128,128]{4,3,2,1,0:T(8,128)(2,1)S(1)}, bf16[2,2,2,128,128]{4,3,2,1,0:T(8,128)(2,1)S(1)}, u32[]{:S(2)}, u32[]{:S(2)}) collective-permute-start(bf16[2,2,2,128,128]{4,3,2,1,0:T(8,128)(2,1)S(1)} %get-tuple-element.43), channel_id=1, source_target_pairs={{0,4},{1,5},{2,6},{3,7},{4,0},{5,1},{6,2},{7,3},{8,12},{9,13},{10,... | collective-permute-start | bytes 786440 | tf_op jit(solution)/shard_map/ppermute | solution.py:342
  17.3 9.3 %collective-permute-start.9 = (bf16[2,2,2,128,128]{4,3,2,1,0:T(8,128)(2,1)S(1)}, bf16[2,2,2,128,128]{4,3,2,1,0:T(8,128)(2,1)S(1)}, u32[]{:S(2)}, u32[]{:S(2)}) collective-permute-start(bf16[2,2,2,128,128]{4,3,2,1,0:T(8,128)(2,1)S(1)} %get-tuple-element.45), channel_id=1, source_target_pairs={{0,1},{1,0},{2,3},{3,2},{4,8},{5,9},{6,10},{7,11},{8,4},{9,5},{10,... | collective-permute-start | bytes 786440 | tf_op jit(solution)/shard_map/ppermute | solution.py:342
  21.4 7.1 %collective-permute-start.7 = (bf16[2,2,2,128,128]{4,3,2,1,0:T(8,128)(2,1)S(1)}, bf16[2,2,2,128,128]{4,3,2,1,0:T(8,128)(2,1)S(1)}, u32[]{:S(2)}, u32[]{:S(2)}) collective-permute-start(bf16[2,2,2,128,128]{4,3,2,1,0:T(8,128)(2,1)S(1)} %get-tuple-element.40), channel_id=1, source_target_pairs={{0,3},{1,2},{2,1},{3,0},{4,7},{5,6},{6,5},{7,4},{8,11},{9,10},{10,... | collective-permute-start | bytes 786440 | tf_op jit(solution)/shard_map/ppermute | solution.py:342
  21.5 7.1 %collective-permute-start.6 = (bf16[2,2,2,128,128]{4,3,2,1,0:T(8,128)(2,1)S(1)}, bf16[2,2,2,128,128]{4,3,2,1,0:T(8,128)(2,1)S(1)}, u32[]{:S(2)}, u32[]{:S(2)}) collective-permute-start(bf16[2,2,2,128,128]{4,3,2,1,0:T(8,128)(2,1)S(1)} %get-tuple-element.39), channel_id=1, source_target_pairs={{0,1},{1,0},{2,3},{3,2},{4,5},{5,4},{6,7},{7,6},{8,9},{9,8},{10,11... | collective-permute-start | bytes 786440 | tf_op jit(solution)/shard_map/ppermute | solution.py:342

commit v6 on v5

--- a/solution.py
+++ b/solution.py
@@ -13,7 +13,8 @@
 EVEN = 3 * DIRS * (2 * REACH + 1)
 AT_REST = EVEN + 1
 INNER = EVEN + 2
-ENTRIES = EVEN + 3
+OWN_ON = EVEN + 3
+ENTRIES = EVEN + 4
 ROWS = 32
 GRANT = 16 * 2**20
 
@@ -34,13 +35,26 @@
     def pairs(step):
         return [(e * n_k + k, to_e * n_k + to_k % n_k) for e in range(n_e) for k in range(n_k) for to_e, to_k in [step(e, k)]]
 
-    def inside(e, otherwise):
-        return e if 0 <= e < n_e else otherwise
+    def relay(e, k):
+        if e in (0, n_e - 1):
+            return e, k ^ 1
+        if e in (1, n_e - 2):
+            return (2 if e == 1 else n_e - 3), k
+        return e + 2 - 4 * (e % 2), k
+
+    def ring(e, k):
+        to_e = e + 2 - 4 * (e % 2)
+        return (to_e if 0 <= to_e < n_e else e ^ 1), k
+
+    def cross(e, k):
+        to_e = e - 1 + 2 * (e % 2)
+        return (to_e, k) if 0 <= to_e < n_e else (e, k ^ 1)
 
     return {
         "pair": pairs(lambda e, k: (e ^ 1, k)),
-        "relay": pairs(lambda e, k: (inside(e + 2 - 4 * (e % 2), e ^ 1), k)),
-        "cross": pairs(lambda e, k: (inside(e - 1 + 2 * (e % 2), e), k ^ (0 <= e - 1 + 2 * (e % 2) < n_e) ^ 1)),
+        "relay": pairs(relay),
+        "ring": pairs(ring),
+        "cross": pairs(cross),
         "core": pairs(lambda e, k: (e, k ^ 1)),
         "far": pairs(lambda e, k: (e, k - 1 + 2 * (k % 2))),
     }
@@ -71,6 +85,7 @@
                 coef[(slot * DIRS + d) * (2 * REACH + 1) + s] = value.astype(jnp.bfloat16).astype(jnp.float32)
     coef[EVEN] = jnp.full((8, 128), 1 - parity[0], jnp.int32).astype(jnp.float32)
     coef[INNER] = jnp.full((8, 128), parity[2], jnp.int32).astype(jnp.float32)
+    coef[OWN_ON] = jnp.full((8, 128), parity[3], jnp.int32).astype(jnp.float32)
     coef[AT_REST] = jnp.full((8, 128), at_rest, jnp.float32)
     for t in range(tile_count):
         lo, hi = pattern[0, t], pattern[1, t]
@@ -310,6 +325,24 @@
     )(*map(in_vmem, (own_a, near_a, far_a, own_b, from_b)))
 
 
+def choose_kernel(own, near, coef, out):
+    first = jnp.broadcast_to(coef[OWN_ON][:1] > 0.5, out.shape[-2:])
+    for index in itertools.product(*map(range, out.shape[:-2])):
+        mine, other = own[index].astype(jnp.float32), near[index].astype(jnp.float32)
+        out[index] = jnp.where(first, mine, other).astype(out.dtype)
+
+
+def choose(own, near, coef):
+    return pl.pallas_call(
+        choose_kernel,
+        out_shape=pltpu.VMEM(own.shape, own.dtype),
+        in_specs=vmem_specs(3),
+        out_specs=vmem_specs(1)[0],
+        compiler_params=pltpu.CompilerParams(vmem_limit_bytes=GRANT),
+        name="choose",
+    )(in_vmem(own), in_vmem(near), in_vmem(coef))
+
+
 def split_kernel(source, *refs):
     outs, sems = refs[:-1], refs[-1]
     copies, tile = [], 0
@@ -348,14 +381,16 @@
     *in_a, in_b = split(green_tiles, [1] * half + [tile_count - half])
     e, k = (lax.axis_index(axis) for axis in AXES)
     inner = (e > 0) & (e < n_e - 1)
-    parity = jnp.stack([e % 2, k % 2, inner]).astype(jnp.int32)
+    parity = jnp.stack([e % 2, k % 2, inner, (e == 1) | (e == n_e - 2)]).astype(jnp.int32)
     near_a = [send(block, "pair") for block in in_a]
     far_b = send(in_b, "far")
     near_b = send(in_b, "core")
     left, right, coef = prepare(parity, phonon_modes.T, phonon_weight.transpose(1, 2, 0), tile_pattern.T, dham_blocks)
     partial_b = premix(shape_b[1], in_b, coef)
     near_a[0], partial_b = lax.optimization_barrier((near_a[0], partial_b))
-    far_a = [send(block, "relay") for block in near_a]
+    cut = half // 2
+    far_a = [send(choose(own, near, coef), "relay") for own, near in zip(in_a[:cut], near_a[:cut])]
+    far_a += [send(near, "ring") for near in near_a[cut:]]
     far_b, near_a = lax.optimization_barrier((far_b, near_a))
     pair_b, cross_b = sent(half, False, shape_b, (near_b, far_b, partial_b), left, right, coef)
     cross_b = send(cross_b, "cross")

time: 29.5 us -> 28.8 us (0.976)
  starting transfers between devices: 8.99 us -> 8.07 us
  Pallas kernels: 9.89 us -> 10.2 us
    ppermute x10, starting transfers between devices: 8.99 us -> 8.07 us  [send(): return lax.ppermute(block, AXES, route[name])]
  transfers between devices with their start and end apart: 10 -> 10, of which waited for: 5 -> 5; matrix products, arithmetic and copies ran while one was open for 0% -> 0% of each run, Pallas kernels for 27% -> 29%
where the time goes in v6:
time: 28.8 us; the launch traced here: 28.6 us
  Pallas kernels  10.2 us (35%)
  waiting for transfers between devices  10.2 us (35%)
  starting transfers between devices  8.07 us (28%)
    ppermute x10, waiting for transfers between devices, send(): return lax.ppermute(block, AXES, route[name])  10.2 us
    ppermute x10, starting transfers between devices, send(): return lax.ppermute(block, AXES, route[name])  8.07 us
    pallas_call x2, Pallas kernels, sent(): pl.pallas_call(functools.partial(sent_kernel, first, forward, places, cou...  3.79 us
    pallas_call x1, Pallas kernels, kept(): pl.pallas_call(functools.partial(kept_kernel, places, count), out_shape=(...  2.32 us
    pallas_call x1, Pallas kernels, prepare(): pl.pallas_call(prepare_kernel, out_shape=(big, big, pltpu.VMEM((ENTRIES,...  1.63 us
    pallas_call x1, Pallas kernels, split(): pl.pallas_call(split_kernel, out_shape=tuple((pltpu.VMEM((e, count, *rest...  1.11 us
    pallas_call x1, Pallas kernels, finish(): pl.pallas_call(finish_kernel, out_shape=jax.ShapeDtypeStruct((1,) + shape...  0.86 us
  transfers between devices with their start and end apart: 10, of which 5 were waited for; matrix products, arithmetic and copies ran while one was open for 0% of the time, Pallas kernels for 29%

profile of v6, /device:TPU:0, one launch (start us, length us, event | category | flops | bytes accessed | tf_op | source)
XLA Modules:
  0.0 28.6 jit_solution(9095236896406698591)
XLA Ops:
  0.0 1.1 %split.1 = (bf16[2,1,2,128,128]{4,3,2,1,0:T(8,128)(2,1)S(1)}, bf16[2,1,2,128,128]{4,3,2,1,0:T(8,128)(2,1)S(1)}, bf16[2,2,2,128,128]{4,3,2,1,0:T(8,128)(2,1)S(1)}) custom-call(bf16[1,2,4,2,128,128]{5,4,3,2,1,0:T(8,128)(2,1)} %source.1), custom_call_target="tpu_custom_call" | custom-call | tf_op jit(solution)/shard_map/split/pallas_call | solution.py:359
  1.1 2.5 %collective-permute-start = (bf16[2,2,2,128,128]{4,3,2,1,0:T(8,128)(2,1)S(1)}, bf16[2,2,2,128,128]{4,3,2,1,0:T(8,128)(2,1)S(1)}, u32[]{:S(2)}, u32[]{:S(2)}) collective-permute-start(bf16[2,2,2,128,128]{4,3,2,1,0:T(8,128)(2,1)S(1)} %get-tuple-element.36.refs_0_.refs_6_), channel_id=1, source_target_pairs={{0,3},{1,2},{2,1},{3,0},{4,7},{5,6},{6,5},{7,4},{8,11},{9,10},{10,... | collective-permute-start | bytes 786440 | tf_op jit(solution)/shard_map/ppermute | solution.py:375
  3.6 0.7 %collective-permute-start.5 = (bf16[2,2,2,128,128]{4,3,2,1,0:T(8,128)(2,1)S(1)}, bf16[2,2,2,128,128]{4,3,2,1,0:T(8,128)(2,1)S(1)}, u32[]{:S(2)}, u32[]{:S(2)}) collective-permute-start(bf16[2,2,2,128,128]{4,3,2,1,0:T(8,128)(2,1)S(1)} %get-tuple-element.36.refs_0_.refs_6_), channel_id=1, source_target_pairs={{0,1},{1,0},{2,3},{3,2},{4,5},{5,4},{6,7},{7,6},{8,9},{9,8},{10,11... | collective-permute-start | bytes 786440 | tf_op jit(solution)/shard_map/ppermute | solution.py:375
  4.3 1.5 %collective-permute-start.1 = (bf16[2,1,2,128,128]{4,3,2,1,0:T(8,128)(2,1)S(1)}, bf16[2,1,2,128,128]{4,3,2,1,0:T(8,128)(2,1)S(1)}, u32[]{:S(2)}, u32[]{:S(2)}) collective-permute-start(bf16[2,1,2,128,128]{4,3,2,1,0:T(8,128)(2,1)S(1)} %get-tuple-element.26.own.refs_0_), channel_id=1, source_target_pairs={{0,4},{1,5},{2,6},{3,7},{4,0},{5,1},{6,2},{7,3},{8,12},{9,13},{10,... | collective-permute-start | bytes 393224 | tf_op jit(solution)/shard_map/ppermute | solution.py:375
  5.8 0.5 %collective-permute-start.2 = (bf16[2,1,2,128,128]{4,3,2,1,0:T(8,128)(2,1)S(1)}, bf16[2,1,2,128,128]{4,3,2,1,0:T(8,128)(2,1)S(1)}, u32[]{:S(2)}, u32[]{:S(2)}) collective-permute-start(bf16[2,1,2,128,128]{4,3,2,1,0:T(8,128)(2,1)S(1)} %get-tuple-element.27.refs_1_), channel_id=1, source_target_pairs={{0,4},{1,5},{2,6},{3,7},{4,0},{5,1},{6,2},{7,3},{8,12},{9,13},{10,... | collective-permute-start | bytes 393224 | tf_op jit(solution)/shard_map/ppermute | solution.py:375
  6.3 0.1 pad_add_fusion.parity
  6.4 1.6 %prepare.1 = (bf16[4,3,256,256]{3,2,1,0:T(8,128)(2,1)S(1)}, bf16[4,3,256,256]{3,2,1,0:T(8,128)(2,1)S(1)}, f32[49,8,128]{2,1,0:T(8,128)S(1)}) custom-call(s32[4]{0:T(128)S(1)} %pad_add_fusion.parity, s32[2,6]{1,0:T(2,128)} %bitcast.8, f32[3,2,6]{2,1,0:T(2,128)} %bitcast.7, s32[2,4]{1,0:T(2,128)} %bitcast.9, bf16[3,4,2,128,128]{4,3,2,1,0:T(8,128)(2,1)} %dham.1), custom_call_target="tpu_custom_call" | custom-call | tf_op jit(solution)/shard_map/prepare/pallas_call | solution.py:108
  8.0 0.4 %premix.1.refs_2_ = f32[2,3,256,512]{3,2,1,0:T(8,128)S(1)} custom-call(bf16[2,2,2,128,128]{4,3,2,1,0:T(8,128)(2,1)S(1)} %get-tuple-element.36.refs_0_.refs_6_, f32[49,8,128]{2,1,0:T(8,128)S(1)} %get-tuple-element.29.refs_1_.coef.refs_8_.refs_11_.refs_5_), custom_call_target="tpu_custom_call" | custom-call | flops 600000000 | bytes 2000000 | tf_op jit(solution)/shard_map/premix/pallas_call | solution.py:202
  8.4 2.2 %collective-permute-done.1.near.refs_2_ = bf16[2,1,2,128,128]{4,3,2,1,0:T(8,128)(2,1)S(1)} collective-permute-done((bf16[2,1,2,128,128]{4,3,2,1,0:T(8,128)(2,1)S(1)}, bf16[2,1,2,128,128]{4,3,2,1,0:T(8,128)(2,1)S(1)}, u32[]{:S(2)}, u32[]{:S(2)}) %collective-permute-start.1) | collective-permute-done | bytes 131104 | tf_op jit(solution)/shard_map/ppermute | solution.py:375
  10.7 0.1 collective-permute-start.3
  10.7 1.7 %collective-permute-done.2.refs_3_ = bf16[2,1,2,128,128]{4,3,2,1,0:T(8,128)(2,1)S(1)} collective-permute-done((bf16[2,1,2,128,128]{4,3,2,1,0:T(8,128)(2,1)S(1)}, bf16[2,1,2,128,128]{4,3,2,1,0:T(8,128)(2,1)S(1)}, u32[]{:S(2)}, u32[]{:S(2)}) %collective-permute-start.2) | collective-permute-done | bytes 131104 | tf_op jit(solution)/shard_map/ppermute | solution.py:375
  12.5 1.6 %collective-permute-start.4 = (bf16[2,1,2,128,128]{4,3,2,1,0:T(8,128)(2,1)S(1)}, bf16[2,1,2,128,128]{4,3,2,1,0:T(8,128)(2,1)S(1)}, u32[]{:S(2)}, u32[]{:S(2)}) collective-permute-start(bf16[2,1,2,128,128]{4,3,2,1,0:T(8,128)(2,1)S(1)} %collective-permute-done.2.refs_3_), channel_id=1, source_target_pairs={{0,8},{1,9},{2,10},{3,11},{4,0},{5,1},{6,2},{7,3},{8,16},{9,17},{1... | collective-permute-start | bytes 393224 | tf_op jit(solution)/shard_map/ppermute | solution.py:375
  14.1 0.0 collective-permute-done.refs_8_.refs_1_
  14.1 0.0 collective-permute-done.5.refs_7_.refs_0_
  14.1 1.9 %sent.3 = (bf16[2,2,2,128,128]{4,3,2,1,0:T(8,128)(2,1)S(1)}, bf16[2,2,2,128,128]{4,3,2,1,0:T(8,128)(2,1)S(1)}) custom-call(bf16[2,2,2,128,128]{4,3,2,1,0:T(8,128)(2,1)S(1)} %collective-permute-done.5.refs_7_.refs_0_, bf16[2,2,2,128,128]{4,3,2,1,0:T(8,128)(2,1)S(1)} %collective-permute-done.refs_8_.refs_1_, f32[2,3,256,512]{3,2,1,0:T(8,128)S(1)} %premix.1.refs_2_, ...), custom_call_target="tpu_custom_call" | custom-call | flops 2400000000 | bytes 8000000 | tf_op jit(solution)/shard_map/sent/pallas_call | solution.py:237
  15.9 0.5 %collective-permute-start.8 = (bf16[2,2,2,128,128]{4,3,2,1,0:T(8,128)(2,1)S(1)}, bf16[2,2,2,128,128]{4,3,2,1,0:T(8,128)(2,1)S(1)}, u32[]{:S(2)}, u32[]{:S(2)}) collective-permute-start(bf16[2,2,2,128,128]{4,3,2,1,0:T(8,128)(2,1)S(1)} %get-tuple-element.43), channel_id=1, source_target_pairs={{0,4},{1,5},{2,6},{3,7},{4,0},{5,1},{6,2},{7,3},{8,12},{9,13},{10,... | collective-permute-start | bytes 786440 | tf_op jit(solution)/shard_map/ppermute | solution.py:375
  16.4 0.0 collective-permute-start.9
  16.4 0.0 collective-permute-done.3.refs_4_
  16.4 1.0 %collective-permute-done.4.refs_5_ = bf16[2,1,2,128,128]{4,3,2,1,0:T(8,128)(2,1)S(1)} collective-permute-done((bf16[2,1,2,128,128]{4,3,2,1,0:T(8,128)(2,1)S(1)}, bf16[2,1,2,128,128]{4,3,2,1,0:T(8,128)(2,1)S(1)}, u32[]{:S(2)}, u32[]{:S(2)}) %collective-permute-start.4) | collective-permute-done | bytes 131104 | tf_op jit(solution)/shard_map/ppermute | solution.py:375
  17.4 1.9 %sent.2 = (bf16[2,2,2,128,128]{4,3,2,1,0:T(8,128)(2,1)S(1)}, bf16[2,2,2,128,128]{4,3,2,1,0:T(8,128)(2,1)S(1)}) custom-call(bf16[2,1,2,128,128]{4,3,2,1,0:T(8,128)(2,1)S(1)} %get-tuple-element.26.own.refs_0_, bf16[2,1,2,128,128]{4,3,2,1,0:T(8,128)(2,1)S(1)} %get-tuple-element.27.refs_1_, bf16[2,1,2,128,128]{4,3,2,1,0:T(8,128)(2,1)S(1)} %collective-permute-done.1.near.refs_2_, ...), custom_call_target="tpu_custom_call" | custom-call | flops 2400000000 | bytes 8000000 | tf_op jit(solution)/shard_map/sent/pallas_call | solution.py:237
  19.4 0.1 collective-permute-start.7
  19.5 0.7 %collective-permute-start.6 = (bf16[2,2,2,128,128]{4,3,2,1,0:T(8,128)(2,1)S(1)}, bf16[2,2,2,128,128]{4,3,2,1,0:T(8,128)(2,1)S(1)}, u32[]{:S(2)}, u32[]{:S(2)}) collective-permute-start(bf16[2,2,2,128,128]{4,3,2,1,0:T(8,128)(2,1)S(1)} %get-tuple-element.39), channel_id=1, source_target_pairs={{0,1},{1,0},{2,3},{3,2},{4,5},{5,4},{6,7},{7,6},{8,9},{9,8},{10,11... | collective-permute-start | bytes 786440 | tf_op jit(solution)/shard_map/ppermute | solution.py:375
  20.1 2.3 %kept.1 = (f32[2,2,2,128,128]{4,3,2,1,0:T(8,128)S(1)}, f32[2,2,2,128,128]{4,3,2,1,0:T(8,128)S(1)}) custom-call(bf16[2,1,2,128,128]{4,3,2,1,0:T(8,128)(2,1)S(1)} %get-tuple-element.26.own.refs_0_, bf16[2,1,2,128,128]{4,3,2,1,0:T(8,128)(2,1)S(1)} %get-tuple-element.27.refs_1_, bf16[2,1,2,128,128]{4,3,2,1,0:T(8,128)(2,1)S(1)} %collective-permute-done.1.near.refs_2_, ...), custom_call_target="tpu_custom_call" | custom-call | flops 2400000000 | bytes 8000000 | tf_op jit(solution)/shard_map/kept/pallas_call | solution.py:267
  22.5 4.2 %collective-permute-done.8.near = bf16[2,2,2,128,128]{4,3,2,1,0:T(8,128)(2,1)S(1)} collective-permute-done((bf16[2,2,2,128,128]{4,3,2,1,0:T(8,128)(2,1)S(1)}, bf16[2,2,2,128,128]{4,3,2,1,0:T(8,128)(2,1)S(1)}, u32[]{:S(2)}, u32[]{:S(2)}) %collective-permute-start.8) | collective-permute-done | bytes 262176 | tf_op jit(solution)/shard_map/ppermute | solution.py:375
  26.7 0.0 collective-permute-done.9.far
  26.7 0.1 gather.1.from_b
  26.7 1.0 %collective-permute-done.7.far_a = bf16[2,2,2,128,128]{4,3,2,1,0:T(8,128)(2,1)S(1)} collective-permute-done((bf16[2,2,2,128,128]{4,3,2,1,0:T(8,128)(2,1)S(1)}, bf16[2,2,2,128,128]{4,3,2,1,0:T(8,128)(2,1)S(1)}, u32[]{:S(2)}, u32[]{:S(2)}) %collective-permute-start.7) | collective-permute-done | bytes 262176 | tf_op jit(solution)/shard_map/ppermute | solution.py:375
  27.7 0.0 collective-permute-done.6.near_a
  27.7 0.9 %finish.1 = bf16[1,2,4,2,128,128]{5,4,3,2,1,0:T(8,128)(2,1)} custom-call(f32[2,2,2,128,128]{4,3,2,1,0:T(8,128)S(1)} %get-tuple-element.38.own_a, bf16[2,2,2,128,128]{4,3,2,1,0:T(8,128)(2,1)S(1)} %collective-permute-done.6.near_a, bf16[2,2,2,128,128]{4,3,2,1,0:T(8,128)(2,1)S(1)} %collective-permute-done.7.far_a, ...), custom_call_target="tpu_custom_call" | custom-call | tf_op jit(solution)/shard_map/finish/pallas_call | solution.py:317
  (1 shorter events, 0.0 us)
Async XLA Ops:
  1.1 13.0 %collective-permute-start = (bf16[2,2,2,128,128]{4,3,2,1,0:T(8,128)(2,1)S(1)}, bf16[2,2,2,128,128]{4,3,2,1,0:T(8,128)(2,1)S(1)}, u32[]{:S(2)}, u32[]{:S(2)}) collective-permute-start(bf16[2,2,2,128,128]{4,3,2,1,0:T(8,128)(2,1)S(1)} %get-tuple-element.36.refs_0_.refs_6_), channel_id=1, source_target_pairs={{0,3},{1,2},{2,1},{3,0},{4,7},{5,6},{6,5},{7,4},{8,11},{9,10},{10,... | collective-permute-start | bytes 786440 | tf_op jit(solution)/shard_map/ppermute | solution.py:375
  3.6 10.5 %collective-permute-start.5 = (bf16[2,2,2,128,128]{4,3,2,1,0:T(8,128)(2,1)S(1)}, bf16[2,2,2,128,128]{4,3,2,1,0:T(8,128)(2,1)S(1)}, u32[]{:S(2)}, u32[]{:S(2)}) collective-permute-start(bf16[2,2,2,128,128]{4,3,2,1,0:T(8,128)(2,1)S(1)} %get-tuple-element.36.refs_0_.refs_6_), channel_id=1, source_target_pairs={{0,1},{1,0},{2,3},{3,2},{4,5},{5,4},{6,7},{7,6},{8,9},{9,8},{10,11... | collective-permute-start | bytes 786440 | tf_op jit(solution)/shard_map/ppermute | solution.py:375
  4.3 6.4 %collective-permute-start.1 = (bf16[2,1,2,128,128]{4,3,2,1,0:T(8,128)(2,1)S(1)}, bf16[2,1,2,128,128]{4,3,2,1,0:T(8,128)(2,1)S(1)}, u32[]{:S(2)}, u32[]{:S(2)}) collective-permute-start(bf16[2,1,2,128,128]{4,3,2,1,0:T(8,128)(2,1)S(1)} %get-tuple-element.26.own.refs_0_), channel_id=1, source_target_pairs={{0,4},{1,5},{2,6},{3,7},{4,0},{5,1},{6,2},{7,3},{8,12},{9,13},{10,... | collective-permute-start | bytes 393224 | tf_op jit(solution)/shard_map/ppermute | solution.py:375
  5.8 6.7 %collective-permute-start.2 = (bf16[2,1,2,128,128]{4,3,2,1,0:T(8,128)(2,1)S(1)}, bf16[2,1,2,128,128]{4,3,2,1,0:T(8,128)(2,1)S(1)}, u32[]{:S(2)}, u32[]{:S(2)}) collective-permute-start(bf16[2,1,2,128,128]{4,3,2,1,0:T(8,128)(2,1)S(1)} %get-tuple-element.27.refs_1_), channel_id=1, source_target_pairs={{0,4},{1,5},{2,6},{3,7},{4,0},{5,1},{6,2},{7,3},{8,12},{9,13},{10,... | collective-permute-start | bytes 393224 | tf_op jit(solution)/shard_map/ppermute | solution.py:375
  10.7 5.8 %collective-permute-start.3 = (bf16[2,1,2,128,128]{4,3,2,1,0:T(8,128)(2,1)S(1)}, bf16[2,1,2,128,128]{4,3,2,1,0:T(8,128)(2,1)S(1)}, u32[]{:S(2)}, u32[]{:S(2)}) collective-permute-start(bf16[2,1,2,128,128]{4,3,2,1,0:T(8,128)(2,1)S(1)} %choose.1), channel_id=1, source_target_pairs={{0,1},{1,0},{2,3},{3,2},{4,8},{5,9},{6,10},{7,11},{8,16},{9,17},{1... | collective-permute-start | bytes 393224 | tf_op jit(solution)/shard_map/ppermute | solution.py:375
  12.5 5.0 %collective-permute-start.4 = (bf16[2,1,2,128,128]{4,3,2,1,0:T(8,128)(2,1)S(1)}, bf16[2,1,2,128,128]{4,3,2,1,0:T(8,128)(2,1)S(1)}, u32[]{:S(2)}, u32[]{:S(2)}) collective-permute-start(bf16[2,1,2,128,128]{4,3,2,1,0:T(8,128)(2,1)S(1)} %collective-permute-done.2.refs_3_), channel_id=1, source_target_pairs={{0,8},{1,9},{2,10},{3,11},{4,0},{5,1},{6,2},{7,3},{8,16},{9,17},{1... | collective-permute-start | bytes 393224 | tf_op jit(solution)/shard_map/ppermute | solution.py:375
  15.9 10.7 %collective-permute-start.8 = (bf16[2,2,2,128,128]{4,3,2,1,0:T(8,128)(2,1)S(1)}, bf16[2,2,2,128,128]{4,3,2,1,0:T(8,128)(2,1)S(1)}, u32[]{:S(2)}, u32[]{:S(2)}) collective-permute-start(bf16[2,2,2,128,128]{4,3,2,1,0:T(8,128)(2,1)S(1)} %get-tuple-element.43), channel_id=1, source_target_pairs={{0,4},{1,5},{2,6},{3,7},{4,0},{5,1},{6,2},{7,3},{8,12},{9,13},{10,... | collective-permute-start | bytes 786440 | tf_op jit(solution)/shard_map/ppermute | solution.py:375
  16.4 10.2 %collective-permute-start.9 = (bf16[2,2,2,128,128]{4,3,2,1,0:T(8,128)(2,1)S(1)}, bf16[2,2,2,128,128]{4,3,2,1,0:T(8,128)(2,1)S(1)}, u32[]{:S(2)}, u32[]{:S(2)}) collective-permute-start(bf16[2,2,2,128,128]{4,3,2,1,0:T(8,128)(2,1)S(1)} %get-tuple-element.45), channel_id=1, source_target_pairs={{0,1},{1,0},{2,3},{3,2},{4,8},{5,9},{6,10},{7,11},{8,4},{9,5},{10,... | collective-permute-start | bytes 786440 | tf_op jit(solution)/shard_map/ppermute | solution.py:375
  19.4 8.4 %collective-permute-start.7 = (bf16[2,2,2,128,128]{4,3,2,1,0:T(8,128)(2,1)S(1)}, bf16[2,2,2,128,128]{4,3,2,1,0:T(8,128)(2,1)S(1)}, u32[]{:S(2)}, u32[]{:S(2)}) collective-permute-start(bf16[2,2,2,128,128]{4,3,2,1,0:T(8,128)(2,1)S(1)} %get-tuple-element.40), channel_id=1, source_target_pairs={{0,3},{1,2},{2,1},{3,0},{4,7},{5,6},{6,5},{7,4},{8,11},{9,10},{10,... | collective-permute-start | bytes 786440 | tf_op jit(solution)/shard_map/ppermute | solution.py:375
  19.5 8.3 %collective-permute-start.6 = (bf16[2,2,2,128,128]{4,3,2,1,0:T(8,128)(2,1)S(1)}, bf16[2,2,2,128,128]{4,3,2,1,0:T(8,128)(2,1)S(1)}, u32[]{:S(2)}, u32[]{:S(2)}) collective-permute-start(bf16[2,2,2,128,128]{4,3,2,1,0:T(8,128)(2,1)S(1)} %get-tuple-element.39), channel_id=1, source_target_pairs={{0,1},{1,0},{2,3},{3,2},{4,5},{5,4},{6,7},{7,6},{8,9},{9,8},{10,11... | collective-permute-start | bytes 786440 | tf_op jit(solution)/shard_map/ppermute | solution.py:375

commit v7 on v6

--- a/solution.py
+++ b/solution.py
@@ -60,7 +60,7 @@
     }
 
 
-def prepare_kernel(parity, modes, weight, pattern, dham, left, right, coef, table):
+def prepare_kernel(parity, modes, weight, pattern, dham, left, right, coef, wide, table):
     mode_count = modes.shape[1]
     tile_count = pattern.shape[1]
     for q in range(4):
@@ -83,6 +83,13 @@
                     at_rest = at_rest + jnp.abs(value)
                 value = jnp.full((8, 128), value, jnp.float32)
                 coef[(slot * DIRS + d) * (2 * REACH + 1) + s] = value.astype(jnp.bfloat16).astype(jnp.float32)
+    for slot, q in enumerate((0, toward, -toward)):
+        for d in range(DIRS):
+            for at in range(2 * REACH + 1):
+                value = jnp.full((8, 256), table[q + 1, d, at], jnp.float32)
+                wide[(slot * DIRS + d) * (2 * REACH + 1) + at] = value.astype(jnp.bfloat16)
+    wide[EVEN] = jnp.full((8, 256), 1 - parity[0], jnp.int32).astype(jnp.float32).astype(jnp.bfloat16)
+    wide[INNER] = jnp.full((8, 256), parity[2], jnp.int32).astype(jnp.float32).astype(jnp.bfloat16)
     coef[EVEN] = jnp.full((8, 128), 1 - parity[0], jnp.int32).astype(jnp.float32)
     coef[INNER] = jnp.full((8, 128), parity[2], jnp.int32).astype(jnp.float32)
     coef[OWN_ON] = jnp.full((8, 128), parity[3], jnp.int32).astype(jnp.float32)
@@ -107,9 +114,9 @@
     big = pltpu.VMEM((tile_count, DIRS, 256, 256), jnp.bfloat16)
     return pl.pallas_call(
         prepare_kernel,
-        out_shape=(big, big, pltpu.VMEM((ENTRIES, 8, 128), jnp.float32)),
+        out_shape=(big, big, pltpu.VMEM((ENTRIES, 8, 128), jnp.float32), pltpu.VMEM((ENTRIES, 8, 256), jnp.bfloat16)),
         in_specs=[pl.BlockSpec(memory_space=pltpu.SMEM)] * 4 + vmem_specs(1),
-        out_specs=tuple(vmem_specs(3)),
+        out_specs=tuple(vmem_specs(4)),
         scratch_shapes=[pltpu.SMEM((4, DIRS, 2 * REACH + 1), jnp.float32)],
         compiler_params=pltpu.CompilerParams(vmem_limit_bytes=GRANT),
         name="prepare",
@@ -152,6 +159,31 @@
                     out[here] = acc.reshape(ROWS, 128).astype(out.dtype)
 
 
+def mix_wide(t, steps, sources, wide, mixed):
+    even, inner = wide[EVEN] > 0.5, wide[INNER] > 0.5
+    for part in range(2):
+        for row in range(0, 128, ROWS):
+            own, near, far = (
+                jnp.concatenate([source[t][j, 0, part, pl.ds(row, ROWS), :] for j in range(2)], axis=1).reshape(ROWS // 8, 8, 256)
+                for source in sources
+            )
+            far = jnp.where(inner, far, jnp.zeros_like(far))
+            below, above = jnp.where(even, far, near), jnp.where(even, near, far)
+            beside = {
+                -2: below,
+                -1: jnp.concatenate([below[..., 128:], own[..., :128]], axis=2),
+                0: own,
+                1: jnp.concatenate([own[..., 128:], above[..., :128]], axis=2),
+                2: above,
+            }
+            for d in range(DIRS):
+                for slot in (1, 2):
+                    terms = [beside[s] * wide[(slot * DIRS + d) * (2 * REACH + 1) + s + REACH] for s in steps]
+                    while len(terms) > 1:
+                        terms = [a + b for a, b in zip(terms[::2], terms[1::2])] + terms[len(terms) - len(terms) % 2 :]
+                    mixed[t, d, pl.ds(part * 128 + row, ROWS), pl.ds(slot * 256 - 256, 256)] = terms[0].reshape(ROWS, 256)
+
+
 def multiply(t, first, count, left, right, mixed, product):
     for d in range(DIRS):
         got = jnp.dot(left[first + t, d], mixed[t, d], preferred_element_type=jnp.float32).astype(jnp.bfloat16)
@@ -215,7 +247,7 @@
 
     def run(t, steps):
         if forward:
-            mix(t, True, steps, (0, 1, 2), SENT_IN, sources, coef, None, mixed)
+            mix_wide(t, steps, sources[:3], sources[3], mixed)
         else:
             mix(t, False, steps, (1, 2), SENT_OUT, {1: sources[0], 2: sources[1]}, coef, sources[2], mixed)
         term = multiply(t, first, 4, left, right, mixed, product)
@@ -385,7 +417,7 @@
     near_a = [send(block, "pair") for block in in_a]
     far_b = send(in_b, "far")
     near_b = send(in_b, "core")
-    left, right, coef = prepare(parity, phonon_modes.T, phonon_weight.transpose(1, 2, 0), tile_pattern.T, dham_blocks)
+    left, right, coef, wide = prepare(parity, phonon_modes.T, phonon_weight.transpose(1, 2, 0), tile_pattern.T, dham_blocks)
     partial_b = premix(shape_b[1], in_b, coef)
     near_a[0], partial_b = lax.optimization_barrier((near_a[0], partial_b))
     cut = half // 2
@@ -395,7 +427,7 @@
     pair_b, cross_b = sent(half, False, shape_b, (near_b, far_b, partial_b), left, right, coef)
     cross_b = send(cross_b, "cross")
     pair_b = send(pair_b, "pair")
-    core_a, next_a = sent(0, True, shape_a, (in_a, near_a, far_a), left, right, coef)
+    core_a, next_a = sent(0, True, shape_a, (in_a, near_a, far_a, wide), left, right, coef)
     in_b, next_a = lax.optimization_barrier((in_b, next_a))
     core_a = send(core_a, "core")
     next_a = send(next_a, "far")

time: 28.8 us -> 28.5 us (0.990)
  transfers between devices with their start and end apart: 10 -> 10, of which waited for: 5 -> 5; matrix products, arithmetic and copies ran while one was open for 0% -> 0% of each run, Pallas kernels for 29% -> 28%
where the time goes in v7:
time: 28.5 us; the launch traced here: 28.4 us
  waiting for transfers between devices  10.2 us (36%)
  Pallas kernels  9.96 us (35%)
  starting transfers between devices  8.07 us (28%)
    ppermute x10, waiting for transfers between devices, send(): return lax.ppermute(block, AXES, route[name])  10.2 us
    ppermute x10, starting transfers between devices, send(): return lax.ppermute(block, AXES, route[name])  8.07 us
    pallas_call x2, Pallas kernels, sent(): pl.pallas_call(functools.partial(sent_kernel, first, forward, places, cou...  3.54 us
    pallas_call x1, Pallas kernels, kept(): pl.pallas_call(functools.partial(kept_kernel, places, count), out_shape=(...  2.33 us
    pallas_call x1, Pallas kernels, prepare(): pl.pallas_call(prepare_kernel, out_shape=(big, big, pltpu.VMEM((ENTRIES,...  1.64 us
    pallas_call x1, Pallas kernels, split(): pl.pallas_call(split_kernel, out_shape=tuple((pltpu.VMEM((e, count, *rest...  1.11 us
    pallas_call x1, Pallas kernels, finish(): pl.pallas_call(finish_kernel, out_shape=jax.ShapeDtypeStruct((1,) + shape...  0.86 us
  transfers between devices with their start and end apart: 10, of which 5 were waited for; matrix products, arithmetic and copies ran while one was open for 0% of the time, Pallas kernels for 28%

profile of v7, /device:TPU:0, one launch (start us, length us, event | category | flops | bytes accessed | tf_op | source)
XLA Modules:
  0.0 28.4 jit_solution(16641153430043507649)
XLA Ops:
  0.0 1.1 %split.1 = (bf16[2,1,2,128,128]{4,3,2,1,0:T(8,128)(2,1)S(1)}, bf16[2,1,2,128,128]{4,3,2,1,0:T(8,128)(2,1)S(1)}, bf16[2,2,2,128,128]{4,3,2,1,0:T(8,128)(2,1)S(1)}) custom-call(bf16[1,2,4,2,128,128]{5,4,3,2,1,0:T(8,128)(2,1)} %source.1), custom_call_target="tpu_custom_call" | custom-call | tf_op jit(solution)/shard_map/split/pallas_call | solution.py:391
  1.1 2.5 %collective-permute-start = (bf16[2,2,2,128,128]{4,3,2,1,0:T(8,128)(2,1)S(1)}, bf16[2,2,2,128,128]{4,3,2,1,0:T(8,128)(2,1)S(1)}, u32[]{:S(2)}, u32[]{:S(2)}) collective-permute-start(bf16[2,2,2,128,128]{4,3,2,1,0:T(8,128)(2,1)S(1)} %get-tuple-element.38.refs_0_.refs_6_), channel_id=1, source_target_pairs={{0,3},{1,2},{2,1},{3,0},{4,7},{5,6},{6,5},{7,4},{8,11},{9,10},{10,... | collective-permute-start | bytes 786440 | tf_op jit(solution)/shard_map/ppermute | solution.py:407
  3.6 0.7 %collective-permute-start.5 = (bf16[2,2,2,128,128]{4,3,2,1,0:T(8,128)(2,1)S(1)}, bf16[2,2,2,128,128]{4,3,2,1,0:T(8,128)(2,1)S(1)}, u32[]{:S(2)}, u32[]{:S(2)}) collective-permute-start(bf16[2,2,2,128,128]{4,3,2,1,0:T(8,128)(2,1)S(1)} %get-tuple-element.38.refs_0_.refs_6_), channel_id=1, source_target_pairs={{0,1},{1,0},{2,3},{3,2},{4,5},{5,4},{6,7},{7,6},{8,9},{9,8},{10,11... | collective-permute-start | bytes 786440 | tf_op jit(solution)/shard_map/ppermute | solution.py:407
  4.3 1.5 %collective-permute-start.1 = (bf16[2,1,2,128,128]{4,3,2,1,0:T(8,128)(2,1)S(1)}, bf16[2,1,2,128,128]{4,3,2,1,0:T(8,128)(2,1)S(1)}, u32[]{:S(2)}, u32[]{:S(2)}) collective-permute-start(bf16[2,1,2,128,128]{4,3,2,1,0:T(8,128)(2,1)S(1)} %get-tuple-element.27.own.refs_0_), channel_id=1, source_target_pairs={{0,4},{1,5},{2,6},{3,7},{4,0},{5,1},{6,2},{7,3},{8,12},{9,13},{10,... | collective-permute-start | bytes 393224 | tf_op jit(solution)/shard_map/ppermute | solution.py:407
  5.8 0.5 %collective-permute-start.2 = (bf16[2,1,2,128,128]{4,3,2,1,0:T(8,128)(2,1)S(1)}, bf16[2,1,2,128,128]{4,3,2,1,0:T(8,128)(2,1)S(1)}, u32[]{:S(2)}, u32[]{:S(2)}) collective-permute-start(bf16[2,1,2,128,128]{4,3,2,1,0:T(8,128)(2,1)S(1)} %get-tuple-element.28.refs_1_), channel_id=1, source_target_pairs={{0,4},{1,5},{2,6},{3,7},{4,0},{5,1},{6,2},{7,3},{8,12},{9,13},{10,... | collective-permute-start | bytes 393224 | tf_op jit(solution)/shard_map/ppermute | solution.py:407
  6.3 0.1 pad_add_fusion.parity
  6.4 1.6 %prepare.1 = (bf16[4,3,256,256]{3,2,1,0:T(8,128)(2,1)S(1)}, bf16[4,3,256,256]{3,2,1,0:T(8,128)(2,1)S(1)}, f32[49,8,128]{2,1,0:T(8,128)S(1)}, bf16[49,8,256]{2,1,0:T(8,128)(2,1)S(1)}) custom-call(s32[4]{0:T(128)S(1)} %pad_add_fusion.parity, s32[2,6]{1,0:T(2,128)} %bitcast.8, f32[3,2,6]{2,1,0:T(2,128)} %bitcast.7, s32[2,4]{1,0:T(2,128)} %bitcast.9, ...), custom_call_target="tpu_custom_call" | custom-call | tf_op jit(solution)/shard_map/prepare/pallas_call | solution.py:115
  8.0 0.4 %premix.1.refs_2_ = f32[2,3,256,512]{3,2,1,0:T(8,128)S(1)} custom-call(bf16[2,2,2,128,128]{4,3,2,1,0:T(8,128)(2,1)S(1)} %get-tuple-element.38.refs_0_.refs_6_, f32[49,8,128]{2,1,0:T(8,128)S(1)} %get-tuple-element.30.refs_1_.coef.refs_9_.refs_11_.refs_5_), custom_call_target="tpu_custom_call" | custom-call | flops 600000000 | bytes 2000000 | tf_op jit(solution)/shard_map/premix/pallas_call | solution.py:234
  8.4 2.2 %collective-permute-done.1.near.refs_2_ = bf16[2,1,2,128,128]{4,3,2,1,0:T(8,128)(2,1)S(1)} collective-permute-done((bf16[2,1,2,128,128]{4,3,2,1,0:T(8,128)(2,1)S(1)}, bf16[2,1,2,128,128]{4,3,2,1,0:T(8,128)(2,1)S(1)}, u32[]{:S(2)}, u32[]{:S(2)}) %collective-permute-start.1) | collective-permute-done | bytes 131104 | tf_op jit(solution)/shard_map/ppermute | solution.py:407
  10.7 0.1 collective-permute-start.3
  10.7 1.7 %collective-permute-done.2.refs_3_ = bf16[2,1,2,128,128]{4,3,2,1,0:T(8,128)(2,1)S(1)} collective-permute-done((bf16[2,1,2,128,128]{4,3,2,1,0:T(8,128)(2,1)S(1)}, bf16[2,1,2,128,128]{4,3,2,1,0:T(8,128)(2,1)S(1)}, u32[]{:S(2)}, u32[]{:S(2)}) %collective-permute-start.2) | collective-permute-done | bytes 131104 | tf_op jit(solution)/shard_map/ppermute | solution.py:407
  12.5 1.6 %collective-permute-start.4 = (bf16[2,1,2,128,128]{4,3,2,1,0:T(8,128)(2,1)S(1)}, bf16[2,1,2,128,128]{4,3,2,1,0:T(8,128)(2,1)S(1)}, u32[]{:S(2)}, u32[]{:S(2)}) collective-permute-start(bf16[2,1,2,128,128]{4,3,2,1,0:T(8,128)(2,1)S(1)} %collective-permute-done.2.refs_3_), channel_id=1, source_target_pairs={{0,8},{1,9},{2,10},{3,11},{4,0},{5,1},{6,2},{7,3},{8,16},{9,17},{1... | collective-permute-start | bytes 393224 | tf_op jit(solution)/shard_map/ppermute | solution.py:407
  14.1 0.0 collective-permute-done.refs_8_.refs_1_
  14.1 0.0 collective-permute-done.5.refs_7_.refs_0_
  14.1 1.9 %sent.3 = (bf16[2,2,2,128,128]{4,3,2,1,0:T(8,128)(2,1)S(1)}, bf16[2,2,2,128,128]{4,3,2,1,0:T(8,128)(2,1)S(1)}) custom-call(bf16[2,2,2,128,128]{4,3,2,1,0:T(8,128)(2,1)S(1)} %collective-permute-done.5.refs_7_.refs_0_, bf16[2,2,2,128,128]{4,3,2,1,0:T(8,128)(2,1)S(1)} %collective-permute-done.refs_8_.refs_1_, f32[2,3,256,512]{3,2,1,0:T(8,128)S(1)} %premix.1.refs_2_, ...), custom_call_target="tpu_custom_call" | custom-call | flops 2400000000 | bytes 8000000 | tf_op jit(solution)/shard_map/sent/pallas_call | solution.py:269
  15.9 0.5 %collective-permute-start.8 = (bf16[2,2,2,128,128]{4,3,2,1,0:T(8,128)(2,1)S(1)}, bf16[2,2,2,128,128]{4,3,2,1,0:T(8,128)(2,1)S(1)}, u32[]{:S(2)}, u32[]{:S(2)}) collective-permute-start(bf16[2,2,2,128,128]{4,3,2,1,0:T(8,128)(2,1)S(1)} %get-tuple-element.45), channel_id=1, source_target_pairs={{0,4},{1,5},{2,6},{3,7},{4,0},{5,1},{6,2},{7,3},{8,12},{9,13},{10,... | collective-permute-start | bytes 786440 | tf_op jit(solution)/shard_map/ppermute | solution.py:407
  16.4 0.0 collective-permute-start.9
  16.4 0.0 collective-permute-done.3.refs_4_
  16.4 1.0 %collective-permute-done.4.refs_5_ = bf16[2,1,2,128,128]{4,3,2,1,0:T(8,128)(2,1)S(1)} collective-permute-done((bf16[2,1,2,128,128]{4,3,2,1,0:T(8,128)(2,1)S(1)}, bf16[2,1,2,128,128]{4,3,2,1,0:T(8,128)(2,1)S(1)}, u32[]{:S(2)}, u32[]{:S(2)}) %collective-permute-start.4) | collective-permute-done | bytes 131104 | tf_op jit(solution)/shard_map/ppermute | solution.py:407
  17.4 1.7 %sent.2 = (bf16[2,2,2,128,128]{4,3,2,1,0:T(8,128)(2,1)S(1)}, bf16[2,2,2,128,128]{4,3,2,1,0:T(8,128)(2,1)S(1)}) custom-call(bf16[2,1,2,128,128]{4,3,2,1,0:T(8,128)(2,1)S(1)} %get-tuple-element.27.own.refs_0_, bf16[2,1,2,128,128]{4,3,2,1,0:T(8,128)(2,1)S(1)} %get-tuple-element.28.refs_1_, bf16[2,1,2,128,128]{4,3,2,1,0:T(8,128)(2,1)S(1)} %collective-permute-done.1.near.refs_2_, ...), custom_call_target="tpu_custom_call" | custom-call | flops 2400000000 | bytes 8000000 | tf_op jit(solution)/shard_map/sent/pallas_call | solution.py:269
  19.1 0.1 collective-permute-start.7
  19.2 0.7 %collective-permute-start.6 = (bf16[2,2,2,128,128]{4,3,2,1,0:T(8,128)(2,1)S(1)}, bf16[2,2,2,128,128]{4,3,2,1,0:T(8,128)(2,1)S(1)}, u32[]{:S(2)}, u32[]{:S(2)}) collective-permute-start(bf16[2,2,2,128,128]{4,3,2,1,0:T(8,128)(2,1)S(1)} %get-tuple-element.41), channel_id=1, source_target_pairs={{0,1},{1,0},{2,3},{3,2},{4,5},{5,4},{6,7},{7,6},{8,9},{9,8},{10,11... | collective-permute-start | bytes 786440 | tf_op jit(solution)/shard_map/ppermute | solution.py:407
  19.9 2.3 %kept.1 = (f32[2,2,2,128,128]{4,3,2,1,0:T(8,128)S(1)}, f32[2,2,2,128,128]{4,3,2,1,0:T(8,128)S(1)}) custom-call(bf16[2,1,2,128,128]{4,3,2,1,0:T(8,128)(2,1)S(1)} %get-tuple-element.27.own.refs_0_, bf16[2,1,2,128,128]{4,3,2,1,0:T(8,128)(2,1)S(1)} %get-tuple-element.28.refs_1_, bf16[2,1,2,128,128]{4,3,2,1,0:T(8,128)(2,1)S(1)} %collective-permute-done.1.near.refs_2_, ...), custom_call_target="tpu_custom_call" | custom-call | flops 2400000000 | bytes 8000000 | tf_op jit(solution)/shard_map/kept/pallas_call | solution.py:299
  22.2 4.4 %collective-permute-done.8.near = bf16[2,2,2,128,128]{4,3,2,1,0:T(8,128)(2,1)S(1)} collective-permute-done((bf16[2,2,2,128,128]{4,3,2,1,0:T(8,128)(2,1)S(1)}, bf16[2,2,2,128,128]{4,3,2,1,0:T(8,128)(2,1)S(1)}, u32[]{:S(2)}, u32[]{:S(2)}) %collective-permute-start.8) | collective-permute-done | bytes 262176 | tf_op jit(solution)/shard_map/ppermute | solution.py:407
  26.7 0.0 collective-permute-done.9.far
  26.7 0.1 gather.1.from_b
  26.7 0.7 %collective-permute-done.7.far_a = bf16[2,2,2,128,128]{4,3,2,1,0:T(8,128)(2,1)S(1)} collective-permute-done((bf16[2,2,2,128,128]{4,3,2,1,0:T(8,128)(2,1)S(1)}, bf16[2,2,2,128,128]{4,3,2,1,0:T(8,128)(2,1)S(1)}, u32[]{:S(2)}, u32[]{:S(2)}) %collective-permute-start.7) | collective-permute-done | bytes 262176 | tf_op jit(solution)/shard_map/ppermute | solution.py:407
  27.5 0.0 collective-permute-done.6.near_a
  27.5 0.9 %finish.1 = bf16[1,2,4,2,128,128]{5,4,3,2,1,0:T(8,128)(2,1)} custom-call(f32[2,2,2,128,128]{4,3,2,1,0:T(8,128)S(1)} %get-tuple-element.40.own_a, bf16[2,2,2,128,128]{4,3,2,1,0:T(8,128)(2,1)S(1)} %collective-permute-done.6.near_a, bf16[2,2,2,128,128]{4,3,2,1,0:T(8,128)(2,1)S(1)} %collective-permute-done.7.far_a, ...), custom_call_target="tpu_custom_call" | custom-call | tf_op jit(solution)/shard_map/finish/pallas_call | solution.py:349
  (1 shorter events, 0.0 us)
Async XLA Ops:
  1.1 13.0 %collective-permute-start = (bf16[2,2,2,128,128]{4,3,2,1,0:T(8,128)(2,1)S(1)}, bf16[2,2,2,128,128]{4,3,2,1,0:T(8,128)(2,1)S(1)}, u32[]{:S(2)}, u32[]{:S(2)}) collective-permute-start(bf16[2,2,2,128,128]{4,3,2,1,0:T(8,128)(2,1)S(1)} %get-tuple-element.38.refs_0_.refs_6_), channel_id=1, source_target_pairs={{0,3},{1,2},{2,1},{3,0},{4,7},{5,6},{6,5},{7,4},{8,11},{9,10},{10,... | collective-permute-start | bytes 786440 | tf_op jit(solution)/shard_map/ppermute | solution.py:407
  3.6 10.5 %collective-permute-start.5 = (bf16[2,2,2,128,128]{4,3,2,1,0:T(8,128)(2,1)S(1)}, bf16[2,2,2,128,128]{4,3,2,1,0:T(8,128)(2,1)S(1)}, u32[]{:S(2)}, u32[]{:S(2)}) collective-permute-start(bf16[2,2,2,128,128]{4,3,2,1,0:T(8,128)(2,1)S(1)} %get-tuple-element.38.refs_0_.refs_6_), channel_id=1, source_target_pairs={{0,1},{1,0},{2,3},{3,2},{4,5},{5,4},{6,7},{7,6},{8,9},{9,8},{10,11... | collective-permute-start | bytes 786440 | tf_op jit(solution)/shard_map/ppermute | solution.py:407
  4.3 6.4 %collective-permute-start.1 = (bf16[2,1,2,128,128]{4,3,2,1,0:T(8,128)(2,1)S(1)}, bf16[2,1,2,128,128]{4,3,2,1,0:T(8,128)(2,1)S(1)}, u32[]{:S(2)}, u32[]{:S(2)}) collective-permute-start(bf16[2,1,2,128,128]{4,3,2,1,0:T(8,128)(2,1)S(1)} %get-tuple-element.27.own.refs_0_), channel_id=1, source_target_pairs={{0,4},{1,5},{2,6},{3,7},{4,0},{5,1},{6,2},{7,3},{8,12},{9,13},{10,... | collective-permute-start | bytes 393224 | tf_op jit(solution)/shard_map/ppermute | solution.py:407
  5.8 6.7 %collective-permute-start.2 = (bf16[2,1,2,128,128]{4,3,2,1,0:T(8,128)(2,1)S(1)}, bf16[2,1,2,128,128]{4,3,2,1,0:T(8,128)(2,1)S(1)}, u32[]{:S(2)}, u32[]{:S(2)}) collective-permute-start(bf16[2,1,2,128,128]{4,3,2,1,0:T(8,128)(2,1)S(1)} %get-tuple-element.28.refs_1_), channel_id=1, source_target_pairs={{0,4},{1,5},{2,6},{3,7},{4,0},{5,1},{6,2},{7,3},{8,12},{9,13},{10,... | collective-permute-start | bytes 393224 | tf_op jit(solution)/shard_map/ppermute | solution.py:407
  10.7 5.8 %collective-permute-start.3 = (bf16[2,1,2,128,128]{4,3,2,1,0:T(8,128)(2,1)S(1)}, bf16[2,1,2,128,128]{4,3,2,1,0:T(8,128)(2,1)S(1)}, u32[]{:S(2)}, u32[]{:S(2)}) collective-permute-start(bf16[2,1,2,128,128]{4,3,2,1,0:T(8,128)(2,1)S(1)} %choose.1), channel_id=1, source_target_pairs={{0,1},{1,0},{2,3},{3,2},{4,8},{5,9},{6,10},{7,11},{8,16},{9,17},{1... | collective-permute-start | bytes 393224 | tf_op jit(solution)/shard_map/ppermute | solution.py:407
  12.5 5.0 %collective-permute-start.4 = (bf16[2,1,2,128,128]{4,3,2,1,0:T(8,128)(2,1)S(1)}, bf16[2,1,2,128,128]{4,3,2,1,0:T(8,128)(2,1)S(1)}, u32[]{:S(2)}, u32[]{:S(2)}) collective-permute-start(bf16[2,1,2,128,128]{4,3,2,1,0:T(8,128)(2,1)S(1)} %collective-permute-done.2.refs_3_), channel_id=1, source_target_pairs={{0,8},{1,9},{2,10},{3,11},{4,0},{5,1},{6,2},{7,3},{8,16},{9,17},{1... | collective-permute-start | bytes 393224 | tf_op jit(solution)/shard_map/ppermute | solution.py:407
  15.9 10.7 %collective-permute-start.8 = (bf16[2,2,2,128,128]{4,3,2,1,0:T(8,128)(2,1)S(1)}, bf16[2,2,2,128,128]{4,3,2,1,0:T(8,128)(2,1)S(1)}, u32[]{:S(2)}, u32[]{:S(2)}) collective-permute-start(bf16[2,2,2,128,128]{4,3,2,1,0:T(8,128)(2,1)S(1)} %get-tuple-element.45), channel_id=1, source_target_pairs={{0,4},{1,5},{2,6},{3,7},{4,0},{5,1},{6,2},{7,3},{8,12},{9,13},{10,... | collective-permute-start | bytes 786440 | tf_op jit(solution)/shard_map/ppermute | solution.py:407
  16.4 10.2 %collective-permute-start.9 = (bf16[2,2,2,128,128]{4,3,2,1,0:T(8,128)(2,1)S(1)}, bf16[2,2,2,128,128]{4,3,2,1,0:T(8,128)(2,1)S(1)}, u32[]{:S(2)}, u32[]{:S(2)}) collective-permute-start(bf16[2,2,2,128,128]{4,3,2,1,0:T(8,128)(2,1)S(1)} %get-tuple-element.47), channel_id=1, source_target_pairs={{0,1},{1,0},{2,3},{3,2},{4,8},{5,9},{6,10},{7,11},{8,4},{9,5},{10,... | collective-permute-start | bytes 786440 | tf_op jit(solution)/shard_map/ppermute | solution.py:407
  19.1 8.4 %collective-permute-start.7 = (bf16[2,2,2,128,128]{4,3,2,1,0:T(8,128)(2,1)S(1)}, bf16[2,2,2,128,128]{4,3,2,1,0:T(8,128)(2,1)S(1)}, u32[]{:S(2)}, u32[]{:S(2)}) collective-permute-start(bf16[2,2,2,128,128]{4,3,2,1,0:T(8,128)(2,1)S(1)} %get-tuple-element.42), channel_id=1, source_target_pairs={{0,3},{1,2},{2,1},{3,0},{4,7},{5,6},{6,5},{7,4},{8,11},{9,10},{10,... | collective-permute-start | bytes 786440 | tf_op jit(solution)/shard_map/ppermute | solution.py:407
  19.2 8.3 %collective-permute-start.6 = (bf16[2,2,2,128,128]{4,3,2,1,0:T(8,128)(2,1)S(1)}, bf16[2,2,2,128,128]{4,3,2,1,0:T(8,128)(2,1)S(1)}, u32[]{:S(2)}, u32[]{:S(2)}) collective-permute-start(bf16[2,2,2,128,128]{4,3,2,1,0:T(8,128)(2,1)S(1)} %get-tuple-element.41), channel_id=1, source_target_pairs={{0,1},{1,0},{2,3},{3,2},{4,5},{5,4},{6,7},{7,6},{8,9},{9,8},{10,11... | collective-permute-start | bytes 786440 | tf_op jit(solution)/shard_map/ppermute | solution.py:407

commit v8 on v6

--- a/solution.py
+++ b/solution.py
@@ -303,9 +303,10 @@
             value = own_a[:, t] + near_a[:, t].astype(f32) + far_a[:, t].astype(f32)
         else:
             value = own_b[:, t - tiles_a] + from_b[:, t - tiles_a]
-        held[:, t] = value.astype(held.dtype)
-        copies.append(pltpu.make_async_copy(held.at[:, t], out.at[0, :, t], sems.at[t]))
-        copies[-1].start()
+        for e in range(held.shape[0]):
+            held[e, t] = value[e].astype(held.dtype)
+            copies.append(pltpu.make_async_copy(held.at[e, t], out.at[0, e, t], sems.at[len(copies)]))
+            copies[-1].start()
     for copy in copies:
         copy.wait()
 
@@ -319,7 +320,7 @@
         out_shape=jax.ShapeDtypeStruct((1,) + shape, jnp.bfloat16),
         in_specs=vmem_specs(5),
         out_specs=pl.BlockSpec(memory_space=pl.ANY),
-        scratch_shapes=[pltpu.VMEM(shape, jnp.bfloat16), pltpu.SemaphoreType.DMA((tiles,))],
+        scratch_shapes=[pltpu.VMEM(shape, jnp.bfloat16), pltpu.SemaphoreType.DMA((e * tiles,))],
         compiler_params=pltpu.CompilerParams(vmem_limit_bytes=GRANT),
         name="finish",
     )(*map(in_vmem, (own_a, near_a, far_a, own_b, from_b)))

time: 28.8 us -> 28.8 us (level)
  no operation moved by 1% of the time
where the time goes in v8:
time: 28.8 us; the launch traced here: 28.6 us
  Pallas kernels  10.2 us (35%)
  waiting for transfers between devices  10.2 us (35%)
  starting transfers between devices  8.07 us (28%)
    ppermute x10, waiting for transfers between devices, send(): return lax.ppermute(block, AXES, route[name])  10.2 us
    ppermute x10, starting transfers between devices, send(): return lax.ppermute(block, AXES, route[name])  8.07 us
    pallas_call x2, Pallas kernels, sent(): pl.pallas_call(functools.partial(sent_kernel, first, forward, places, cou...  3.79 us
    pallas_call x1, Pallas kernels, kept(): pl.pallas_call(functools.partial(kept_kernel, places, count), out_shape=(...  2.32 us
    pallas_call x1, Pallas kernels, prepare(): pl.pallas_call(prepare_kernel, out_shape=(big, big, pltpu.VMEM((ENTRIES,...  1.63 us
    pallas_call x1, Pallas kernels, split(): pl.pallas_call(split_kernel, out_shape=tuple((pltpu.VMEM((e, count, *rest...  1.11 us
    pallas_call x1, Pallas kernels, finish(): pl.pallas_call(finish_kernel, out_shape=jax.ShapeDtypeStruct((1,) + shape...  0.87 us
  transfers between devices with their start and end apart: 10, of which 5 were waited for; matrix products, arithmetic and copies ran while one was open for 0% of the time, Pallas kernels for 29%

profile of v8, /device:TPU:0, one launch (start us, length us, event | category | flops | bytes accessed | tf_op | source)
XLA Modules:
  0.0 28.6 jit_solution(3184264488700338224)
XLA Ops:
  0.0 1.1 %split.1 = (bf16[2,1,2,128,128]{4,3,2,1,0:T(8,128)(2,1)S(1)}, bf16[2,1,2,128,128]{4,3,2,1,0:T(8,128)(2,1)S(1)}, bf16[2,2,2,128,128]{4,3,2,1,0:T(8,128)(2,1)S(1)}) custom-call(bf16[1,2,4,2,128,128]{5,4,3,2,1,0:T(8,128)(2,1)} %source.1), custom_call_target="tpu_custom_call" | custom-call | tf_op jit(solution)/shard_map/split/pallas_call | solution.py:360
  1.1 2.5 %collective-permute-start = (bf16[2,2,2,128,128]{4,3,2,1,0:T(8,128)(2,1)S(1)}, bf16[2,2,2,128,128]{4,3,2,1,0:T(8,128)(2,1)S(1)}, u32[]{:S(2)}, u32[]{:S(2)}) collective-permute-start(bf16[2,2,2,128,128]{4,3,2,1,0:T(8,128)(2,1)S(1)} %get-tuple-element.36.refs_0_.refs_6_), channel_id=1, source_target_pairs={{0,3},{1,2},{2,1},{3,0},{4,7},{5,6},{6,5},{7,4},{8,11},{9,10},{10,... | collective-permute-start | bytes 786440 | tf_op jit(solution)/shard_map/ppermute | solution.py:376
  3.6 0.7 %collective-permute-start.5 = (bf16[2,2,2,128,128]{4,3,2,1,0:T(8,128)(2,1)S(1)}, bf16[2,2,2,128,128]{4,3,2,1,0:T(8,128)(2,1)S(1)}, u32[]{:S(2)}, u32[]{:S(2)}) collective-permute-start(bf16[2,2,2,128,128]{4,3,2,1,0:T(8,128)(2,1)S(1)} %get-tuple-element.36.refs_0_.refs_6_), channel_id=1, source_target_pairs={{0,1},{1,0},{2,3},{3,2},{4,5},{5,4},{6,7},{7,6},{8,9},{9,8},{10,11... | collective-permute-start | bytes 786440 | tf_op jit(solution)/shard_map/ppermute | solution.py:376
  4.3 1.5 %collective-permute-start.1 = (bf16[2,1,2,128,128]{4,3,2,1,0:T(8,128)(2,1)S(1)}, bf16[2,1,2,128,128]{4,3,2,1,0:T(8,128)(2,1)S(1)}, u32[]{:S(2)}, u32[]{:S(2)}) collective-permute-start(bf16[2,1,2,128,128]{4,3,2,1,0:T(8,128)(2,1)S(1)} %get-tuple-element.26.own.refs_0_), channel_id=1, source_target_pairs={{0,4},{1,5},{2,6},{3,7},{4,0},{5,1},{6,2},{7,3},{8,12},{9,13},{10,... | collective-permute-start | bytes 393224 | tf_op jit(solution)/shard_map/ppermute | solution.py:376
  5.8 0.5 %collective-permute-start.2 = (bf16[2,1,2,128,128]{4,3,2,1,0:T(8,128)(2,1)S(1)}, bf16[2,1,2,128,128]{4,3,2,1,0:T(8,128)(2,1)S(1)}, u32[]{:S(2)}, u32[]{:S(2)}) collective-permute-start(bf16[2,1,2,128,128]{4,3,2,1,0:T(8,128)(2,1)S(1)} %get-tuple-element.27.refs_1_), channel_id=1, source_target_pairs={{0,4},{1,5},{2,6},{3,7},{4,0},{5,1},{6,2},{7,3},{8,12},{9,13},{10,... | collective-permute-start | bytes 393224 | tf_op jit(solution)/shard_map/ppermute | solution.py:376
  6.3 0.1 pad_add_fusion.parity
  6.4 1.6 %prepare.1 = (bf16[4,3,256,256]{3,2,1,0:T(8,128)(2,1)S(1)}, bf16[4,3,256,256]{3,2,1,0:T(8,128)(2,1)S(1)}, f32[49,8,128]{2,1,0:T(8,128)S(1)}) custom-call(s32[4]{0:T(128)S(1)} %pad_add_fusion.parity, s32[2,6]{1,0:T(2,128)} %bitcast.8, f32[3,2,6]{2,1,0:T(2,128)} %bitcast.7, s32[2,4]{1,0:T(2,128)} %bitcast.9, bf16[3,4,2,128,128]{4,3,2,1,0:T(8,128)(2,1)} %dham.1), custom_call_target="tpu_custom_call" | custom-call | tf_op jit(solution)/shard_map/prepare/pallas_call | solution.py:108
  8.0 0.4 %premix.1.refs_2_ = f32[2,3,256,512]{3,2,1,0:T(8,128)S(1)} custom-call(bf16[2,2,2,128,128]{4,3,2,1,0:T(8,128)(2,1)S(1)} %get-tuple-element.36.refs_0_.refs_6_, f32[49,8,128]{2,1,0:T(8,128)S(1)} %get-tuple-element.29.refs_1_.coef.refs_8_.refs_11_.refs_5_), custom_call_target="tpu_custom_call" | custom-call | flops 600000000 | bytes 2000000 | tf_op jit(solution)/shard_map/premix/pallas_call | solution.py:202
  8.4 2.2 %collective-permute-done.1.near.refs_2_ = bf16[2,1,2,128,128]{4,3,2,1,0:T(8,128)(2,1)S(1)} collective-permute-done((bf16[2,1,2,128,128]{4,3,2,1,0:T(8,128)(2,1)S(1)}, bf16[2,1,2,128,128]{4,3,2,1,0:T(8,128)(2,1)S(1)}, u32[]{:S(2)}, u32[]{:S(2)}) %collective-permute-start.1) | collective-permute-done | bytes 131104 | tf_op jit(solution)/shard_map/ppermute | solution.py:376
  10.7 0.1 collective-permute-start.3
  10.7 1.7 %collective-permute-done.2.refs_3_ = bf16[2,1,2,128,128]{4,3,2,1,0:T(8,128)(2,1)S(1)} collective-permute-done((bf16[2,1,2,128,128]{4,3,2,1,0:T(8,128)(2,1)S(1)}, bf16[2,1,2,128,128]{4,3,2,1,0:T(8,128)(2,1)S(1)}, u32[]{:S(2)}, u32[]{:S(2)}) %collective-permute-start.2) | collective-permute-done | bytes 131104 | tf_op jit(solution)/shard_map/ppermute | solution.py:376
  12.5 1.6 %collective-permute-start.4 = (bf16[2,1,2,128,128]{4,3,2,1,0:T(8,128)(2,1)S(1)}, bf16[2,1,2,128,128]{4,3,2,1,0:T(8,128)(2,1)S(1)}, u32[]{:S(2)}, u32[]{:S(2)}) collective-permute-start(bf16[2,1,2,128,128]{4,3,2,1,0:T(8,128)(2,1)S(1)} %collective-permute-done.2.refs_3_), channel_id=1, source_target_pairs={{0,8},{1,9},{2,10},{3,11},{4,0},{5,1},{6,2},{7,3},{8,16},{9,17},{1... | collective-permute-start | bytes 393224 | tf_op jit(solution)/shard_map/ppermute | solution.py:376
  14.1 0.0 collective-permute-done.refs_8_.refs_1_
  14.1 0.0 collective-permute-done.5.refs_7_.refs_0_
  14.1 1.9 %sent.3 = (bf16[2,2,2,128,128]{4,3,2,1,0:T(8,128)(2,1)S(1)}, bf16[2,2,2,128,128]{4,3,2,1,0:T(8,128)(2,1)S(1)}) custom-call(bf16[2,2,2,128,128]{4,3,2,1,0:T(8,128)(2,1)S(1)} %collective-permute-done.5.refs_7_.refs_0_, bf16[2,2,2,128,128]{4,3,2,1,0:T(8,128)(2,1)S(1)} %collective-permute-done.refs_8_.refs_1_, f32[2,3,256,512]{3,2,1,0:T(8,128)S(1)} %premix.1.refs_2_, ...), custom_call_target="tpu_custom_call" | custom-call | flops 2400000000 | bytes 8000000 | tf_op jit(solution)/shard_map/sent/pallas_call | solution.py:237
  15.9 0.5 %collective-permute-start.8 = (bf16[2,2,2,128,128]{4,3,2,1,0:T(8,128)(2,1)S(1)}, bf16[2,2,2,128,128]{4,3,2,1,0:T(8,128)(2,1)S(1)}, u32[]{:S(2)}, u32[]{:S(2)}) collective-permute-start(bf16[2,2,2,128,128]{4,3,2,1,0:T(8,128)(2,1)S(1)} %get-tuple-element.43), channel_id=1, source_target_pairs={{0,4},{1,5},{2,6},{3,7},{4,0},{5,1},{6,2},{7,3},{8,12},{9,13},{10,... | collective-permute-start | bytes 786440 | tf_op jit(solution)/shard_map/ppermute | solution.py:376
  16.4 0.0 collective-permute-start.9
  16.4 0.0 collective-permute-done.3.refs_4_
  16.4 1.0 %collective-permute-done.4.refs_5_ = bf16[2,1,2,128,128]{4,3,2,1,0:T(8,128)(2,1)S(1)} collective-permute-done((bf16[2,1,2,128,128]{4,3,2,1,0:T(8,128)(2,1)S(1)}, bf16[2,1,2,128,128]{4,3,2,1,0:T(8,128)(2,1)S(1)}, u32[]{:S(2)}, u32[]{:S(2)}) %collective-permute-start.4) | collective-permute-done | bytes 131104 | tf_op jit(solution)/shard_map/ppermute | solution.py:376
  17.4 1.9 %sent.2 = (bf16[2,2,2,128,128]{4,3,2,1,0:T(8,128)(2,1)S(1)}, bf16[2,2,2,128,128]{4,3,2,1,0:T(8,128)(2,1)S(1)}) custom-call(bf16[2,1,2,128,128]{4,3,2,1,0:T(8,128)(2,1)S(1)} %get-tuple-element.26.own.refs_0_, bf16[2,1,2,128,128]{4,3,2,1,0:T(8,128)(2,1)S(1)} %get-tuple-element.27.refs_1_, bf16[2,1,2,128,128]{4,3,2,1,0:T(8,128)(2,1)S(1)} %collective-permute-done.1.near.refs_2_, ...), custom_call_target="tpu_custom_call" | custom-call | flops 2400000000 | bytes 8000000 | tf_op jit(solution)/shard_map/sent/pallas_call | solution.py:237
  19.4 0.1 collective-permute-start.7
  19.5 0.7 %collective-permute-start.6 = (bf16[2,2,2,128,128]{4,3,2,1,0:T(8,128)(2,1)S(1)}, bf16[2,2,2,128,128]{4,3,2,1,0:T(8,128)(2,1)S(1)}, u32[]{:S(2)}, u32[]{:S(2)}) collective-permute-start(bf16[2,2,2,128,128]{4,3,2,1,0:T(8,128)(2,1)S(1)} %get-tuple-element.39), channel_id=1, source_target_pairs={{0,1},{1,0},{2,3},{3,2},{4,5},{5,4},{6,7},{7,6},{8,9},{9,8},{10,11... | collective-permute-start | bytes 786440 | tf_op jit(solution)/shard_map/ppermute | solution.py:376
  20.1 2.3 %kept.1 = (f32[2,2,2,128,128]{4,3,2,1,0:T(8,128)S(1)}, f32[2,2,2,128,128]{4,3,2,1,0:T(8,128)S(1)}) custom-call(bf16[2,1,2,128,128]{4,3,2,1,0:T(8,128)(2,1)S(1)} %get-tuple-element.26.own.refs_0_, bf16[2,1,2,128,128]{4,3,2,1,0:T(8,128)(2,1)S(1)} %get-tuple-element.27.refs_1_, bf16[2,1,2,128,128]{4,3,2,1,0:T(8,128)(2,1)S(1)} %collective-permute-done.1.near.refs_2_, ...), custom_call_target="tpu_custom_call" | custom-call | flops 2400000000 | bytes 8000000 | tf_op jit(solution)/shard_map/kept/pallas_call | solution.py:267
  22.5 4.2 %collective-permute-done.8.near = bf16[2,2,2,128,128]{4,3,2,1,0:T(8,128)(2,1)S(1)} collective-permute-done((bf16[2,2,2,128,128]{4,3,2,1,0:T(8,128)(2,1)S(1)}, bf16[2,2,2,128,128]{4,3,2,1,0:T(8,128)(2,1)S(1)}, u32[]{:S(2)}, u32[]{:S(2)}) %collective-permute-start.8) | collective-permute-done | bytes 262176 | tf_op jit(solution)/shard_map/ppermute | solution.py:376
  26.7 0.0 collective-permute-done.9.far
  26.7 0.1 gather.1.from_b
  26.7 1.0 %collective-permute-done.7.far_a = bf16[2,2,2,128,128]{4,3,2,1,0:T(8,128)(2,1)S(1)} collective-permute-done((bf16[2,2,2,128,128]{4,3,2,1,0:T(8,128)(2,1)S(1)}, bf16[2,2,2,128,128]{4,3,2,1,0:T(8,128)(2,1)S(1)}, u32[]{:S(2)}, u32[]{:S(2)}) %collective-permute-start.7) | collective-permute-done | bytes 262176 | tf_op jit(solution)/shard_map/ppermute | solution.py:376
  27.7 0.0 collective-permute-done.6.near_a
  27.7 0.9 %finish.1 = bf16[1,2,4,2,128,128]{5,4,3,2,1,0:T(8,128)(2,1)} custom-call(f32[2,2,2,128,128]{4,3,2,1,0:T(8,128)S(1)} %get-tuple-element.38.own_a, bf16[2,2,2,128,128]{4,3,2,1,0:T(8,128)(2,1)S(1)} %collective-permute-done.6.near_a, bf16[2,2,2,128,128]{4,3,2,1,0:T(8,128)(2,1)S(1)} %collective-permute-done.7.far_a, ...), custom_call_target="tpu_custom_call" | custom-call | tf_op jit(solution)/shard_map/finish/pallas_call | solution.py:318
  (1 shorter events, 0.0 us)
Async XLA Ops:
  1.1 13.0 %collective-permute-start = (bf16[2,2,2,128,128]{4,3,2,1,0:T(8,128)(2,1)S(1)}, bf16[2,2,2,128,128]{4,3,2,1,0:T(8,128)(2,1)S(1)}, u32[]{:S(2)}, u32[]{:S(2)}) collective-permute-start(bf16[2,2,2,128,128]{4,3,2,1,0:T(8,128)(2,1)S(1)} %get-tuple-element.36.refs_0_.refs_6_), channel_id=1, source_target_pairs={{0,3},{1,2},{2,1},{3,0},{4,7},{5,6},{6,5},{7,4},{8,11},{9,10},{10,... | collective-permute-start | bytes 786440 | tf_op jit(solution)/shard_map/ppermute | solution.py:376
  3.6 10.5 %collective-permute-start.5 = (bf16[2,2,2,128,128]{4,3,2,1,0:T(8,128)(2,1)S(1)}, bf16[2,2,2,128,128]{4,3,2,1,0:T(8,128)(2,1)S(1)}, u32[]{:S(2)}, u32[]{:S(2)}) collective-permute-start(bf16[2,2,2,128,128]{4,3,2,1,0:T(8,128)(2,1)S(1)} %get-tuple-element.36.refs_0_.refs_6_), channel_id=1, source_target_pairs={{0,1},{1,0},{2,3},{3,2},{4,5},{5,4},{6,7},{7,6},{8,9},{9,8},{10,11... | collective-permute-start | bytes 786440 | tf_op jit(solution)/shard_map/ppermute | solution.py:376
  4.3 6.4 %collective-permute-start.1 = (bf16[2,1,2,128,128]{4,3,2,1,0:T(8,128)(2,1)S(1)}, bf16[2,1,2,128,128]{4,3,2,1,0:T(8,128)(2,1)S(1)}, u32[]{:S(2)}, u32[]{:S(2)}) collective-permute-start(bf16[2,1,2,128,128]{4,3,2,1,0:T(8,128)(2,1)S(1)} %get-tuple-element.26.own.refs_0_), channel_id=1, source_target_pairs={{0,4},{1,5},{2,6},{3,7},{4,0},{5,1},{6,2},{7,3},{8,12},{9,13},{10,... | collective-permute-start | bytes 393224 | tf_op jit(solution)/shard_map/ppermute | solution.py:376
  5.8 6.7 %collective-permute-start.2 = (bf16[2,1,2,128,128]{4,3,2,1,0:T(8,128)(2,1)S(1)}, bf16[2,1,2,128,128]{4,3,2,1,0:T(8,128)(2,1)S(1)}, u32[]{:S(2)}, u32[]{:S(2)}) collective-permute-start(bf16[2,1,2,128,128]{4,3,2,1,0:T(8,128)(2,1)S(1)} %get-tuple-element.27.refs_1_), channel_id=1, source_target_pairs={{0,4},{1,5},{2,6},{3,7},{4,0},{5,1},{6,2},{7,3},{8,12},{9,13},{10,... | collective-permute-start | bytes 393224 | tf_op jit(solution)/shard_map/ppermute | solution.py:376
  10.7 5.8 %collective-permute-start.3 = (bf16[2,1,2,128,128]{4,3,2,1,0:T(8,128)(2,1)S(1)}, bf16[2,1,2,128,128]{4,3,2,1,0:T(8,128)(2,1)S(1)}, u32[]{:S(2)}, u32[]{:S(2)}) collective-permute-start(bf16[2,1,2,128,128]{4,3,2,1,0:T(8,128)(2,1)S(1)} %choose.1), channel_id=1, source_target_pairs={{0,1},{1,0},{2,3},{3,2},{4,8},{5,9},{6,10},{7,11},{8,16},{9,17},{1... | collective-permute-start | bytes 393224 | tf_op jit(solution)/shard_map/ppermute | solution.py:376
  12.5 5.0 %collective-permute-start.4 = (bf16[2,1,2,128,128]{4,3,2,1,0:T(8,128)(2,1)S(1)}, bf16[2,1,2,128,128]{4,3,2,1,0:T(8,128)(2,1)S(1)}, u32[]{:S(2)}, u32[]{:S(2)}) collective-permute-start(bf16[2,1,2,128,128]{4,3,2,1,0:T(8,128)(2,1)S(1)} %collective-permute-done.2.refs_3_), channel_id=1, source_target_pairs={{0,8},{1,9},{2,10},{3,11},{4,0},{5,1},{6,2},{7,3},{8,16},{9,17},{1... | collective-permute-start | bytes 393224 | tf_op jit(solution)/shard_map/ppermute | solution.py:376
  15.9 10.7 %collective-permute-start.8 = (bf16[2,2,2,128,128]{4,3,2,1,0:T(8,128)(2,1)S(1)}, bf16[2,2,2,128,128]{4,3,2,1,0:T(8,128)(2,1)S(1)}, u32[]{:S(2)}, u32[]{:S(2)}) collective-permute-start(bf16[2,2,2,128,128]{4,3,2,1,0:T(8,128)(2,1)S(1)} %get-tuple-element.43), channel_id=1, source_target_pairs={{0,4},{1,5},{2,6},{3,7},{4,0},{5,1},{6,2},{7,3},{8,12},{9,13},{10,... | collective-permute-start | bytes 786440 | tf_op jit(solution)/shard_map/ppermute | solution.py:376
  16.4 10.2 %collective-permute-start.9 = (bf16[2,2,2,128,128]{4,3,2,1,0:T(8,128)(2,1)S(1)}, bf16[2,2,2,128,128]{4,3,2,1,0:T(8,128)(2,1)S(1)}, u32[]{:S(2)}, u32[]{:S(2)}) collective-permute-start(bf16[2,2,2,128,128]{4,3,2,1,0:T(8,128)(2,1)S(1)} %get-tuple-element.45), channel_id=1, source_target_pairs={{0,1},{1,0},{2,3},{3,2},{4,8},{5,9},{6,10},{7,11},{8,4},{9,5},{10,... | collective-permute-start | bytes 786440 | tf_op jit(solution)/shard_map/ppermute | solution.py:376
  19.4 8.4 %collective-permute-start.7 = (bf16[2,2,2,128,128]{4,3,2,1,0:T(8,128)(2,1)S(1)}, bf16[2,2,2,128,128]{4,3,2,1,0:T(8,128)(2,1)S(1)}, u32[]{:S(2)}, u32[]{:S(2)}) collective-permute-start(bf16[2,2,2,128,128]{4,3,2,1,0:T(8,128)(2,1)S(1)} %get-tuple-element.40), channel_id=1, source_target_pairs={{0,3},{1,2},{2,1},{3,0},{4,7},{5,6},{6,5},{7,4},{8,11},{9,10},{10,... | collective-permute-start | bytes 786440 | tf_op jit(solution)/shard_map/ppermute | solution.py:376
  19.5 8.3 %collective-permute-start.6 = (bf16[2,2,2,128,128]{4,3,2,1,0:T(8,128)(2,1)S(1)}, bf16[2,2,2,128,128]{4,3,2,1,0:T(8,128)(2,1)S(1)}, u32[]{:S(2)}, u32[]{:S(2)}) collective-permute-start(bf16[2,2,2,128,128]{4,3,2,1,0:T(8,128)(2,1)S(1)} %get-tuple-element.39), channel_id=1, source_target_pairs={{0,1},{1,0},{2,3},{3,2},{4,5},{5,4},{6,7},{7,6},{8,9},{9,8},{10,11... | collective-permute-start | bytes 786440 | tf_op jit(solution)/shard_map/ppermute | solution.py:376
